TPU v7x, 128 devices: a whole 4x4x4 slice. The times are simulated.
128 devices in a mesh: seq: 32 (over x, y, core), head: 4 (over z).
Axes of the slice: x: 4, y: 4, z: 4, core: 2. Of those that a mesh axis runs over, the one named last changes fastest.
Arguments:
- x_in: bfloat16 [24576, 16384], P('seq', 'head'), may hold values from -6 to 6
- z_in: bfloat16 [24576, 16384], P('seq', 'head'), may hold values from -6 to 6
- bc_in: bfloat16 [24576, 2, 2048], P('seq', None, 'head'), may hold values from -6 to 6
- dt_in: float32 [24576, 256], P('seq', 'head'), may hold values from -6 to 6
- conv_x_weight: float32 [4, 16384], P(None, 'head'), may hold values from -3 to 3
- conv_x_bias: float32 [16384], P('head'), may hold values from -0.5 to 0.5
- conv_bc_weight: float32 [4, 2, 2048], P(None, None, 'head'), may hold values from -3 to 3
- conv_bc_bias: float32 [2, 2048], P(None, 'head'), may hold values from -0.5 to 0.5
- dt_bias: float32 [256], P('head'), may hold values from -1 to 1
- a_log: float32 [256], P('head')
- norm_gain: float32 [16384], P('head'), may hold values from 0.5 to 1.5
- reward_w: float32 [16384], P('head'), may hold values from -0.046875 to 0.046875
- step_ends: int32 [64], replicated, may hold values from 0 to 24575, as said below
Outputs:
- normed: bfloat16 [24576, 16384], P('seq', 'head')
- rewards: float32 [64], replicated
Inputs may be any that keep to these rules, and one draw needn't show every extreme that they name: `step_ends`: each is a token position of the trace; the last step ends at the trace's last token.
All inputs are finite; a program needn't handle non-finite values.
Results may differ from a plain program's by a relative error of at most 0.0034.
Values may be sent and summed in bfloat16 or wider, within the bound.
No kernel may reach another device: no remote copies, remote signals or barrier semaphores. Data moves between devices by JAX's collectives and lax.ppermute only.
A program may use at most 448 MiB of HBM per device.

v0:
```python
import jax
import jax.numpy as jnp
from jax import lax
from jax.sharding import PartitionSpec as P

HEADS = 256
HEAD_DIM = 64
STATE = 256
GROUPS = 8
SPAN = 256


def from_behind(value, axis, steps):
    count = lax.axis_size(axis)
    first, last = (max(0, -steps), min(count, count - steps))
    return lax.ppermute(value, axis, [(source, source + steps) for source in range(first, last)])


def prefix(part, axis, combine, identity):
    place = lax.axis_index(axis)
    gathered = jax.tree.map(lambda a: lax.all_gather(a, axis), part)
    state = jax.tree.map(lambda a, e: jnp.zeros_like(a) + jnp.asarray(e, a.dtype), part, identity)

    def one(turn, state):
        return combine(
            state, jax.tree.map(lambda a: lax.dynamic_index_in_dim(a, turn, 0, False), gathered)
        )

    return lax.fori_loop(0, place, one, state)


def conv_silu(tail, series, taps, offset):
    length = series.shape[0]
    width = taps.shape[0]
    padded = jnp.concatenate([tail, series], 0)
    total = jnp.zeros(series.shape, jnp.float32) + offset
    for tap in range(width):
        total = total + taps[tap] * padded[tap : tap + length].astype(jnp.float32)
    return jax.nn.silu(total).astype(jnp.bfloat16)


def span_terms(state, x_blk, b_blk, c_blk, dt_blk, log_blk):
    length = x_blk.shape[0]
    row_idx = lax.broadcasted_iota(jnp.int32, (length, length), 0)
    col_idx = lax.broadcasted_iota(jnp.int32, (length, length), 1)
    lower = row_idx >= col_idx
    running = jnp.cumsum(log_blk, axis=0)
    along = jnp.transpose(running, (1, 2, 0))
    spread = along[..., :, None] - along[..., None, :]
    decay = (
        jnp.where(lower, jnp.exp(jnp.where(lower, spread, 0.0)), 0.0)
        * jnp.transpose(dt_blk, (1, 2, 0))[..., None, :]
    )
    scores = jnp.einsum("tgn,sgn->gts", c_blk, b_blk, preferred_element_type=jnp.float32)
    mixing = (scores[:, None] * decay).astype(jnp.bfloat16)
    inner = jnp.einsum("ghts,sghp->tghp", mixing, x_blk, preferred_element_type=jnp.float32)
    carried = jnp.exp(running)[..., None] * jnp.einsum(
        "tgn,ghnp->tghp", c_blk.astype(jnp.float32), state, precision=lax.Precision.HIGHEST
    )
    weights = jnp.exp(running[-1][None] - running) * dt_blk
    scaled = (b_blk.astype(jnp.float32)[:, :, None, :] * weights[..., None]).astype(jnp.bfloat16)
    update = jnp.einsum("sghn,sghp->ghnp", scaled, x_blk, preferred_element_type=jnp.float32)
    state = jnp.exp(running[-1])[..., None, None] * state + update
    return (state, inner + carried, running)


def gated_norm(values, gate, gain):
    length = values.shape[0]
    groups_here = values.shape[1]
    grouped = values.reshape(length, groups_here, -1)
    gated = grouped * jax.nn.silu(gate.reshape(length, groups_here, -1).astype(jnp.float32))
    meansq = jnp.mean(gated * gated, axis=-1, keepdims=True)
    result = gated * lax.rsqrt(meansq + 1e-05) * gain.reshape(groups_here, -1)
    return result.reshape(length, -1).astype(jnp.bfloat16)


def join_states(earlier, later):
    return (earlier[0] + later[0], jnp.exp(later[0])[:, None, None] * earlier[1] + later[1])


def per_device(
    x_in,
    z_in,
    bc_in,
    dt_in,
    conv_x_weight,
    conv_x_bias,
    conv_bc_weight,
    conv_bc_bias,
    dt_bias,
    a_log,
    norm_gain,
    reward_w,
    step_ends,
):
    width = conv_x_weight.shape[0] - 1
    rows = x_in.shape[0]
    tail_x, tail_bc = from_behind((x_in[rows - width :], bc_in[rows - width :]), "seq", 1)
    conv_x = conv_silu(tail_x, x_in, conv_x_weight, conv_x_bias)
    conv_bc = conv_silu(tail_bc, bc_in, conv_bc_weight, conv_bc_bias)
    local_heads = dt_in.shape[1]
    per_group = HEADS // GROUPS
    groups_here = local_heads // per_group
    count = rows // SPAN
    step_size = jax.nn.softplus(dt_in + dt_bias)
    log_decay = step_size * -jnp.exp(a_log)
    blocks = (
        conv_x.reshape(count, SPAN, groups_here, per_group, HEAD_DIM),
        conv_bc[:, 0].reshape(count, SPAN, groups_here, STATE),
        conv_bc[:, 1].reshape(count, SPAN, groups_here, STATE),
        step_size.reshape(count, SPAN, groups_here, per_group),
        log_decay.reshape(count, SPAN, groups_here, per_group),
    )

    def advance(carry, items):
        state, offset = carry
        state, values, running = span_terms(state, *items)
        return ((state, offset + running[-1]), (values, running + offset))

    start = (
        jnp.zeros((groups_here, per_group, STATE, HEAD_DIM), jnp.float32),
        jnp.zeros((groups_here, per_group), jnp.float32),
    )
    (final, total), (values, absolute) = lax.scan(advance, start, blocks)
    flat_state = final.reshape(local_heads, STATE, HEAD_DIM)
    flat_total = total.reshape(local_heads)
    identity = (jnp.zeros_like(flat_total), jnp.zeros_like(flat_state))
    _, incoming = prefix((flat_total, flat_state), "seq", join_states, identity)
    incoming = incoming.reshape(groups_here, per_group, STATE, HEAD_DIM)
    c_all = conv_bc[:, 1].reshape(rows, groups_here, STATE).astype(jnp.float32)
    entering = jnp.einsum("tgn,ghnp->tghp", c_all, incoming, precision=lax.Precision.HIGHEST)
    values = (
        values.reshape(rows, groups_here, per_group, HEAD_DIM)
        + jnp.exp(absolute.reshape(rows, groups_here, per_group))[..., None] * entering
    )
    normed = gated_norm(values, z_in, norm_gain)
    offset_rows = lax.axis_index("seq") * rows
    local_pos = step_ends - offset_rows
    inside = (local_pos >= 0) & (local_pos < rows)
    picked = jnp.take(normed, jnp.clip(local_pos, 0, rows - 1), axis=0).astype(jnp.float32)
    partial_terms = jnp.where(inside, jnp.sum(picked * reward_w, axis=-1), 0.0)
    rewards = lax.psum(partial_terms, ("seq", "head"))
    return (normed, rewards)


def solution(mesh):
    return jax.shard_map(
        per_device,
        mesh=mesh,
        in_specs=(
            P("seq", "head"),
            P("seq", "head"),
            P("seq", None, "head"),
            P("seq", "head"),
            P(None, "head"),
            P("head"),
            P(None, None, "head"),
            P(None, "head"),
            P("head"),
            P("head"),
            P("head"),
            P("head"),
            P(),
        ),
        out_specs=(P("seq", "head"), P()),
        check_vma=False,
    )
```

profile of v0, /device:TPU:1, one launch (start us, length us, event | category | flops | bytes accessed | tf_op | source)
XLA Modules:
  0.0 1702.6 jit_solution(6972649322123998177)
XLA Ops:
  8.1 4.6 collective-permute-start
  30.2 15.4 multiply_convert_fusion.9
  45.6 17.9 %reshape.115 = bf16[3,256,2,32,64]{4,3,2,1,0:T(8,128)(2,1)} reshape(bf16[768,4096]{1,0:T(8,128)(2,1)} %multiply_convert_fusion.9) | data formatting | bytes 12582912 | tf_op jit(solution)/shard_map/reshape | solution.py:108
  63.6 15.1 copy.87
  78.6 356.8 %while.30 = (s32[]{:T(128)}, f32[2,32,256,64]{2,3,1,0:T(8,128)}, f32[2,32]{1,0:T(2,128)S(1)}, f32[3,256,2,32,64]{1,0,4,3,2:T(4,128)}, f32[3,256,2,32]{1,3,2,0:T(...) while((s32[]{:T(128)}, f32[2,32,256,64]{2,3,1,0:T(8,128)}, ...), condition=%wide.region_3.4_spmd.clone, body=%wide.region_0.3_spmd.clone.sunk | while | flops 4403249152 | bytes 76165056 | solution.py:124
  85.5 6.9 fusion.61
  92.4 6.3 copy.151
  98.7 90.6 %dynamic_update_slice.14 = f32[3,256,2,32,64]{1,0,4,3,2:T(4,128)} dynamic-update-slice(f32[3,256,2,32,64]{1,0,4,3,2:T(4,128)} %get-tuple-element.366, f32[1,256,2,32,64]{1,0,4,3,2:T(1,128)} %copy.151, s32[]{:T(128)} %get-tuple-element.363, s32[]{:T(128)} %constant.54.clone.1..sunk.1, s32[]{:T(128)} %constant.54.clone.1..sunk.1, s32[]{:T(128)} %constant.54.clone.1..sunk.1, s32[]{:T(128)} %constant.54.clone.1..sunk.1) | dynamic-update-slice | bytes 8388612 | tf_op jit(solution)/shard_map/while/body/jit(dynamic_update_index_in_dim)/dynamic_update_slice | solution.py:124
  189.3 6.2 multiply_add_fusion.2
  205.1 6.9 fusion.61
  212.0 6.3 copy.151
  218.3 90.6 %dynamic_update_slice.14 = f32[3,256,2,32,64]{1,0,4,3,2:T(4,128)} dynamic-update-slice(f32[3,256,2,32,64]{1,0,4,3,2:T(4,128)} %get-tuple-element.366, f32[1,256,2,32,64]{1,0,4,3,2:T(1,128)} %copy.151, s32[]{:T(128)} %get-tuple-element.363, s32[]{:T(128)} %constant.54.clone.1..sunk.1, s32[]{:T(128)} %constant.54.clone.1..sunk.1, s32[]{:T(128)} %constant.54.clone.1..sunk.1, s32[]{:T(128)} %constant.54.clone.1..sunk.1) | dynamic-update-slice | bytes 8388612 | tf_op jit(solution)/shard_map/while/body/jit(dynamic_update_index_in_dim)/dynamic_update_slice | solution.py:124
  308.9 6.2 multiply_add_fusion.2
  324.7 6.9 fusion.61
  331.6 6.3 copy.151
  337.9 90.6 %dynamic_update_slice.14 = f32[3,256,2,32,64]{1,0,4,3,2:T(4,128)} dynamic-update-slice(f32[3,256,2,32,64]{1,0,4,3,2:T(4,128)} %get-tuple-element.366, f32[1,256,2,32,64]{1,0,4,3,2:T(1,128)} %copy.151, s32[]{:T(128)} %get-tuple-element.363, s32[]{:T(128)} %constant.54.clone.1..sunk.1, s32[]{:T(128)} %constant.54.clone.1..sunk.1, s32[]{:T(128)} %constant.54.clone.1..sunk.1, s32[]{:T(128)} %constant.54.clone.1..sunk.1) | dynamic-update-slice | bytes 8388612 | tf_op jit(solution)/shard_map/while/body/jit(dynamic_update_index_in_dim)/dynamic_update_slice | solution.py:124
  428.6 6.2 multiply_add_fusion.2
  435.5 9.4 copy.95
  445.1 22.0 %reshape.93 = f32[768,2,32,64]{0,3,2,1:T(8,128)} reshape(f32[3,256,2,32,64]{1,0,4,3,2:T(4,128)} %get-tuple-element.101) | data formatting | bytes 25165824 | tf_op jit(solution)/shard_map/reshape | solution.py:133
  467.1 21.9 %all-gather = f32[32,1,64]{2,1,0:T(1,128)S(1)} all-gather(f32[1,1,64]{2,1,0:T(1,128)S(1)} %reshape.106), channel_id=1, replica_groups=mesh['seq'=32,'head'=4] {'seq'}, dimensions={0}, use_global_device_ids=true | all-gather | bytes 8448 | tf_op jit(solution)/shard_map/all_gather | solution.py:21
  489.0 324.5 %all-gather.3.cloned.1.call-done = f32[32,64,256,64]{2,3,1,0:T(8,128)} async-done(((f32[1,64,256,64]{2,3,1,0:T(8,128)}), f32[32,64,256,64]{2,3,1,0:T(8,128)}) %all-gather.3.cloned.1.call-update) | async-done | bytes 134217744 | tf_op jit(solution)/shard_map/all_gather | solution.py:21
  817.7 23.4 %while.29 = (s32[]{:T(128)}, f32[64,256,64]{2,1,0:T(8,128)}, s32[]{:T(128)}, f32[32,64]{1,0:T(8,128)S(1)}, f32[32,64,256,64]{2,3,1,0:T(8,128)}, /*index=5*/s32[]{:T(128)}, s32[]{:T(128)}, s32[]{:T(128)}) while((s32[]{:T(128)}, f32[64,256,64]{2,1,0:T(8,128)}, s32[]{:T(128)}, f32[32,64]{1,0:T(8,128)S(1)}, f32[32,64,256,64]{2,3,1,0:T(8,128)}, ...), condition=%wide.region_5.6_spmd, body=%wide.region_4.5_spmd.sunk | while | flops 2097157 | bytes 29361024 | solution.py:29
  817.7 4.8 constant_dynamic-slice_fusion.5
  822.5 6.9 copy.142
  829.4 11.7 bitcast_add_fusion.3
  841.1 29.0 %multiply_reduce_fusion = (f32[768,2]{0,1:T(2,128)S(1)}, f32[768,2,32,64]{0,3,2,1:T(8,128)}) fusion(f32[768,4096]{0,1:T(8,128)} %copy.95, f32[768,2,32,64]{0,3,2,1:T(8,128)} %reshape.93, f32[2,32,256,64]{3,2,1,0:T(8,128)} %bitcast.171, bf16[768,2,256,1]{0,2,3,1:T(8,128)(2,1)S(1)} %bitcast.177, f32[768,2,32]{0,2,1:T(8,128)S(1)} %bitcast.180), kind=kOutput, calls=%fused_computation.55 | convolution fusion | flops 9691985920 | bytes 42932224 | tf_op jit(solution)/shard_map/tgn,ghnp->tghp/dot_general | solution.py:131
  870.3 5.6 mul.249
  875.9 21.7 %copy.117 = f32[96,8,2,2048]{3,1,2,0:T(8,128)} copy(f32[96,8,2,2048]{3,2,1,0:T(2,128)} %bitcast.174) | data formatting | bytes 25165824
  897.6 12.6 copy.94
  910.2 14.6 multiply_convert_fusion.8
  924.8 5.0 gather_fusion
  930.1 765.5 %psum.7 = f32[64]{0:T(128)} all-reduce(f32[64]{0:T(128)S(1)} %and_select_fusion), channel_id=1, replica_groups=mesh['seq'=32,'head'=4] {'seq','head'}, use_global_device_ids=true, to_apply=%region_8.9 | all-reduce | flops 64 | bytes 512 | tf_op jit(solution)/shard_map/psum | solution.py:142
  (113 shorter events, 49.6 us)
Async XLA Ops:
  7.2 806.3 %all-gather.3.cloned.1.call-start = ((), (), s32[]{:S(2)}) async-start(), calls=%async_computation | async-start | bytes 138412032 | tf_op jit(solution)/shard_map/all_gather | solution.py:21
  8.1 14.8 collective-permute-start
  13.6 16.6 collective-permute-start.1
  19.1 11.1 copy-start.4
  27.3 0.9 copy-start.1
  81.1 1.9 copy-start
  200.7 1.9 copy-start
  320.3 1.9 copy-start
  435.5 9.5 copy-start.7
  445.1 22.0 %copy-start.3 = (f32[3,256,2,32]{1,3,2,0:T(8,128)S(1)}, f32[3,256,2,32]{1,3,2,0:T(8,128)}, u32[]{:S(2)}) copy-start(f32[3,256,2,32]{1,3,2,0:T(8,128)} %get-tuple-element.102) | copy-start | bytes 589828
  817.7 23.4 %copy-start.2 = (bf16[768,1,512]{0,2,1:T(8,128)(2,1)S(1)}, bf16[768,1,512]{0,2,1:T(8,128)(2,1)}, u32[]{:S(2)}) copy-start(bf16[768,1,512]{0,2,1:T(8,128)(2,1)} %copy-done.1) | copy-start | bytes 2359300
  897.6 12.7 copy-start.5
  910.2 19.6 %copy-start.6 = (f32[4096]{0:T(1024)S(1)}, f32[4096]{0:T(1024)}, u32[]{:S(2)}) copy-start(f32[4096]{0:T(1024)} %param.28) | copy-start | bytes 49156
Sparse Core Ops, SparseCore 0:
  435.6 377.7 all-gather.2
where the time goes:
time: 1720 us; the launch traced here: 1700 us
  blocking collectives  787 us (46%)
  local copies, waits for them, and re-layouts  434 us (25%)
  waiting for transfers between devices  324 us (19%)
  matrix products  75.4 us (4%)
  other arithmetic  60.2 us (4%)
    psum x1, blocking collectives, per_device(): rewards = lax.psum(partial_terms, ('seq', 'head'))  765 us
    all_gather x1, waiting for transfers between devices, prefix(): gathered = jax.tree.map(lambda a: lax.all_gather(a, axis), part)  324 us
    dynamic_update_slice x6, local copies, waits for them, and re-layouts, per_device(): (final, total), (values, absolute) = lax.scan(advance, start, blocks)  291 us
    unnamed x21, local copies, waits for them, and re-layouts  42.5 us
  transfers between devices with their start and end apart: 3, of which 1 were waited for; matrix products, arithmetic and copies ran while one was open for 3% of the time, Pallas kernels for 0%

commit v1 on v0

v1 whole, which is shorter than its diff:
```python
import functools

import jax
import jax.numpy as jnp
import numpy as np
from jax import lax
from jax.experimental import pallas as pl
from jax.experimental.pallas import tpu as pltpu
from jax.sharding import PartitionSpec as P

HEAD_DIM = 64
STATE = 256
PER_GROUP = 32
LANES = PER_GROUP * HEAD_DIM
CHUNK = 128
TAIL = 16
EXTRA = 16
TILE = 512
LOG2E = 1.4426950408889634
F32 = jnp.float32
BF16 = jnp.bfloat16
VMEM_LIMIT = 56 * 1024 * 1024


def params(*semantics):
    return pltpu.CompilerParams(
        dimension_semantics=semantics or None, vmem_limit_bytes=VMEM_LIMIT
    )


def dot(a, b, ca=1, cb=0):
    return lax.dot_general(a, b, (((ca,), (cb,)), ((), ())), preferred_element_type=F32)


def split2(v):
    high = v.astype(BF16)
    return high, (v - high.astype(F32)).astype(BF16)


def split3(v):
    high = v.astype(BF16)
    rest = v - high.astype(F32)
    mid = rest.astype(BF16)
    return high, mid, (rest - mid.astype(F32)).astype(BF16)


def silu(v):
    half = 0.5 * v
    return half + half * jnp.tanh(half)


def decay_kernel(dt_ref, ld_ref, row_ref, col_ref, ehl_ref, whl_ref, eabs_ref, wabs_ref, tot_ref):
    heads, rows = dt_ref.shape
    count = rows // CHUNK
    u = lax.broadcasted_iota(jnp.int32, (CHUNK, CHUNK), 0)
    t = lax.broadcasted_iota(jnp.int32, (CHUNK, CHUNK), 1)
    upto = (u <= t).astype(BF16)
    after = (u > t).astype(BF16)
    running, suffix, total = [], [], []
    for c in range(count):
        ld = ld_ref[:, c * CHUNK : (c + 1) * CHUNK]
        terms = jnp.concatenate(split3(ld), axis=0)
        r = dot(terms, upto)
        s = dot(terms, after)
        r = r[:heads] + r[heads : 2 * heads] + r[2 * heads :]
        s = s[:heads] + s[heads : 2 * heads] + s[2 * heads :]
        running.append(r)
        suffix.append(s)
        total.append(r[:, CHUNK - 1 :])
    before = [jnp.zeros_like(total[0])]
    for c in range(count):
        before.append(before[-1] + total[c])
    behind = [jnp.zeros_like(total[0])]
    for c in range(count - 1, 0, -1):
        behind.append(behind[-1] + total[c])
    behind = behind[::-1]

    def put(ref, v, c):
        for g in range(heads // PER_GROUP):
            part = v[g * PER_GROUP : (g + 1) * PER_GROUP]
            high, low = split2(part)
            ref[g, 0:PER_GROUP, c * CHUNK : (c + 1) * CHUNK] = high
            ref[g, PER_GROUP : 2 * PER_GROUP, c * CHUNK : (c + 1) * CHUNK] = low

    for c in range(count):
        where = slice(c * CHUNK, (c + 1) * CHUNK)
        dt = dt_ref[:, where]
        row_ref[:, where] = running[c] - jnp.log2(dt)
        col = running[c].T
        for g in range(heads // PER_GROUP):
            col_ref[g, where, :] = col[:, g * PER_GROUP : (g + 1) * PER_GROUP]
        put(ehl_ref, jnp.exp2(running[c]), c)
        put(whl_ref, jnp.exp2(suffix[c]) * dt, c)
        put(eabs_ref, jnp.exp2(running[c] + before[c]), c)
        put(wabs_ref, jnp.exp2(suffix[c] + behind[c]) * dt, c)
    tot_ref[...] = before[count] + jnp.zeros((heads, 128), F32)


def decays(dt, ld):
    heads, rows = dt.shape
    groups = heads // PER_GROUP
    pair = jax.ShapeDtypeStruct((groups, 2 * PER_GROUP, rows), BF16)
    return pl.pallas_call(
        decay_kernel,
        out_shape=[
            jax.ShapeDtypeStruct((heads, rows), F32),
            jax.ShapeDtypeStruct((groups, rows, PER_GROUP), F32),
            pair,
            pair,
            pair,
            pair,
            jax.ShapeDtypeStruct((heads, 128), F32),
        ],
        compiler_params=params(),
    )(dt, ld)


def conv_column(pad, series, tail, taps, offset, store):
    rows = series.shape[0]
    pad[0:8, :] = tail[TAIL - 8 :, :].astype(F32)
    pad[8 : 8 + rows, :] = series[...].astype(F32)
    for start in range(0, rows, CHUNK):
        total = offset[...] + taps[3:4, :] * pad[8 + start : 8 + start + CHUNK, :]
        for k in range(3):
            total = total + taps[k : k + 1, :] * pad[5 + k + start : 5 + k + start + CHUNK, :]
        store(start, silu(total))


def state_kernel(
    x_ref, xt_ref, b_ref, bt_ref, c_ref, ct_ref, wx_ref, ox_ref, wb_ref, ob_ref, wc_ref, oc_ref,
    wabs_ref, spread_ref, tot_ref,
    cx_ref, cb_ref, cc_ref, state_ref, pad, scaled, bturn,
):
    rows = x_ref.shape[0]

    @pl.when(pl.program_id(0) == 0)
    def _():
        for src, tail, taps, offset, dst in (
            (b_ref, bt_ref, wb_ref, ob_ref, cb_ref),
            (c_ref, ct_ref, wc_ref, oc_ref, cc_ref),
        ):
            for lane in range(0, STATE, 128):
                cut = (slice(None), slice(lane, lane + 128))

                def store(start, v, dst=dst, lane=lane):
                    dst[start : start + CHUNK, lane : lane + 128] = v.astype(BF16)

                conv_column(pad, src.at[cut], tail.at[cut], taps.at[cut], offset.at[cut], store)
        bturn[...] = cb_ref[...].T

    spread = spread_ref[...]
    weight = wabs_ref[0]
    for lane in range(0, TILE, 128):
        cut = (slice(None), slice(lane, lane + 128))

        def store(start, v, lane=lane):
            v = v.astype(BF16)
            cx_ref[start : start + CHUNK, lane : lane + 128] = v
            w = dot(weight[:, start : start + CHUNK], spread[:, lane : lane + 128], 0, 0)
            scaled[start : start + CHUNK, lane : lane + 128] = (w * v.astype(F32)).astype(BF16)

        conv_column(pad, x_ref.at[cut], xt_ref.at[cut], wx_ref.at[cut], ox_ref.at[cut], store)
    state_ref[0:STATE, :] = dot(bturn[...], scaled[...]).astype(BF16)
    state_ref[STATE:, :] = dot(tot_ref[0], spread[:PER_GROUP]).astype(BF16)


def local_states(g, x, x_tail, bc, bc_tail, wx, ox, wbc, obc, wabs, spread, tot):
    rows = x.shape[0]
    groups = x.shape[1] // LANES
    tiles = LANES // TILE
    lane = lambda j: (0, g * tiles + j)
    at = lambda n: lambda j: (0, n)
    part = lambda n, w: [
        pl.BlockSpec((rows, STATE), at(n)),
        pl.BlockSpec((TAIL, STATE), at(n)),
    ]
    return pl.pallas_call(
        state_kernel,
        grid=(tiles,),
        in_specs=[
            pl.BlockSpec((rows, TILE), lane),
            pl.BlockSpec((TAIL, TILE), lane),
            *part(g, STATE),
            *part(groups + g, STATE),
            pl.BlockSpec((4, TILE), lane),
            pl.BlockSpec((1, TILE), lane),
            pl.BlockSpec((4, STATE), at(g)),
            pl.BlockSpec((1, STATE), at(g)),
            pl.BlockSpec((4, STATE), at(groups + g)),
            pl.BlockSpec((1, STATE), at(groups + g)),
            pl.BlockSpec((1, 2 * PER_GROUP, rows), lambda j: (g, 0, 0)),
            pl.BlockSpec((2 * PER_GROUP, TILE), lambda j: (0, j)),
            pl.BlockSpec((1, EXTRA, PER_GROUP), lambda j: (g, 0, 0)),
        ],
        out_specs=[
            pl.BlockSpec((rows, TILE), lambda j: (0, j)),
            pl.BlockSpec((rows, STATE), lambda j: (0, 0)),
            pl.BlockSpec((rows, STATE), lambda j: (0, 0)),
            pl.BlockSpec((STATE + EXTRA, TILE), lambda j: (0, j)),
        ],
        out_shape=[
            jax.ShapeDtypeStruct((rows, LANES), BF16),
            jax.ShapeDtypeStruct((rows, STATE), BF16),
            jax.ShapeDtypeStruct((rows, STATE), BF16),
            jax.ShapeDtypeStruct((STATE + EXTRA, LANES), BF16),
        ],
        scratch_shapes=[
            pltpu.VMEM((rows + 8, 128), F32),
            pltpu.VMEM((rows, TILE), BF16),
            pltpu.VMEM((STATE, rows), BF16),
        ],
        compiler_params=params("arbitrary"),
        cost_estimate=pl.CostEstimate(
            flops=2 * rows * STATE * LANES, bytes_accessed=4 * rows * LANES, transcendentals=rows * LANES
        ),
    )(x, x_tail, bc, bc_tail, bc, bc_tail, wx, ox, wbc, obc, wbc, obc, wabs, spread, tot)


def values_kernel(
    x_ref, b_ref, c_ref, row_ref, col_ref, ehl_ref, whl_ref, spread_ref, out_ref, state, state16
):
    chunk = pl.program_id(0)

    @pl.when(chunk == 0)
    def _():
        state[...] = jnp.zeros_like(state)
        state16[...] = jnp.zeros_like(state16)

    b = b_ref[...]
    c = c_ref[...]
    scores = dot(c, b, 1, 1)
    t = lax.broadcasted_iota(jnp.int32, (CHUNK, CHUNK), 0)
    s = lax.broadcasted_iota(jnp.int32, (CHUNK, CHUNK), 1)
    scores = jnp.where(t >= s, scores, 0.0)
    bturn = b.T
    left = lax.broadcasted_iota(jnp.int32, (CHUNK, 128), 1) < HEAD_DIM
    decay = ehl_ref[0]
    weight = whl_ref[0]
    for lane in range(0, LANES, 256):
        cut = slice(lane, lane + 256)
        spread = spread_ref[:, cut]
        grown = dot(decay, spread, 0, 0)
        carried = grown * dot(c, state16[:, cut])
        for pair in range(2):
            first = lane // HEAD_DIM + 2 * pair
            at = slice(lane + 128 * pair, lane + 128 * pair + 128)
            mixes = []
            for h in (first, first + 1):
                spread_log = col_ref[0, :, h : h + 1] - row_ref[h : h + 1, :]
                mixes.append((scores * jnp.exp2(jnp.minimum(spread_log, 64.0))).astype(BF16))
            both = dot(jnp.concatenate(mixes, axis=0), x_ref[:, at])
            inner = jnp.where(left, both[:CHUNK], both[CHUNK:])
            out_ref[:, at] = (inner + carried[:, 128 * pair : 128 * pair + 128]).astype(out_ref.dtype)
        x = x_ref[:, cut].astype(F32)
        scaled = (dot(weight, spread, 0, 0) * x).astype(BF16)
        later = grown[CHUNK - 1 :, :] * state[:, cut] + dot(bturn, scaled)
        state[:, cut] = later
        state16[:, cut] = later.astype(BF16)


def local_values(g, x, b, c, row, col, ehl, whl, spread):
    rows = x.shape[0]
    return pl.pallas_call(
        values_kernel,
        grid=(rows // CHUNK,),
        in_specs=[
            pl.BlockSpec((CHUNK, LANES), lambda i: (i, 0)),
            pl.BlockSpec((CHUNK, STATE), lambda i: (i, 0)),
            pl.BlockSpec((CHUNK, STATE), lambda i: (i, 0)),
            pl.BlockSpec((PER_GROUP, CHUNK), lambda i: (g, i)),
            pl.BlockSpec((1, CHUNK, PER_GROUP), lambda i: (g, i, 0)),
            pl.BlockSpec((1, 2 * PER_GROUP, CHUNK), lambda i: (g, 0, i)),
            pl.BlockSpec((1, 2 * PER_GROUP, CHUNK), lambda i: (g, 0, i)),
            pl.BlockSpec((2 * PER_GROUP, LANES), lambda i: (0, 0)),
        ],
        out_specs=pl.BlockSpec((CHUNK, LANES), lambda i: (i, 0)),
        out_shape=jax.ShapeDtypeStruct((rows, LANES), F32),
        scratch_shapes=[pltpu.VMEM((STATE, LANES), F32), pltpu.VMEM((STATE, LANES), BF16)],
        compiler_params=params("arbitrary"),
        cost_estimate=pl.CostEstimate(
            flops=8 * rows * STATE * LANES, bytes_accessed=8 * rows * LANES, transcendentals=rows * CHUNK * PER_GROUP
        ),
    )(x, b, c, row, col, ehl, whl, spread)


def norm_kernel(values_ref, c_ref, state_ref, eabs_ref, spread_ref, z_ref, gain_ref, *rest):
    out_ref, gated = rest[-2:]
    rows = values_ref.shape[0]
    c = c_ref[...]
    decay = eabs_ref[0]
    squares = jnp.zeros((rows, 128), F32)
    for lane in range(0, LANES, 256):
        cut = slice(lane, lane + 256)
        v = values_ref[:, cut].astype(F32) + dot(decay, spread_ref[:, cut], 0, 0) * dot(c, state_ref[:, cut])
        v = v * silu(z_ref[:, cut].astype(F32))
        gated[:, cut] = v
        squares = squares + v[:, :128] * v[:, :128] + v[:, 128:] * v[:, 128:]
    scale = lax.rsqrt(jnp.sum(squares, axis=1, keepdims=True) * (1.0 / LANES) + 1e-05)
    for lane in range(0, LANES, 256):
        cut = slice(lane, lane + 256)
        out_ref[:, cut] = (gated[:, cut] * scale * gain_ref[:, cut]).astype(BF16)


def gated_norm(g, values, c, state, eabs, spread, z, gain, target):
    rows = values.shape[0]
    return pl.pallas_call(
        norm_kernel,
        grid=(rows // CHUNK,),
        in_specs=[
            pl.BlockSpec((CHUNK, LANES), lambda i: (i, 0)),
            pl.BlockSpec((CHUNK, STATE), lambda i: (i, 0)),
            pl.BlockSpec((STATE, LANES), lambda i: (0, 0)),
            pl.BlockSpec((1, 2 * PER_GROUP, CHUNK), lambda i: (g, 0, i)),
            pl.BlockSpec((2 * PER_GROUP, LANES), lambda i: (0, 0)),
            pl.BlockSpec((CHUNK, LANES), lambda i: (i, g)),
            pl.BlockSpec((1, LANES), lambda i: (0, g)),
        ]
        + ([] if target is None else [pl.BlockSpec(memory_space=pl.ANY)]),
        out_specs=pl.BlockSpec((CHUNK, LANES), lambda i: (i, g)),
        out_shape=jax.ShapeDtypeStruct(z.shape, BF16),
        scratch_shapes=[pltpu.VMEM((CHUNK, LANES), F32)],
        input_output_aliases={} if target is None else {7: 0},
        compiler_params=params("arbitrary"),
        cost_estimate=pl.CostEstimate(
            flops=2 * rows * STATE * LANES, bytes_accessed=8 * rows * LANES, transcendentals=rows * LANES
        ),
    )(values, c, state, eabs, spread, z, gain, *(() if target is None else (target,)))


def total_of(payload):
    extra = payload[STATE : STATE + 3].astype(F32)
    return extra[0:1] + extra[1:2] + extra[2:3]


def with_total(state, total):
    rows = jnp.concatenate(split3(total), axis=0)
    rows = jnp.pad(rows, ((0, EXTRA - 3), (0, 0)))
    return jnp.concatenate([state.astype(BF16), rows], axis=0)


def advance(state, payload):
    return jnp.exp2(total_of(payload)) * state + payload[:STATE].astype(F32)


def over(value, move):
    count = lax.axis_size("seq")
    return lax.ppermute(value, "seq", [(i, move(i)) for i in range(count) if move(i) is not None])


def entering_state(payload):
    place = lax.axis_index("seq")
    core, y = place % 2, place // 2 % 4
    half = LANES // 2
    quarter = half // 4
    halves = lambda n: lax.dynamic_slice_in_dim(payload, n * half, half, 1)
    mine, other = halves(core), over(halves(1 - core), lambda i: i ^ 1)
    first = jnp.where(core == 0, mine, other)
    second = jnp.where(core == 0, other, mine)
    chip = with_total(
        advance(first[:STATE].astype(F32), second), total_of(first) + total_of(second)
    )
    along_y = lambda k: lambda i: i // 8 * 8 + (i // 2 + k) % 4 * 2 + i % 2
    piece = lambda n: lax.dynamic_slice_in_dim(chip, n * quarter, quarter, 1)
    came = jnp.stack([piece(y)] + [over(piece((y + k) % 4), along_y(k)) for k in (1, 2, 3)])
    parts = [lax.dynamic_index_in_dim(came, (y - n) % 4, 0, False) for n in range(4)]
    state, total = parts[0][:STATE].astype(F32), total_of(parts[0])
    for n in range(1, 4):
        state, total = advance(state, parts[n]), total + total_of(parts[n])
    row = with_total(state, total)
    near, mid, far = (
        over(row, lambda i, k=k: i + 8 * k if i + 8 * k < 32 else None) for k in (1, 2, 3)
    )
    state = advance(advance(far[:STATE].astype(F32), mid), near)
    entering = []
    for n in range(4):
        entering.append(state.astype(BF16))
        state = advance(state, parts[n])
    entering = jnp.stack(entering)
    give = lambda n: lax.dynamic_index_in_dim(entering, n, 0, False)
    back = jnp.stack([give(y)] + [over(give((y + k) % 4), along_y(k)) for k in (1, 2, 3)])
    chip_in = jnp.concatenate(
        [lax.dynamic_index_in_dim(back, (y - n) % 4, 0, False) for n in range(4)], axis=1
    )
    later = advance(chip_in.astype(F32), first).astype(BF16)
    keep = jnp.where(core == 0, chip_in, later)
    got = over(jnp.where(core == 0, later, chip_in), lambda i: i ^ 1)
    return jnp.concatenate([jnp.where(core == 0, keep, got), jnp.where(core == 0, got, keep)], axis=1)


def per_device(
    x_in, z_in, bc_in, dt_in, conv_x_weight, conv_x_bias, conv_bc_weight, conv_bc_bias,
    dt_bias, a_log, norm_gain, reward_w, step_ends,
):
    rows, channels = x_in.shape
    groups = channels // LANES
    bc = bc_in.reshape(rows, -1)
    following = lambda v: over(v, lambda i: i + 1 if i + 1 < 32 else None)
    x_tail = following(x_in[rows - TAIL :])
    bc_tail = following(bc_in[rows - TAIL :].reshape(TAIL, -1))
    dt = jax.nn.softplus(dt_in.T + dt_bias[:, None])
    ld = dt * (-LOG2E * jnp.exp(a_log))[:, None]
    row, col, ehl, whl, eabs, wabs, tot = decays(dt, ld)
    tot = jnp.stack(split3(tot[:, 0].reshape(groups, PER_GROUP)), axis=1)
    tot = jnp.pad(tot, ((0, 0), (0, EXTRA - 3), (0, 0)))
    head = np.arange(LANES) // HEAD_DIM
    spread = jnp.asarray(np.arange(2 * PER_GROUP)[:, None] % PER_GROUP == head, BF16)
    wx, ox = conv_x_weight, conv_x_bias[None]
    wbc, obc = conv_bc_weight.reshape(4, -1), conv_bc_bias.reshape(1, -1)
    made = [
        local_states(g, x_in, x_tail, bc, bc_tail, wx, ox, wbc, obc, wabs, spread, tot)
        for g in range(groups)
    ]
    states = [entering_state(m[3]) for m in made]
    values = [
        local_values(g, m[0], m[1], m[2], row, col, ehl, whl, spread) for g, m in enumerate(made)
    ]
    normed = None
    for g, m in enumerate(made):
        normed = gated_norm(g, values[g], m[2], states[g], eabs, spread, z_in, norm_gain[None], normed)
    local_pos = step_ends - lax.axis_index("seq") * rows
    inside = (local_pos >= 0) & (local_pos < rows)
    picked = jnp.take(normed, jnp.clip(local_pos, 0, rows - 1), axis=0).astype(F32)
    terms = jnp.where(inside, jnp.sum(picked * reward_w, axis=-1), 0.0)
    devices = lax.axis_size("seq") * lax.axis_size("head")
    terms = lax.all_to_all(jnp.broadcast_to(terms, (devices, terms.shape[0])), ("seq", "head"), 0, 0)
    return normed, jnp.sum(terms, axis=0)


def solution(mesh):
    return jax.shard_map(
        per_device,
        mesh=mesh,
        in_specs=(
            P("seq", "head"),
            P("seq", "head"),
            P("seq", None, "head"),
            P("seq", "head"),
            P(None, "head"),
            P("head"),
            P(None, None, "head"),
            P(None, "head"),
            P("head"),
            P("head"),
            P("head"),
            P("head"),
            P(),
        ),
        out_specs=(P("seq", "head"), P()),
        check_vma=False,
    )
```

time: 1720 us -> 166 us (0.10)
  blocking collectives: 787 us -> 21 us
  local copies, waits for them, and re-layouts: 434 us -> 14.9 us
  waiting for transfers between devices: 324 us -> 2.13 us
  matrix products: 75.4 us -> 0 us
  Pallas kernels: 0 us -> 72.4 us
  other arithmetic: 60.2 us -> 10.7 us
  starting transfers between devices: 6.55 us -> 42.6 us
    psum x1 -> x0, blocking collectives: 765 us -> none  [per_device(): rewards = lax.psum(partial_terms, ('seq', 'head'))]
    all_gather x1 -> x0, waiting for transfers between devices: 324 us -> none  [prefix(): gathered = jax.tree.map(lambda a: lax.all_gather(a, axis), part)]
    dynamic_update_slice x6 -> x0, local copies, waits for them, and re-layouts: 291 us -> none  [per_device(): (final, total), (values, absolute) = lax.scan(advance, start, blocks)]
    pallas_call x0 -> x7, Pallas kernels: none -> 72.4 us  [the longest x2 33.2 us: local_values(): pl.pallas_call(values_kernel, grid=(rows // CHUNK,), in_specs=[pl.BlockSp...]
    dot_general x10 -> x0, matrix products: 69.1 us -> none  [the longest x1 29 us: per_device(): jnp.einsum('tgn,ghnp->tghp', c_all, incoming, precision=lax.Precision.HIG...]
    reshape x8 -> x0, local copies, waits for them, and re-layouts: 52.8 us -> none  [the longest x1 22 us: per_device(): values.reshape(rows, groups_here, per_group, HEAD_DIM)]
    unnamed x21 -> x20, local copies, waits for them, and re-layouts: 42.5 us -> 4.86 us
    ppermute x2 -> x24, starting transfers between devices: 6.52 us -> 42.6 us  [over(): lax.ppermute(value, 'seq', [(i, move(i)) for i in range(count) if move(i)...]
  transfers between devices with their start and end apart: 3 -> 24, of which waited for: 1 -> 2; matrix products, arithmetic and copies ran while one was open for 3% -> 9% of each run, Pallas kernels for 0% -> 28%
where the time goes in v1:
time: 166 us; the launch traced here: 165 us
  Pallas kernels  72.4 us (44%)
  starting transfers between devices  42.6 us (26%)
  blocking collectives  21 us (13%)
  local copies, waits for them, and re-layouts  14.9 us (9%)
  other arithmetic  10.7 us (6%)
  waiting for transfers between devices  2.13 us (1%)
    ppermute x24, starting transfers between devices, over(): lax.ppermute(value, 'seq', [(i, move(i)) for i in range(count) if move(i)...  42.6 us
    pallas_call x2, Pallas kernels, local_values(): pl.pallas_call(values_kernel, grid=(rows // CHUNK,), in_specs=[pl.BlockSp...  33.2 us
    all_to_all x1, blocking collectives, per_device(): lax.all_to_all(jnp.broadcast_to(terms, (devices, terms.shape[0])), ('seq'...  21 us
    pallas_call x2, Pallas kernels, local_states(): pl.pallas_call(state_kernel, grid=(tiles,), in_specs=[pl.BlockSpec((rows,...  18.7 us
    pallas_call x2, Pallas kernels, gated_norm(): pl.pallas_call(norm_kernel, grid=(rows // CHUNK,), in_specs=[pl.BlockSpec...  17.6 us
    gather x1, local copies, waits for them, and re-layouts, per_device(): jnp.take(normed, jnp.clip(local_pos, 0, rows - 1), axis=0).astype(F32)  4.99 us
    unnamed x20, local copies, waits for them, and re-layouts  4.86 us
  transfers between devices with their start and end apart: 24, of which 2 were waited for; matrix products, arithmetic and copies ran while one was open for 9% of the time, Pallas kernels for 28%

profile of v1, /device:TPU:1, one launch (start us, length us, event | category | flops | bytes accessed | tf_op | source)
XLA Modules:
  0.0 165.1 jit_solution(5394736395921402596)
XLA Ops:
  1.5 4.6 %collective-permute-start = (bf16[16,4096]{1,0:T(8,128)(2,1)S(1)}, bf16[16,4096]{1,0:T(8,128)(2,1)S(1)}, u32[]{:S(2)}, u32[]{:S(2)}) collective-permute-start(bf16[16,4096]{1,0:T(8,128)(2,1)S(1)} %slice.367), channel_id=1, source_target_pairs={{0,4},{4,8},{8,12},{12,16},{16,20},{20,24},{24,28},{28,32},{32,36}... | collective-permute-start | bytes 393224 | tf_op jit(solution)/shard_map/ppermute | solution.py:347
  7.0 1.9 %collective-permute-start.1 = (bf16[16,1024]{1,0:T(8,128)(2,1)S(1)}, bf16[16,1024]{1,0:T(8,128)(2,1)S(1)}, u32[]{:S(2)}, u32[]{:S(2)}) collective-permute-start(bf16[16,1024]{1,0:T(8,128)(2,1)S(1)} %bitcast.237), channel_id=1, source_target_pairs={{0,4},{4,8},{8,12},{12,16},{16,20},{20,24},{24,28},{28,32},{32,36}... | collective-permute-start | bytes 98312 | tf_op jit(solution)/shard_map/ppermute | solution.py:347
  9.6 1.9 %broadcast_multiply_fusion = (f32[64,768]{1,0:T(8,128)}, f32[64,768]{1,0:T(8,128)}) fusion(f32[64]{0:T(128)S(1)} %exponential_multiply_fusion, f32[768,64]{0,1:T(8,128)} %param.17, f32[64]{0:T(128)} %param.22), kind=kLoop, calls=%fused_computation.125 | loop fusion | flops 393216 | bytes 590336 | tf_op jit(solution)/shard_map/mul | solution.py:401
  11.4 2.8 %shard_map.149 = (f32[64,768]{1,0:T(8,128)}, f32[2,768,32]{2,1,0:T(8,128)}, bf16[2,64,768]{2,1,0:T(8,128)(2,1)}, bf16[2,64,768]{2,1,0:T(8,128)(2,1)}, bf16[2,64,...) custom-call(f32[64,768]{1,0:T(8,128)} %get-tuple-element.55.dt_ref, ...), custom_call_target="tpu_custom_call" | custom-call | tf_op jit(solution)/shard_map/pallas_call | solution.py:103
  16.5 3.0 %copy.27 = bf16[96,8,2,512]{3,1,2,0:T(8,128)(2,1)} copy(bf16[96,8,2,512]{3,2,1,0:T(2,128)(2,1)} %bitcast.207) | data formatting | bytes 3145728
  21.4 9.4 %shard_map.152 = (bf16[768,2048]{1,0:T(8,128)(2,1)}, bf16[768,256]{1,0:T(8,128)(2,1)}, bf16[768,256]{1,0:T(8,128)(2,1)}, bf16[272,2048]{1,0:T(8,128)(2,1)}) custom-call(bf16[768,4096]{1,0:T(8,128)(2,1)} %x_ref.3, bf16[16,4096]{1,0:T(8,128)(2,1)} %copy-done.2, bf16[768,1024]{1,0:T(8,128)(2,1)} %bitcast.203, bf16[16,1024]{1,0:T(8,128)(2,1)} %copy-done.3, ...), custom_call_target="tpu_custom_call" | custom-call | flops 805306368 | bytes 6291456 | tf_op jit(solution)/shard_map/pallas_call | solution.py:177
  30.8 1.1 constant_dynamic-slice_fusion.7
  32.4 9.3 %shard_map.150 = (bf16[768,2048]{1,0:T(8,128)(2,1)}, bf16[768,256]{1,0:T(8,128)(2,1)}, bf16[768,256]{1,0:T(8,128)(2,1)}, bf16[272,2048]{1,0:T(8,128)(2,1)}) custom-call(bf16[768,4096]{1,0:T(8,128)(2,1)} %x_ref.3, bf16[16,4096]{1,0:T(8,128)(2,1)} %copy-done.2, bf16[768,1024]{1,0:T(8,128)(2,1)} %bitcast.205, bf16[16,1024]{1,0:T(8,128)(2,1)} %copy-done.3, ...), custom_call_target="tpu_custom_call" | custom-call | flops 805306368 | bytes 6291456 | tf_op jit(solution)/shard_map/pallas_call | solution.py:177
  41.8 1.1 constant_dynamic-slice_fusion.11
  43.2 16.6 %shard_map.153.values_ref = f32[768,2048]{1,0:T(8,128)} custom-call(bf16[768,2048]{1,0:T(8,128)(2,1)} %get-tuple-element.28.x_ref, bf16[768,256]{1,0:T(8,128)(2,1)} %get-tuple-element.29.b_ref, bf16[768,256]{1,0:T(8,128)(2,1)} %get-tuple-element.30.c_ref, f32[64,768]{1,0:T(8,128)} %get-tuple-element.22.row_ref, f32[2,768,32]{2,1,0:T(8,128)} %get-tuple-element.23.col_ref, ...), custom_call_target="tpu_custom_call" | custom-call | flops 3221225472 | bytes 12582912 | tf_op jit(solution)/shard_map/pallas_call | solution.py:263
  60.6 1.4 collective-permute-start.14
  62.0 2.2 %collective-permute-start.15 = (bf16[272,256]{1,0:T(8,128)(2,1)S(1)}, bf16[272,256]{1,0:T(8,128)(2,1)S(1)}, u32[]{:S(2)}, u32[]{:S(2)}) collective-permute-start(bf16[272,256]{1,0:T(8,128)(2,1)S(1)} %get-tuple-element.76), channel_id=1, source_target_pairs={{0,16},{4,20},{8,24},{12,28},{16,0},{20,4},{24,8},{28,12},{32,48},... | collective-permute-start | bytes 417800 | tf_op jit(solution)/shard_map/ppermute | solution.py:347
  64.2 1.2 collective-permute-start.16
  67.3 1.7 %collective-permute-start.5 = (bf16[272,256]{1,0:T(8,128)(2,1)S(1)}, bf16[272,256]{1,0:T(8,128)(2,1)S(1)}, u32[]{:S(2)}, u32[]{:S(2)}) collective-permute-start(bf16[272,256]{1,0:T(8,128)(2,1)S(1)} %get-tuple-element.85), channel_id=1, source_target_pairs={{0,24},{4,28},{8,0},{12,4},{16,8},{20,12},{24,16},{28,20},{32,56},... | collective-permute-start | bytes 417800 | tf_op jit(solution)/shard_map/ppermute | solution.py:347
  69.1 1.6 collective-permute-done.15
  71.0 3.1 %collective-permute-start.17 = (bf16[272,256]{1,0:T(8,128)(2,1)S(1)}, bf16[272,256]{1,0:T(8,128)(2,1)S(1)}, u32[]{:S(2)}, u32[]{:S(2)}) collective-permute-start(bf16[272,256]{1,0:T(8,128)(2,1)S(1)} %pad_maximum_fusion.11), channel_id=1, source_target_pairs={{0,32},{4,36},{8,40},{12,44},{16,48},{20,52},{24,56},{28,60},{32,6... | collective-permute-start | bytes 417800 | tf_op jit(solution)/shard_map/ppermute | solution.py:347
  74.1 3.8 %collective-permute-start.18 = (bf16[272,256]{1,0:T(8,128)(2,1)S(1)}, bf16[272,256]{1,0:T(8,128)(2,1)S(1)}, u32[]{:S(2)}, u32[]{:S(2)}) collective-permute-start(bf16[272,256]{1,0:T(8,128)(2,1)S(1)} %pad_maximum_fusion.11), channel_id=1, source_target_pairs={{0,64},{4,68},{8,72},{12,76},{16,80},{20,84},{24,88},{28,92},{32,9... | collective-permute-start | bytes 417800 | tf_op jit(solution)/shard_map/ppermute | solution.py:347
  78.0 1.3 collective-permute-start.19
  79.6 1.3 collective-permute-start.6
  80.9 3.0 %collective-permute-start.7 = (bf16[272,256]{1,0:T(8,128)(2,1)S(1)}, bf16[272,256]{1,0:T(8,128)(2,1)S(1)}, u32[]{:S(2)}, u32[]{:S(2)}) collective-permute-start(bf16[272,256]{1,0:T(8,128)(2,1)S(1)} %pad_maximum_fusion.10), channel_id=1, source_target_pairs={{0,64},{4,68},{8,72},{12,76},{16,80},{20,84},{24,88},{28,92},{32,9... | collective-permute-start | bytes 417800 | tf_op jit(solution)/shard_map/ppermute | solution.py:347
  84.0 1.3 collective-permute-start.8
  85.7 1.8 %collective-permute-start.20 = (bf16[256,256]{1,0:T(8,128)(2,1)S(1)}, bf16[256,256]{1,0:T(8,128)(2,1)S(1)}, u32[]{:S(2)}, u32[]{:S(2)}) collective-permute-start(bf16[256,256]{1,0:T(8,128)(2,1)S(1)} %get-tuple-element.93), channel_id=1, source_target_pairs={{0,8},{4,12},{8,16},{12,20},{16,24},{20,28},{24,0},{28,4},{32,40},... | collective-permute-start | bytes 393224 | tf_op jit(solution)/shard_map/ppermute | solution.py:347
  87.5 2.3 %collective-permute-start.21 = (bf16[256,256]{1,0:T(8,128)(2,1)S(1)}, bf16[256,256]{1,0:T(8,128)(2,1)S(1)}, u32[]{:S(2)}, u32[]{:S(2)}) collective-permute-start(bf16[256,256]{1,0:T(8,128)(2,1)S(1)} %get-tuple-element.92), channel_id=1, source_target_pairs={{0,16},{4,20},{8,24},{12,28},{16,0},{20,4},{24,8},{28,12},{32,48},... | collective-permute-start | bytes 393224 | tf_op jit(solution)/shard_map/ppermute | solution.py:347
  91.8 1.9 %collective-permute-start.10 = (bf16[256,256]{1,0:T(8,128)(2,1)S(1)}, bf16[256,256]{1,0:T(8,128)(2,1)S(1)}, u32[]{:S(2)}, u32[]{:S(2)}) collective-permute-start(bf16[256,256]{1,0:T(8,128)(2,1)S(1)} %get-tuple-element.100), channel_id=1, source_target_pairs={{0,16},{4,20},{8,24},{12,28},{16,0},{20,4},{24,8},{28,12},{32,48},... | collective-permute-start | bytes 393224 | tf_op jit(solution)/shard_map/ppermute | solution.py:347
  94.9 4.9 %collective-permute-start.23 = (bf16[256,1024]{1,0:T(8,128)(2,1)S(1)}, bf16[256,1024]{1,0:T(8,128)(2,1)S(1)}, u32[]{:S(2)}, u32[]{:S(2)}) collective-permute-start(bf16[256,1024]{1,0:T(8,128)(2,1)S(1)} %fusion.6), channel_id=1, source_target_pairs={{0,4},{4,0},{8,12},{12,8},{16,20},{20,16},{24,28},{28,24},{32,36},... | collective-permute-start | bytes 1572872 | tf_op jit(solution)/shard_map/ppermute | solution.py:347
  99.9 16.6 %shard_map.151.values_ref = f32[768,2048]{1,0:T(8,128)} custom-call(bf16[768,2048]{1,0:T(8,128)(2,1)} %get-tuple-element.19.x_ref, bf16[768,256]{1,0:T(8,128)(2,1)} %get-tuple-element.20.b_ref, bf16[768,256]{1,0:T(8,128)(2,1)} %get-tuple-element.21.c_ref, f32[64,768]{1,0:T(8,128)} %get-tuple-element.22.row_ref, f32[2,768,32]{2,1,0:T(8,128)} %get-tuple-element.23.col_ref, ...), custom_call_target="tpu_custom_call" | custom-call | flops 3221225472 | bytes 12582912 | tf_op jit(solution)/shard_map/pallas_call | solution.py:263
  117.5 1.1 pad_maximum_fusion.1.state_ref
  119.4 1.1 pad_maximum_fusion.state_ref
  120.4 8.8 %shard_map.154.rest_0_ = bf16[768,4096]{1,0:T(8,128)(2,1)} custom-call(f32[768,2048]{1,0:T(8,128)} %shard_map.153.values_ref, bf16[768,256]{1,0:T(8,128)(2,1)} %get-tuple-element.30.c_ref, bf16[256,2048]{1,0:T(8,128)(2,1)} %pad_maximum_fusion.1.state_ref, bf16[2,64,768]{2,1,0:T(8,128)(2,1)} %get-tuple-element.27.eabs_ref, ...), custom_call_target="tpu_custom_call" | custom-call | flops 805306368 | bytes 12582912 | tf_op jit(solution)/shard_map/pallas_call | solution.py:306
  129.2 8.8 %shard_map.155 = bf16[768,4096]{1,0:T(8,128)(2,1)} custom-call(f32[768,2048]{1,0:T(8,128)} %shard_map.151.values_ref, bf16[768,256]{1,0:T(8,128)(2,1)} %get-tuple-element.21.c_ref, bf16[256,2048]{1,0:T(8,128)(2,1)} %pad_maximum_fusion.state_ref, bf16[2,64,768]{2,1,0:T(8,128)(2,1)} %get-tuple-element.27.eabs_ref, ...), custom_call_target="tpu_custom_call", output_to_operand_aliasing={{}: (7, {})} | custom-call | flops 805306368 | bytes 12582912 | tf_op jit(solution)/shard_map/pallas_call | solution.py:306
  138.0 5.0 %gather_fusion = bf16[64,4096]{1,0:T(8,128)(2,1)S(1)} fusion(bf16[768,4096]{1,0:T(8,128)(2,1)} %shard_map.155, s32[1024]{0:T(1024)S(1)} %pad_clamp_fusion), kind=kCustom, calls=%fused_computation | custom fusion | bytes 1048832 | tf_op jit(solution)/shard_map/jit(_take)/gather | solution.py:422
  143.4 21.0 %all_to_all.6 = f32[128,1,64]{2,1,0:T(1,128)S(1)} all-to-all(f32[128,1,64]{2,1,0:T(1,128)S(1)} %broadcast_in_dim.35), channel_id=1, replica_groups=mesh['seq'=32,'head'=4] {'seq','head'}, dimensions={0} | all-to-all | bytes 65536 | tf_op jit(solution)/shard_map/all_to_all | solution.py:425
  (124 shorter events, 16.9 us)
Async XLA Ops:
  1.5 19.2 %collective-permute-start = (bf16[16,4096]{1,0:T(8,128)(2,1)S(1)}, bf16[16,4096]{1,0:T(8,128)(2,1)S(1)}, u32[]{:S(2)}, u32[]{:S(2)}) collective-permute-start(bf16[16,4096]{1,0:T(8,128)(2,1)S(1)} %slice.367), channel_id=1, source_target_pairs={{0,4},{4,8},{8,12},{12,16},{16,20},{20,24},{24,28},{28,32},{32,36}... | collective-permute-start | bytes 393224 | tf_op jit(solution)/shard_map/ppermute | solution.py:347
  7.0 13.8 %collective-permute-start.1 = (bf16[16,1024]{1,0:T(8,128)(2,1)S(1)}, bf16[16,1024]{1,0:T(8,128)(2,1)S(1)}, u32[]{:S(2)}, u32[]{:S(2)}) collective-permute-start(bf16[16,1024]{1,0:T(8,128)(2,1)S(1)} %bitcast.237), channel_id=1, source_target_pairs={{0,4},{4,8},{8,12},{12,16},{16,20},{20,24},{24,28},{28,32},{32,36}... | collective-permute-start | bytes 98312 | tf_op jit(solution)/shard_map/ppermute | solution.py:347
  9.6 10.0 %copy-start.5 = (f32[4,2,512]{2,1,0:T(2,128)S(1)}, f32[4,2,512]{2,1,0:T(2,128)}, u32[]{:S(2)}) copy-start(f32[4,2,512]{2,1,0:T(2,128)} %param.20) | copy-start | bytes 49156
  9.6 10.6 %copy-start.6 = (f32[2,512]{1,0:T(2,128)S(1)}, f32[2,512]{1,0:T(2,128)}, u32[]{:S(2)}) copy-start(f32[2,512]{1,0:T(2,128)} %param.21) | copy-start | bytes 12292
  20.7 0.6 copy-start.3
  20.7 0.6 copy-start.2
  31.9 28.0 %collective-permute-start.13 = (bf16[272,1024]{1,0:T(8,128)(2,1)S(1)}, bf16[272,1024]{1,0:T(8,128)(2,1)S(1)}, u32[]{:S(2)}, u32[]{:S(2)}) collective-permute-start(bf16[272,1024]{1,0:T(8,128)(2,1)S(1)} %constant_dynamic-slice_fusion.7), channel_id=1, source_target_pairs={{0,4},{4,0},{8,12},{12,8},{16,20},{20,16},{24,28},{28,24},{32,36},... | collective-permute-start | bytes 1671176 | tf_op jit(solution)/shard_map/ppermute | solution.py:347
  42.9 22.5 %collective-permute-start.2 = (bf16[272,1024]{1,0:T(8,128)(2,1)S(1)}, bf16[272,1024]{1,0:T(8,128)(2,1)S(1)}, u32[]{:S(2)}, u32[]{:S(2)}) collective-permute-start(bf16[272,1024]{1,0:T(8,128)(2,1)S(1)} %constant_dynamic-slice_fusion.11), channel_id=1, source_target_pairs={{0,4},{4,0},{8,12},{12,8},{16,20},{20,16},{24,28},{28,24},{32,36},... | collective-permute-start | bytes 1671176 | tf_op jit(solution)/shard_map/ppermute | solution.py:347
  43.2 16.7 %copy-start = (bf16[272,2048]{1,0:T(8,128)(2,1)S(1)}, bf16[272,2048]{1,0:T(8,128)(2,1)}, u32[]{:S(2)}) copy-start(bf16[272,2048]{1,0:T(8,128)(2,1)} %get-tuple-element.31) | copy-start | bytes 3342340
  59.8 5.5 %copy-start.1 = (bf16[272,2048]{1,0:T(8,128)(2,1)S(1)}, bf16[272,2048]{1,0:T(8,128)(2,1)}, u32[]{:S(2)}) copy-start(bf16[272,2048]{1,0:T(8,128)(2,1)} %get-tuple-element.26) | copy-start | bytes 3342340
  60.6 6.8 %collective-permute-start.14 = (bf16[272,256]{1,0:T(8,128)(2,1)S(1)}, bf16[272,256]{1,0:T(8,128)(2,1)S(1)}, u32[]{:S(2)}, u32[]{:S(2)}) collective-permute-start(bf16[272,256]{1,0:T(8,128)(2,1)S(1)} %get-tuple-element.75), channel_id=1, source_target_pairs={{0,8},{4,12},{8,16},{12,20},{16,24},{20,28},{24,0},{28,4},{32,40},... | collective-permute-start | bytes 417800 | tf_op jit(solution)/shard_map/ppermute | solution.py:347
  62.0 8.7 %collective-permute-start.15 = (bf16[272,256]{1,0:T(8,128)(2,1)S(1)}, bf16[272,256]{1,0:T(8,128)(2,1)S(1)}, u32[]{:S(2)}, u32[]{:S(2)}) collective-permute-start(bf16[272,256]{1,0:T(8,128)(2,1)S(1)} %get-tuple-element.76), channel_id=1, source_target_pairs={{0,16},{4,20},{8,24},{12,28},{16,0},{20,4},{24,8},{28,12},{32,48},... | collective-permute-start | bytes 417800 | tf_op jit(solution)/shard_map/ppermute | solution.py:347
  64.2 6.5 %collective-permute-start.16 = (bf16[272,256]{1,0:T(8,128)(2,1)S(1)}, bf16[272,256]{1,0:T(8,128)(2,1)S(1)}, u32[]{:S(2)}, u32[]{:S(2)}) collective-permute-start(bf16[272,256]{1,0:T(8,128)(2,1)S(1)} %get-tuple-element.77), channel_id=1, source_target_pairs={{0,24},{4,28},{8,0},{12,4},{16,8},{20,12},{24,16},{28,20},{32,56},... | collective-permute-start | bytes 417800 | tf_op jit(solution)/shard_map/ppermute | solution.py:347
  66.1 11.9 %collective-permute-start.3 = (bf16[272,256]{1,0:T(8,128)(2,1)S(1)}, bf16[272,256]{1,0:T(8,128)(2,1)S(1)}, u32[]{:S(2)}, u32[]{:S(2)}) collective-permute-start(bf16[272,256]{1,0:T(8,128)(2,1)S(1)} %get-tuple-element.83), channel_id=1, source_target_pairs={{0,8},{4,12},{8,16},{12,20},{16,24},{20,28},{24,0},{28,4},{32,40},... | collective-permute-start | bytes 417800 | tf_op jit(solution)/shard_map/ppermute | solution.py:347
  66.4 12.9 %collective-permute-start.4 = (bf16[272,256]{1,0:T(8,128)(2,1)S(1)}, bf16[272,256]{1,0:T(8,128)(2,1)S(1)}, u32[]{:S(2)}, u32[]{:S(2)}) collective-permute-start(bf16[272,256]{1,0:T(8,128)(2,1)S(1)} %get-tuple-element.84), channel_id=1, source_target_pairs={{0,16},{4,20},{8,24},{12,28},{16,0},{20,4},{24,8},{28,12},{32,48},... | collective-permute-start | bytes 417800 | tf_op jit(solution)/shard_map/ppermute | solution.py:347
  67.3 11.9 %collective-permute-start.5 = (bf16[272,256]{1,0:T(8,128)(2,1)S(1)}, bf16[272,256]{1,0:T(8,128)(2,1)S(1)}, u32[]{:S(2)}, u32[]{:S(2)}) collective-permute-start(bf16[272,256]{1,0:T(8,128)(2,1)S(1)} %get-tuple-element.85), channel_id=1, source_target_pairs={{0,24},{4,28},{8,0},{12,4},{16,8},{20,12},{24,16},{28,20},{32,56},... | collective-permute-start | bytes 417800 | tf_op jit(solution)/shard_map/ppermute | solution.py:347
  71.0 13.0 %collective-permute-start.17 = (bf16[272,256]{1,0:T(8,128)(2,1)S(1)}, bf16[272,256]{1,0:T(8,128)(2,1)S(1)}, u32[]{:S(2)}, u32[]{:S(2)}) collective-permute-start(bf16[272,256]{1,0:T(8,128)(2,1)S(1)} %pad_maximum_fusion.11), channel_id=1, source_target_pairs={{0,32},{4,36},{8,40},{12,44},{16,48},{20,52},{24,56},{28,60},{32,6... | collective-permute-start | bytes 417800 | tf_op jit(solution)/shard_map/ppermute | solution.py:347
  74.1 11.2 %collective-permute-start.18 = (bf16[272,256]{1,0:T(8,128)(2,1)S(1)}, bf16[272,256]{1,0:T(8,128)(2,1)S(1)}, u32[]{:S(2)}, u32[]{:S(2)}) collective-permute-start(bf16[272,256]{1,0:T(8,128)(2,1)S(1)} %pad_maximum_fusion.11), channel_id=1, source_target_pairs={{0,64},{4,68},{8,72},{12,76},{16,80},{20,84},{24,88},{28,92},{32,9... | collective-permute-start | bytes 417800 | tf_op jit(solution)/shard_map/ppermute | solution.py:347
  78.0 7.4 %collective-permute-start.19 = (bf16[272,256]{1,0:T(8,128)(2,1)S(1)}, bf16[272,256]{1,0:T(8,128)(2,1)S(1)}, u32[]{:S(2)}, u32[]{:S(2)}) collective-permute-start(bf16[272,256]{1,0:T(8,128)(2,1)S(1)} %pad_maximum_fusion.11), channel_id=1, source_target_pairs={{0,96},{4,100},{8,104},{12,108},{16,112},{20,116},{24,120},{28,124... | collective-permute-start | bytes 417800 | tf_op jit(solution)/shard_map/ppermute | solution.py:347
  79.6 10.2 %collective-permute-start.6 = (bf16[272,256]{1,0:T(8,128)(2,1)S(1)}, bf16[272,256]{1,0:T(8,128)(2,1)S(1)}, u32[]{:S(2)}, u32[]{:S(2)}) collective-permute-start(bf16[272,256]{1,0:T(8,128)(2,1)S(1)} %pad_maximum_fusion.10), channel_id=1, source_target_pairs={{0,32},{4,36},{8,40},{12,44},{16,48},{20,52},{24,56},{28,60},{32,6... | collective-permute-start | bytes 417800 | tf_op jit(solution)/shard_map/ppermute | solution.py:347
  80.9 9.7 %collective-permute-start.7 = (bf16[272,256]{1,0:T(8,128)(2,1)S(1)}, bf16[272,256]{1,0:T(8,128)(2,1)S(1)}, u32[]{:S(2)}, u32[]{:S(2)}) collective-permute-start(bf16[272,256]{1,0:T(8,128)(2,1)S(1)} %pad_maximum_fusion.10), channel_id=1, source_target_pairs={{0,64},{4,68},{8,72},{12,76},{16,80},{20,84},{24,88},{28,92},{32,9... | collective-permute-start | bytes 417800 | tf_op jit(solution)/shard_map/ppermute | solution.py:347
  84.0 6.7 %collective-permute-start.8 = (bf16[272,256]{1,0:T(8,128)(2,1)S(1)}, bf16[272,256]{1,0:T(8,128)(2,1)S(1)}, u32[]{:S(2)}, u32[]{:S(2)}) collective-permute-start(bf16[272,256]{1,0:T(8,128)(2,1)S(1)} %pad_maximum_fusion.10), channel_id=1, source_target_pairs={{0,96},{4,100},{8,104},{12,108},{16,112},{20,116},{24,120},{28,124... | collective-permute-start | bytes 417800 | tf_op jit(solution)/shard_map/ppermute | solution.py:347
  85.7 8.0 %collective-permute-start.20 = (bf16[256,256]{1,0:T(8,128)(2,1)S(1)}, bf16[256,256]{1,0:T(8,128)(2,1)S(1)}, u32[]{:S(2)}, u32[]{:S(2)}) collective-permute-start(bf16[256,256]{1,0:T(8,128)(2,1)S(1)} %get-tuple-element.93), channel_id=1, source_target_pairs={{0,8},{4,12},{8,16},{12,20},{16,24},{20,28},{24,0},{28,4},{32,40},... | collective-permute-start | bytes 393224 | tf_op jit(solution)/shard_map/ppermute | solution.py:347
  87.5 7.1 %collective-permute-start.21 = (bf16[256,256]{1,0:T(8,128)(2,1)S(1)}, bf16[256,256]{1,0:T(8,128)(2,1)S(1)}, u32[]{:S(2)}, u32[]{:S(2)}) collective-permute-start(bf16[256,256]{1,0:T(8,128)(2,1)S(1)} %get-tuple-element.92), channel_id=1, source_target_pairs={{0,16},{4,20},{8,24},{12,28},{16,0},{20,4},{24,8},{28,12},{32,48},... | collective-permute-start | bytes 393224 | tf_op jit(solution)/shard_map/ppermute | solution.py:347
  89.8 4.8 %collective-permute-start.22 = (bf16[256,256]{1,0:T(8,128)(2,1)S(1)}, bf16[256,256]{1,0:T(8,128)(2,1)S(1)}, u32[]{:S(2)}, u32[]{:S(2)}) collective-permute-start(bf16[256,256]{1,0:T(8,128)(2,1)S(1)} %get-tuple-element.91), channel_id=1, source_target_pairs={{0,24},{4,28},{8,0},{12,4},{16,8},{20,12},{24,16},{28,20},{32,56},... | collective-permute-start | bytes 393224 | tf_op jit(solution)/shard_map/ppermute | solution.py:347
  91.1 25.4 %collective-permute-start.9 = (bf16[256,256]{1,0:T(8,128)(2,1)S(1)}, bf16[256,256]{1,0:T(8,128)(2,1)S(1)}, u32[]{:S(2)}, u32[]{:S(2)}) collective-permute-start(bf16[256,256]{1,0:T(8,128)(2,1)S(1)} %get-tuple-element.101), channel_id=1, source_target_pairs={{0,8},{4,12},{8,16},{12,20},{16,24},{20,28},{24,0},{28,4},{32,40},... | collective-permute-start | bytes 393224 | tf_op jit(solution)/shard_map/ppermute | solution.py:347
  91.8 24.6 %collective-permute-start.10 = (bf16[256,256]{1,0:T(8,128)(2,1)S(1)}, bf16[256,256]{1,0:T(8,128)(2,1)S(1)}, u32[]{:S(2)}, u32[]{:S(2)}) collective-permute-start(bf16[256,256]{1,0:T(8,128)(2,1)S(1)} %get-tuple-element.100), channel_id=1, source_target_pairs={{0,16},{4,20},{8,24},{12,28},{16,0},{20,4},{24,8},{28,12},{32,48},... | collective-permute-start | bytes 393224 | tf_op jit(solution)/shard_map/ppermute | solution.py:347
  93.7 22.7 %collective-permute-start.11 = (bf16[256,256]{1,0:T(8,128)(2,1)S(1)}, bf16[256,256]{1,0:T(8,128)(2,1)S(1)}, u32[]{:S(2)}, u32[]{:S(2)}) collective-permute-start(bf16[256,256]{1,0:T(8,128)(2,1)S(1)} %get-tuple-element.99), channel_id=1, source_target_pairs={{0,24},{4,28},{8,0},{12,4},{16,8},{20,12},{24,16},{28,20},{32,56},... | collective-permute-start | bytes 393224 | tf_op jit(solution)/shard_map/ppermute | solution.py:347
  94.9 22.2 %collective-permute-start.23 = (bf16[256,1024]{1,0:T(8,128)(2,1)S(1)}, bf16[256,1024]{1,0:T(8,128)(2,1)S(1)}, u32[]{:S(2)}, u32[]{:S(2)}) collective-permute-start(bf16[256,1024]{1,0:T(8,128)(2,1)S(1)} %fusion.6), channel_id=1, source_target_pairs={{0,4},{4,0},{8,12},{12,8},{16,20},{20,16},{24,28},{28,24},{32,36},... | collective-permute-start | bytes 1572872 | tf_op jit(solution)/shard_map/ppermute | solution.py:347
  116.8 2.2 %collective-permute-start.12 = (bf16[256,1024]{1,0:T(8,128)(2,1)S(1)}, bf16[256,1024]{1,0:T(8,128)(2,1)S(1)}, u32[]{:S(2)}, u32[]{:S(2)}) collective-permute-start(bf16[256,1024]{1,0:T(8,128)(2,1)S(1)} %fusion.8), channel_id=1, source_target_pairs={{0,4},{4,0},{8,12},{12,8},{16,20},{20,16},{24,28},{28,24},{32,36},... | collective-permute-start | bytes 1572872 | tf_op jit(solution)/shard_map/ppermute | solution.py:347
  138.0 5.0 %copy-start.4 = (f32[4096]{0:T(1024)S(1)}, f32[4096]{0:T(1024)}, u32[]{:S(2)}) copy-start(f32[4096]{0:T(1024)} %param.25) | copy-start | bytes 49156
  138.0 5.3 %copy-start.7 = (s32[64]{0:T(128)S(1)}, s32[64]{0:T(128)}, u32[]{:S(2)}) copy-start(s32[64]{0:T(128)} %param.26) | copy-start | bytes 772

commit v2 on v1

v2 whole, which is shorter than its diff:
```python
import functools

import jax
import jax.numpy as jnp
import numpy as np
from jax import lax
from jax.experimental import pallas as pl
from jax.experimental.pallas import tpu as pltpu
from jax.sharding import PartitionSpec as P

HEAD_DIM = 64
STATE = 256
PER_GROUP = 32
LANES = PER_GROUP * HEAD_DIM
CHUNK = 128
TAIL = 16
EXTRA = 16
TILE = 512
ROWS = 256
BLOCK = 2 * CHUNK
VTILE = 512
HALVES = 1
LOG2E = 1.4426950408889634
F32 = jnp.float32
BF16 = jnp.bfloat16
VMEM_LIMIT = 56 * 1024 * 1024


def params(*semantics):
    return pltpu.CompilerParams(
        dimension_semantics=semantics or None, vmem_limit_bytes=VMEM_LIMIT
    )


def dot(a, b, ca=1, cb=0):
    return lax.dot_general(a, b, (((ca,), (cb,)), ((), ())), preferred_element_type=F32)


def split2(v):
    high = v.astype(BF16)
    return high, (v - high.astype(F32)).astype(BF16)


def split3(v):
    high = v.astype(BF16)
    rest = v - high.astype(F32)
    mid = rest.astype(BF16)
    return high, mid, (rest - mid.astype(F32)).astype(BF16)


def silu(v):
    half = 0.5 * v
    return half + half * jnp.tanh(half)


def decay_kernel(
    dtin_ref, bias_ref, alog_ref, run_ref, row_ref, ehl_ref, whl_ref, eabs_ref, wabs_ref, tot_ref
):
    heads, rows = dtin_ref.shape
    count = rows // CHUNK
    h0 = lax.broadcasted_iota(jnp.int32, (heads, heads), 0)
    h1 = lax.broadcasted_iota(jnp.int32, (heads, heads), 1)
    upright = lambda v: jnp.sum(jnp.where(h0 == h1, v, 0.0), axis=1, keepdims=True)
    bias = upright(bias_ref[...])
    rate = upright(-LOG2E * jnp.exp(alog_ref[...]))
    u = lax.broadcasted_iota(jnp.int32, (CHUNK, CHUNK), 0)
    t = lax.broadcasted_iota(jnp.int32, (CHUNK, CHUNK), 1)
    upto = (u <= t).astype(BF16)
    after = (u > t).astype(BF16)
    steps, running, suffix, kept = [], [], [], []
    for c in range(count):
        v = dtin_ref[:, c * CHUNK : (c + 1) * CHUNK] + bias
        dt = jnp.maximum(v, 0.0) + jnp.log1p(jnp.exp(-jnp.abs(v)))
        terms = jnp.concatenate(split3(dt * rate), axis=0)
        r = dot(terms, upto)
        s = dot(terms, after)
        r = r[:heads] + r[heads : 2 * heads] + r[2 * heads :]
        s = s[:heads] + s[heads : 2 * heads] + s[2 * heads :]
        steps.append(dt)
        running.append(r)
        suffix.append(s)
    def put(ref, v, c):
        where = slice(c * CHUNK, (c + 1) * CHUNK)
        ref[where, 0:heads], ref[where, heads : 2 * heads] = split2(v)

    whole = jnp.zeros((1, heads), F32)
    for c in range(count):
        where = slice(c * CHUNK, (c + 1) * CHUNK)
        run_ref[:, where] = running[c]
        row_ref[:, where] = running[c] - jnp.log2(steps[c])
        run, rest, dt = running[c].T, suffix[c].T, steps[c].T
        grown, weight = jnp.exp2(run), jnp.exp2(rest) * dt
        put(ehl_ref, grown, c)
        put(whl_ref, weight, c)
        put(eabs_ref, grown * jnp.exp2(whole), c)
        whole = whole + run[CHUNK - 1 :, :]
        kept.append((weight, run[CHUNK - 1 :, :]))
    later = jnp.zeros((1, heads), F32)
    for c in range(count - 1, -1, -1):
        put(wabs_ref, kept[c][0] * jnp.exp2(later), c)
        later = later + kept[c][1]
    high, mid, low = split3(whole)
    place = lax.broadcasted_iota(jnp.int32, (EXTRA, heads), 0)
    terms = jnp.where(
        place == 0,
        high.astype(F32),
        jnp.where(place == 1, mid.astype(F32), jnp.where(place == 2, low.astype(F32), 0.0)),
    ).astype(BF16)
    tot_ref[:, 0:heads] = terms
    tot_ref[:, heads : 2 * heads] = jnp.zeros_like(terms)


def decays(dt_in, bias, a_log):
    heads, rows = dt_in.shape
    pair = jax.ShapeDtypeStruct((rows, 2 * heads), BF16)
    return pl.pallas_call(
        decay_kernel,
        out_shape=[
            jax.ShapeDtypeStruct((heads, rows), F32),
            jax.ShapeDtypeStruct((heads, rows), F32),
            pair,
            pair,
            pair,
            pair,
            jax.ShapeDtypeStruct((EXTRA, 2 * heads), BF16),
        ],
        compiler_params=params(),
        cost_estimate=pl.CostEstimate(flops=10**8, bytes_accessed=2 * 10**6, transcendentals=heads * rows * 5),
    )(dt_in, bias, a_log)


def conv_column(pad, series, tail, taps, offset, store):
    rows = series.shape[0]
    pad[0:8, :] = tail[...].astype(F32)[TAIL - 8 :]
    pad[8 : 8 + rows, :] = series[...].astype(F32)
    for start in range(0, rows, CHUNK):
        total = offset + taps[3] * pad[8 + start : 8 + start + CHUNK, :]
        for k in range(3):
            total = total + taps[k] * pad[5 + k + start : 5 + k + start + CHUNK, :]
        store(start, silu(total))


def state_kernel(core_ref, x_ref, xt_ref, wx_ref, ox_ref, wabs_ref, spread_ref, tot_ref, *rest):
    cx_ref, state_ref, pad, scaled, bturn = rest[-5:]
    if len(rest) == 6:
        made_ref = rest[0]

        @pl.when(pl.program_id(0) == 0)
        def _():
            bturn[...] = made_ref[...].T

    else:
        b_ref, bt_ref, c_ref, ct_ref, wb_ref, ob_ref, cb_ref, cc_ref = rest[:8]

        @pl.when(pl.program_id(0) == 0)
        def _():
            for n, (src, tail, dst) in enumerate(((b_ref, bt_ref, cb_ref), (c_ref, ct_ref, cc_ref))):
                for lane in range(0, STATE, 128):
                    cut = (slice(None), slice(lane, lane + 128))

                    def store(start, v, dst=dst, lane=lane):
                        dst[start : start + CHUNK, lane : lane + 128] = v.astype(BF16)

                    taps = [wb_ref[k, n : n + 1, lane : lane + 128] for k in range(4)]
                    offset = ob_ref[n : n + 1, lane : lane + 128]
                    conv_column(pad, src.at[cut], tail.at[cut], taps, offset, store)
            bturn[...] = cb_ref[...].T

    for lane in range(0, TILE, 128):
        own = slice(lane, lane + 128)
        cut = (slice(None), own)

        def store(start, v, own=own):
            v = v.astype(BF16)
            cx_ref[start : start + CHUNK, own] = v
            w = dot(wabs_ref[start : start + CHUNK, :], spread_ref[0, :, own])
            scaled[start : start + CHUNK, own] = (w * v.astype(F32)).astype(BF16)

        taps = [wx_ref[k : k + 1, own] for k in range(4)]
        conv_column(pad, x_ref.at[cut], xt_ref.at[cut], taps, ox_ref[:, own], store)
    state_ref[0:STATE, :] = dot(bturn[...], scaled[...]).astype(BF16)
    state_ref[STATE:, :] = dot(tot_ref[...], spread_ref[0]).astype(BF16)


def group_of(turn, core):
    return core[0] if turn else 1 - core[0]


def local_states(turn, half, core, x, tails, wx, ox, wabs, spread, tot, bc, wbc, obc, made=None):
    rows, channels = x.shape
    groups = channels // LANES
    width = LANES // HALVES
    tiles = width // TILE
    first = channels // STATE
    lane = lambda j, core: (0, (group_of(turn, core) * HALVES + half) * tiles + j)
    own = lambda shift: lambda j, core: (0, shift + group_of(turn, core))
    still = lambda j, core: (0, 0)
    out = lambda j, core: (0, j)
    if made is None:
        ends = [
            pl.BlockSpec((rows, STATE), own(0)),
            pl.BlockSpec((TAIL, STATE), own(first)),
            pl.BlockSpec((rows, STATE), own(groups)),
            pl.BlockSpec((TAIL, STATE), own(first + groups)),
            pl.BlockSpec((4, 2, STATE), lambda j, core: (0, 0, group_of(turn, core))),
            pl.BlockSpec((2, STATE), own(0)),
        ]
        last = (bc, tails, bc, tails, wbc, obc)
    else:
        ends = [pl.BlockSpec((rows, STATE), still)]
        last = (made,)
    fresh = 2 if made is None else 0
    return pl.pallas_call(
        state_kernel,
        grid_spec=pltpu.PrefetchScalarGridSpec(
            num_scalar_prefetch=1,
            grid=(tiles,),
            in_specs=[
                pl.BlockSpec((rows, TILE), lane),
                pl.BlockSpec((TAIL, TILE), lane),
                pl.BlockSpec((4, TILE), lane),
                pl.BlockSpec((1, TILE), lane),
                pl.BlockSpec(wabs.shape, still),
                pl.BlockSpec((1, spread.shape[1], TILE), lambda j, core: (group_of(turn, core), 0, half * tiles + j)),
                pl.BlockSpec(tot.shape, still),
                *ends,
            ],
            out_specs=[pl.BlockSpec((rows, STATE), still)] * fresh
            + [pl.BlockSpec((rows, TILE), out), pl.BlockSpec((STATE + EXTRA, TILE), out)],
            scratch_shapes=[
                pltpu.VMEM((rows + 8, 128), F32),
                pltpu.VMEM((rows, TILE), BF16),
                pltpu.VMEM((STATE, rows), BF16),
            ],
        ),
        out_shape=[jax.ShapeDtypeStruct((rows, STATE), BF16)] * fresh
        + [
            jax.ShapeDtypeStruct((rows, width), BF16),
            jax.ShapeDtypeStruct((STATE + EXTRA, width), BF16),
        ],
        compiler_params=params("arbitrary"),
        cost_estimate=pl.CostEstimate(
            flops=2 * rows * STATE * width, bytes_accessed=4 * rows * width, transcendentals=rows * width
        ),
    )(core, x, tails, wx, ox, wabs, spread, tot, *last)


def values_kernel(
    core_ref, x_ref, b_ref, c_ref, run_ref, row_ref, ehl_ref, whl_ref, spread_ref, sent_ref, out_ref, done_ref, near, inside, across
):
    done_ref[0] = 0
    rows = x_ref.shape[0]
    blocks = rows // BLOCK
    part = lambda n: slice(n * CHUNK, (n + 1) * CHUNK)
    whole = lambda n: slice(n * BLOCK, (n + 1) * BLOCK)
    pairs = [(late, early) for late in range(blocks) for early in range(late)]

    @pl.when(pl.program_id(0) == 0)
    def _():
        t = lax.broadcasted_iota(jnp.int32, (CHUNK, CHUNK), 0)
        s = lax.broadcasted_iota(jnp.int32, (CHUNK, CHUNK), 1)
        for n in range(2 * blocks):
            near[n] = jnp.where(t >= s, dot(c_ref[part(n), :], b_ref[part(n), :], 1, 1), 0.0)
        for n in range(blocks):
            inside[n] = dot(c_ref[part(2 * n + 1), :], b_ref[part(2 * n), :], 1, 1).astype(BF16)
        for n, (late, early) in enumerate(pairs):
            across[n] = dot(c_ref[whole(late), :], b_ref[whole(early), :], 1, 1).astype(BF16)

    left = lax.broadcasted_iota(jnp.int32, (CHUNK, 128), 1) < HEAD_DIM
    turned = [run_ref[:, part(n)].T for n in range(2 * blocks)]
    for lane in range(0, VTILE, 256):
        cut = slice(lane, lane + 256)
        spread = spread_ref[0, :, cut]
        sent, faded = [], []
        for n in range(blocks):
            grown = dot(ehl_ref[whole(n), :], spread)
            weight = dot(whl_ref[whole(n), :], spread)
            x = x_ref[whole(n), cut].astype(F32)
            early_fade = grown[CHUNK - 1 : CHUNK, :]
            late_fade = grown[BLOCK - 1 : BLOCK, :]
            scaled = weight * x
            ended = jnp.concatenate([scaled[:CHUNK] * late_fade, scaled[CHUNK:]], axis=0).astype(BF16)
            sent.append(ended)
            faded.append(early_fade * late_fade)
            carried = None
            for early in range(n):
                came = dot(across[pairs.index((n, early))], sent[early])
                carried = came if carried is None else carried * faded[early] + came
            second = dot(inside[n], scaled[:CHUNK].astype(BF16))
            if carried is not None:
                second = second + carried[CHUNK:] * early_fade
            from_before = (None if carried is None else carried[:CHUNK], second)
            for side in range(2):
                m = 2 * n + side
                base = near[m]
                for pair in range(2):
                    first = lane // HEAD_DIM + 2 * pair
                    low = lane + 128 * pair
                    mixes = []
                    for h in (first, first + 1):
                        along = turned[m][:, h : h + 1] - row_ref[h : h + 1, part(m)]
                        mixes.append((base * jnp.exp2(jnp.minimum(along, 64.0))).astype(BF16))
                    xs = x_ref[part(m), low : low + 128]
                    none = jnp.zeros_like(xs)
                    sides = jnp.concatenate([jnp.where(left, xs, none), jnp.where(left, none, xs)], axis=0)
                    total = dot(jnp.concatenate(mixes, axis=1), sides)
                    if from_before[side] is not None:
                        own = slice(128 * pair, 128 * pair + 128)
                        total = total + grown[side * CHUNK : (side + 1) * CHUNK, own] * from_before[side][:, own]
                    out_ref[part(m), low : low + 128] = total.astype(out_ref.dtype)


def local_values(turn, half, core, x, b, c, run, row, ehl, whl, spread, sent):
    rows, width = x.shape
    blocks = rows // BLOCK
    tiles = width // VTILE
    heads = VTILE // HEAD_DIM
    head = lambda j, core: ((group_of(turn, core) * HALVES + half) * tiles + j, 0)
    still = lambda j, core: (0, 0)
    lane = lambda j, core: (0, j)
    return pl.pallas_call(
        values_kernel,
        grid_spec=pltpu.PrefetchScalarGridSpec(
            num_scalar_prefetch=1,
            grid=(tiles,),
            in_specs=[
                pl.BlockSpec((rows, VTILE), lane),
                pl.BlockSpec((rows, STATE), still),
                pl.BlockSpec((rows, STATE), still),
                pl.BlockSpec((heads, rows), head),
                pl.BlockSpec((heads, rows), head),
                pl.BlockSpec(ehl.shape, still),
                pl.BlockSpec(whl.shape, still),
                pl.BlockSpec((1, spread.shape[1], VTILE), lambda j, core: (group_of(turn, core), 0, half * tiles + j)),
                pl.BlockSpec(memory_space=pl.ANY),
            ],
            out_specs=[pl.BlockSpec((rows, VTILE), lane), pl.BlockSpec(memory_space=pltpu.SMEM)],
            scratch_shapes=[
                pltpu.VMEM((2 * blocks, CHUNK, CHUNK), F32),
                pltpu.VMEM((blocks, CHUNK, CHUNK), BF16),
                pltpu.VMEM((blocks * (blocks - 1) // 2, BLOCK, BLOCK), BF16),
            ],
        ),
        out_shape=[jax.ShapeDtypeStruct((rows, width), BF16), jax.ShapeDtypeStruct((1,), jnp.int32)],
        compiler_params=params("arbitrary"),
        cost_estimate=pl.CostEstimate(
            flops=8 * rows * STATE * width, bytes_accessed=8 * rows * width, transcendentals=rows * CHUNK * width // HEAD_DIM
        ),
    )(core, x, b, c, run, row, ehl, whl, spread, sent)


def norm_kernel(core_ref, c_ref, eabs_ref, spread_ref, z_ref, gain_ref, reward_ref, *rest):
    values, states = rest[:HALVES], rest[HALVES : 2 * HALVES]
    out_ref, term_ref, gated = rest[-3:]
    rows = c_ref.shape[0]
    c = c_ref[...]
    decay = eabs_ref[...]
    squares = jnp.zeros((rows, 128), F32)
    for lane in range(0, LANES, 256):
        cut = slice(lane, lane + 256)
        half, low = divmod(lane, LANES // HALVES)
        own = slice(low, low + 256)
        v = values[half][:, own].astype(F32) + dot(decay, spread_ref[0, :, cut]) * dot(c, states[half][:, own])
        v = v * silu(z_ref[:, cut].astype(F32))
        gated[:, cut] = v
        squares = squares + v[:, :128] * v[:, :128] + v[:, 128:] * v[:, 128:]
    scale = lax.rsqrt(jnp.sum(squares, axis=1, keepdims=True) * (1.0 / LANES) + 1e-05)
    terms = jnp.zeros((rows, 128), F32)
    for lane in range(0, LANES, 128):
        cut = slice(lane, lane + 128)
        v = (gated[:, cut] * scale * gain_ref[:, cut]).astype(BF16)
        out_ref[:, cut] = v
        terms = terms + v.astype(F32) * reward_ref[:, cut]
    term_ref[...] = terms


def gated_norm(turn, core, values, c, states, eabs, spread, z, gain, reward, target):
    rows = c.shape[0]
    width = LANES // HALVES
    own = lambda i, core: (i, group_of(turn, core))
    side = lambda i, core: (0, group_of(turn, core))
    down = lambda i, core: (i, 0)
    still = lambda i, core: (0, 0)
    return pl.pallas_call(
        norm_kernel,
        grid_spec=pltpu.PrefetchScalarGridSpec(
            num_scalar_prefetch=1,
            grid=(rows // ROWS,),
            in_specs=[
                pl.BlockSpec((ROWS, STATE), down),
                pl.BlockSpec((ROWS, eabs.shape[1]), down),
                pl.BlockSpec((1, spread.shape[1], LANES), lambda i, core: (group_of(turn, core), 0, 0)),
                pl.BlockSpec((ROWS, LANES), own),
                pl.BlockSpec((1, LANES), side),
                pl.BlockSpec((1, LANES), side),
            ]
            + [pl.BlockSpec((ROWS, width), down)] * HALVES
            + [pl.BlockSpec((STATE, width), still)] * HALVES
            + ([] if target is None else [pl.BlockSpec(memory_space=pl.ANY)]),
            out_specs=[pl.BlockSpec((ROWS, LANES), own), pl.BlockSpec((ROWS, 128), down)],
            scratch_shapes=[pltpu.VMEM((ROWS, LANES), F32)],
        ),
        out_shape=[jax.ShapeDtypeStruct(z.shape, BF16), jax.ShapeDtypeStruct((rows, 128), F32)],
        input_output_aliases={} if target is None else {7 + 2 * HALVES: 0},
        compiler_params=params("arbitrary"),
        cost_estimate=pl.CostEstimate(
            flops=2 * rows * STATE * LANES, bytes_accessed=8 * rows * LANES, transcendentals=rows * LANES
        ),
    )(core, c, eabs, spread, z, gain, reward, *values, *states, *(() if target is None else (target,)))


def total_of(payload):
    extra = payload[STATE : STATE + 3].astype(F32)
    return extra[0:1] + extra[1:2] + extra[2:3]


def with_total(state, total):
    rows = jnp.concatenate(split3(total), axis=0)
    rows = jnp.pad(rows, ((0, EXTRA - 3), (0, 0)))
    return jnp.concatenate([state.astype(BF16), rows], axis=0)


def advance(state, payload):
    return jnp.exp2(total_of(payload)) * state + payload[:STATE].astype(F32)


def over(value, move):
    count = lax.axis_size("seq")
    return lax.ppermute(value, "seq", [(i, move(i)) for i in range(count) if move(i) is not None])


def along_y(k):
    return lambda i: i // 8 * 8 + (i // 2 + k) % 4 * 2 + i % 2


def entering_state(away, mine):
    place = lax.axis_index("seq")
    core = place % 2
    y = place // 2 % 4
    other = over(away, lambda i: i ^ 1)
    first = jnp.where(core == 0, mine, other)
    second = jnp.where(core == 0, other, mine)
    chip = with_total(
        advance(first[:STATE].astype(F32), second), total_of(first) + total_of(second)
    )
    quarter = chip.shape[1] // 4
    piece = lambda n: lax.dynamic_slice_in_dim(chip, n * quarter, quarter, 1)
    going = [piece((y + k) % 4) for k in range(4)]
    came = jnp.stack([going[0]] + [over(going[k], along_y(k)) for k in (1, 2, 3)])
    y = y + (yield going[3])
    parts = [lax.dynamic_index_in_dim(came, (y - n) % 4, 0, False) for n in range(4)]
    state, total = parts[0][:STATE].astype(F32), total_of(parts[0])
    for n in range(1, 4):
        state, total = advance(state, parts[n]), total + total_of(parts[n])
    row = with_total(state, total)
    near, mid, far = (
        over(row, lambda i, k=k: i + 8 * k if i + 8 * k < 32 else None) for k in (1, 2, 3)
    )
    state = advance(advance(far[:STATE].astype(F32), mid), near)
    entering = []
    for n in range(4):
        entering.append(state.astype(BF16))
        state = advance(state, parts[n])
    entering = jnp.stack(entering)
    going = [lax.dynamic_index_in_dim(entering, (y + k) % 4, 0, False) for k in range(4)]
    back = jnp.stack([going[0]] + [over(going[k], along_y(k)) for k in (1, 2, 3)])
    y = y + (yield going[3])
    chip_in = jnp.concatenate(
        [lax.dynamic_index_in_dim(back, (y - n) % 4, 0, False) for n in range(4)], axis=1
    )
    later = advance(chip_in.astype(F32), first).astype(BF16)
    got = over(jnp.where(core == 0, later, chip_in), lambda i: i ^ 1)
    yield got, jnp.where(core == 0, chip_in, later)


def per_device(
    x_in, z_in, bc_in, dt_in, conv_x_weight, conv_x_bias, conv_bc_weight, conv_bc_bias,
    dt_bias, a_log, norm_gain, reward_w, step_ends,
):
    rows = x_in.shape[0]
    place = lax.axis_index("seq")
    core = (place % 2).reshape(1)
    bc = bc_in.reshape(rows, -1)
    tails = jnp.concatenate([x_in[rows - TAIL :], bc_in[rows - TAIL :].reshape(TAIL, -1)], axis=1)
    tails = over(tails, lambda i: i + 1 if i + 1 < 32 else None)
    run, row, ehl, whl, eabs, wabs, tot = decays(dt_in.T, dt_bias[None], a_log[None])
    heads = dt_in.shape[1]
    groups = heads // PER_GROUP
    head = np.arange(heads * HEAD_DIM).reshape(groups, 1, LANES) // HEAD_DIM
    spread = jnp.asarray(np.arange(2 * heads)[:, None] % heads == head, BF16)
    wx, ox = conv_x_weight, conv_x_bias[None]
    made = [[], []]
    for half in range(HALVES):
        for turn in range(2):
            made[turn].append(
                local_states(
                    turn, half, core, x_in, tails, wx, ox, wabs, spread, tot, bc, conv_bc_weight, conv_bc_bias,
                    made[turn][0][0] if half else None,
                )
            )
    values = [[], []]

    def inner(turn, sent):
        m = made[turn]
        done = None
        for half in range(HALVES):
            v, done = local_values(
                turn, half, core, m[half][-2], m[0][0], m[0][1], run, row, ehl, whl, spread, sent
            )
            values[turn].append(v)
        return done[0]

    steps = entering_state(made[0][0][-1], made[1][0][-1])
    sent = next(steps)
    sent = steps.send(inner(1, sent))
    entered = [steps.send(inner(0, sent))]
    normed, sums = None, []
    for turn in (1, 0):
        normed, part = gated_norm(
            turn, core, values[turn], made[turn][0][1], [e[turn] for e in entered], eabs, spread, z_in,
            norm_gain[None], reward_w[None], normed,
        )
        sums.append(part)
    local_pos = step_ends - place * rows
    inside = (local_pos >= 0) & (local_pos < rows)
    at = jnp.clip(local_pos, 0, rows - 1)
    terms = jnp.sum(jnp.take(sums[0], at, axis=0) + jnp.take(sums[1], at, axis=0), axis=1)
    terms = jnp.where(inside, terms, 0.0)
    devices = lax.axis_size("seq") * lax.axis_size("head")
    terms = lax.all_to_all(jnp.broadcast_to(terms, (devices, terms.shape[0])), ("seq", "head"), 0, 0)
    return normed, jnp.sum(terms, axis=0)


def solution(mesh):
    return jax.shard_map(
        per_device,
        mesh=mesh,
        in_specs=(
            P("seq", "head"),
            P("seq", "head"),
            P("seq", None, "head"),
            P("seq", "head"),
            P(None, "head"),
            P("head"),
            P(None, None, "head"),
            P(None, "head"),
            P("head"),
            P("head"),
            P("head"),
            P("head"),
            P(),
        ),
        out_specs=(P("seq", "head"), P()),
        check_vma=False,
    )
```

time: 166 us -> 130 us (0.78)
  starting transfers between devices: 42.6 us -> 23.9 us
  Pallas kernels: 72.4 us -> 58.2 us
  waiting for transfers between devices: 2.13 us -> 9.99 us
  local copies, waits for them, and re-layouts: 14.9 us -> 9.76 us
  other arithmetic: 10.7 us -> 5.65 us
  blocking collectives: 21 us -> 19 us
    ppermute x24 -> x12, starting transfers between devices: 42.6 us -> 23.9 us  [over(): lax.ppermute(value, 'seq', [(i, move(i)) for i in range(count) if move(i)...]
    pallas_call x6, Pallas kernels: 69.6 us -> 55.3 us  [the longest x2 20.9 us: local_values(): pl.pallas_call(values_kernel, grid_spec=pltpu.PrefetchScalarGridSpec(num_...]
    ppermute x24 -> x12, waiting for transfers between devices: 2.13 us -> 9.99 us  [over(): lax.ppermute(value, 'seq', [(i, move(i)) for i in range(count) if move(i)...]
    mul x2 -> x0, other arithmetic: 2.55 us -> none  [per_device(): ld = dt * (-LOG2E * jnp.exp(a_log))[:, None]]
    dynamic_slice x4 -> x1, local copies, waits for them, and re-layouts: 2.29 us -> 0.08 us  [entering_state(): lax.dynamic_index_in_dim(entering, (y + k) % 4, 0, False)]
    concatenate x2 -> x1, other arithmetic: 2.12 us -> 0.01 us  [per_device(): jnp.concatenate([x_in[rows - TAIL:], bc_in[rows - TAIL:].reshape(TAIL, -1...]
    all_to_all x1, blocking collectives: 21 us -> 19 us  [per_device(): lax.all_to_all(jnp.broadcast_to(terms, (devices, terms.shape[0])), ('seq'...]
    gather x1 -> x2, local copies, waits for them, and re-layouts: 4.99 us -> 3.18 us  [the longest x1 1.59 us: per_device(): jnp.take(sums[1], at, axis=0)]
  transfers between devices with their start and end apart: 24 -> 12, of which waited for: 2 -> 3; matrix products, arithmetic and copies ran while one was open for 9% -> 4% of each run, Pallas kernels for 28% -> 32%
where the time goes in v2:
time: 130 us; the launch traced here: 129 us
  Pallas kernels  58.2 us (45%)
  starting transfers between devices  23.9 us (18%)
  blocking collectives  19 us (15%)
  waiting for transfers between devices  9.99 us (8%)
  local copies, waits for them, and re-layouts  9.76 us (8%)
  other arithmetic  5.65 us (4%)
  between operations  2.61 us (2%)
    ppermute x12, starting transfers between devices, over(): lax.ppermute(value, 'seq', [(i, move(i)) for i in range(count) if move(i)...  23.9 us
    pallas_call x2, Pallas kernels, local_values(): pl.pallas_call(values_kernel, grid_spec=pltpu.PrefetchScalarGridSpec(num_...  20.9 us
    pallas_call x2, Pallas kernels, local_states(): pl.pallas_call(state_kernel, grid_spec=pltpu.PrefetchScalarGridSpec(num_s...  19.1 us
    all_to_all x1, blocking collectives, per_device(): lax.all_to_all(jnp.broadcast_to(terms, (devices, terms.shape[0])), ('seq'...  19 us
    pallas_call x2, Pallas kernels, gated_norm(): pl.pallas_call(norm_kernel, grid_spec=pltpu.PrefetchScalarGridSpec(num_sc...  15.4 us
    ppermute x12, waiting for transfers between devices, over(): lax.ppermute(value, 'seq', [(i, move(i)) for i in range(count) if move(i)...  9.99 us
    unnamed x12, local copies, waits for them, and re-layouts  4.68 us
    pallas_call x1, Pallas kernels, decays(): pl.pallas_call(decay_kernel, out_shape=[jax.ShapeDtypeStruct((heads, rows...  2.91 us
  transfers between devices with their start and end apart: 12, of which 3 were waited for; matrix products, arithmetic and copies ran while one was open for 4% of the time, Pallas kernels for 32%

profile of v2, /device:TPU:1, one launch (start us, length us, event | category | flops | bytes accessed | tf_op | source)
XLA Modules:
  0.0 129.1 jit_solution(5450773668312411786)
XLA Ops:
  0.6 0.9 slice.185
  1.5 0.8 slice.186
  2.4 4.6 %collective-permute-start = (bf16[16,5120]{1,0:T(8,128)(2,1)S(1)}, bf16[16,5120]{1,0:T(8,128)(2,1)S(1)}, u32[]{:S(2)}, u32[]{:S(2)}) collective-permute-start(bf16[16,5120]{1,0:T(8,128)(2,1)S(1)} %pad_maximum_fusion.5), channel_id=1, source_target_pairs={{0,4},{4,8},{8,12},{12,16},{16,20},{20,24},{24,28},{28,32},{32,36}... | collective-permute-start | bytes 491528 | tf_op jit(solution)/shard_map/ppermute | solution.py:429
  7.0 3.0 %copy.20 = bf16[96,8,2,512]{3,1,2,0:T(8,128)(2,1)} copy(bf16[96,8,2,512]{3,2,1,0:T(2,128)(2,1)} %bitcast.104) | data formatting | bytes 3145728
  10.0 2.9 %shard_map.149 = (f32[64,768]{1,0:T(8,128)}, f32[64,768]{1,0:T(8,128)}, bf16[768,128]{1,0:T(8,128)(2,1)}, bf16[768,128]{1,0:T(8,128)(2,1)}, bf16[768,128]{1,0:T(...) custom-call(f32[64,768]{1,0:T(8,128)} %bitcast.131, f32[1,64]{1,0:T(1,128)} %bitcast.132, f32[1,64]{1,0:T(1,128)} %bitcast.133), custom_call_target="tpu_custom_call" | custom-call | flops 100000000 | bytes 2000000 | tf_op jit(solution)/shard_map/pallas_call | solution.py:116
  12.9 0.7 copy-done
  13.6 9.5 %shard_map.150 = (bf16[768,256]{1,0:T(8,128)(2,1)}, bf16[768,256]{1,0:T(8,128)(2,1)}, bf16[768,2048]{1,0:T(8,128)(2,1)}, bf16[272,2048]{1,0:T(8,128)(2,1)}) custom-call(s32[1]{0:T(128)} %bitcast.core_ref, bf16[768,4096]{1,0:T(8,128)(2,1)} %x_ref.3, bf16[16,5120]{1,0:T(8,128)(2,1)} %copy-done, f32[4,4096]{1,0:T(4,128)} %wx_ref.3, f32[1,4096]{1,0:T(1,128)} %bitcast.113, ...), custom_call_target="tpu_custom_call" | custom-call | flops 805306368 | bytes 6291456 | tf_op jit(solution)/shard_map/pallas_call | solution.py:213
  23.3 9.6 %shard_map.151 = (bf16[768,256]{1,0:T(8,128)(2,1)}, bf16[768,256]{1,0:T(8,128)(2,1)}, bf16[768,2048]{1,0:T(8,128)(2,1)}, bf16[272,2048]{1,0:T(8,128)(2,1)}) custom-call(s32[1]{0:T(128)} %bitcast.core_ref, bf16[768,4096]{1,0:T(8,128)(2,1)} %x_ref.3, bf16[16,5120]{1,0:T(8,128)(2,1)} %copy-done, f32[4,4096]{1,0:T(4,128)} %wx_ref.3, f32[1,4096]{1,0:T(1,128)} %bitcast.114, ...), custom_call_target="tpu_custom_call" | custom-call | flops 805306368 | bytes 6291456 | tf_op jit(solution)/shard_map/pallas_call | solution.py:213
  32.9 1.4 %broadcast_select_fusion = (bf16[272,2048]{1,0:T(8,128)(2,1)S(1)}, bf16[272,2048]{1,0:T(8,128)(2,1)S(1)}) fusion(bf16[272,2048]{1,0:T(8,128)(2,1)} %get-tuple-element.37, bf16[272,2048]{1,0:T(8,128)(2,1)S(1)} %collective-permute-done.1, pred[]{:T(512)S(6)} %eq.26), kind=kLoop, calls=%fused_computation.14 | loop fusion | flops 1114112 | bytes 4456449 | tf_op jit(solution)/shard_map/jit(_where)/select_n | solution.py:441
  34.4 0.4 fusion.1
  35.0 2.7 %collective-permute-start.3 = (bf16[272,512]{1,0:T(8,128)(2,1)S(1)}, bf16[272,512]{1,0:T(8,128)(2,1)S(1)}, u32[]{:S(2)}, u32[]{:S(2)}) collective-permute-start(bf16[272,512]{1,0:T(8,128)(2,1)S(1)} %get-tuple-element.75), channel_id=1, source_target_pairs={{0,16},{4,20},{8,24},{12,28},{16,0},{20,4},{24,8},{28,12},{32,48},... | collective-permute-start | bytes 835592 | tf_op jit(solution)/shard_map/ppermute | solution.py:429
  37.7 1.1 collective-permute-start.4
  39.2 10.4 %shard_map.152 = (bf16[768,2048]{1,0:T(8,128)(2,1)}, s32[1]{0:T(128)}) custom-call(s32[1]{0:T(128)} %bitcast.core_ref, bf16[768,2048]{1,0:T(8,128)(2,1)} %get-tuple-element.38.x_ref, bf16[768,256]{1,0:T(8,128)(2,1)} %get-tuple-element.39.b_ref, bf16[768,256]{1,0:T(8,128)(2,1)} %get-tuple-element.40.c_ref, f32[64,768]{1,0:T(8,128)} %get-tuple-element.32.run_ref, ...), custom_call_target="tpu_custom_call" | custom-call | flops 3221225472 | bytes 12582912 | tf_op jit(solution)/shard_map/pallas_call | solution.py:321
  50.4 0.7 collective-permute-done.2
  51.6 3.1 %collective-permute-start.5 = (bf16[272,512]{1,0:T(8,128)(2,1)S(1)}, bf16[272,512]{1,0:T(8,128)(2,1)S(1)}, u32[]{:S(2)}, u32[]{:S(2)}) collective-permute-start(bf16[272,512]{1,0:T(8,128)(2,1)S(1)} %pad_maximum_fusion.4), channel_id=1, source_target_pairs={{0,32},{4,36},{8,40},{12,44},{16,48},{20,52},{24,56},{28,60},{32,6... | collective-permute-start | bytes 835592 | tf_op jit(solution)/shard_map/ppermute | solution.py:429
  54.9 4.4 %collective-permute-start.6 = (bf16[272,512]{1,0:T(8,128)(2,1)S(1)}, bf16[272,512]{1,0:T(8,128)(2,1)S(1)}, u32[]{:S(2)}, u32[]{:S(2)}) collective-permute-start(bf16[272,512]{1,0:T(8,128)(2,1)S(1)} %pad_maximum_fusion.4), channel_id=1, source_target_pairs={{0,64},{4,68},{8,72},{12,76},{16,80},{20,84},{24,88},{28,92},{32,9... | collective-permute-start | bytes 835592 | tf_op jit(solution)/shard_map/ppermute | solution.py:429
  59.2 1.5 %collective-permute-start.7 = (bf16[272,512]{1,0:T(8,128)(2,1)S(1)}, bf16[272,512]{1,0:T(8,128)(2,1)S(1)}, u32[]{:S(2)}, u32[]{:S(2)}) collective-permute-start(bf16[272,512]{1,0:T(8,128)(2,1)S(1)} %pad_maximum_fusion.4), channel_id=1, source_target_pairs={{0,96},{4,100},{8,104},{12,108},{16,112},{20,116},{24,120},{28,124... | collective-permute-start | bytes 835592 | tf_op jit(solution)/shard_map/ppermute | solution.py:429
  60.8 5.5 %collective-permute-done.6 = bf16[272,512]{1,0:T(8,128)(2,1)S(1)} collective-permute-done((bf16[272,512]{1,0:T(8,128)(2,1)S(1)}, bf16[272,512]{1,0:T(8,128)(2,1)S(1)}, u32[]{:S(2)}, u32[]{:S(2)}) %collective-permute-start.6) | collective-permute-done | bytes 278560 | tf_op jit(solution)/shard_map/ppermute | solution.py:429
  66.3 3.7 %collective-permute-done.7 = bf16[272,512]{1,0:T(8,128)(2,1)S(1)} collective-permute-done((bf16[272,512]{1,0:T(8,128)(2,1)S(1)}, bf16[272,512]{1,0:T(8,128)(2,1)S(1)}, u32[]{:S(2)}, u32[]{:S(2)}) %collective-permute-start.7) | collective-permute-done | bytes 278560 | tf_op jit(solution)/shard_map/ppermute | solution.py:429
  70.7 0.5 collective-permute-start.8
  71.2 2.3 %collective-permute-start.9 = (bf16[256,512]{1,0:T(8,128)(2,1)S(1)}, bf16[256,512]{1,0:T(8,128)(2,1)S(1)}, u32[]{:S(2)}, u32[]{:S(2)}) collective-permute-start(bf16[256,512]{1,0:T(8,128)(2,1)S(1)} %get-tuple-element.82), channel_id=1, source_target_pairs={{0,16},{4,20},{8,24},{12,28},{16,0},{20,4},{24,8},{28,12},{32,48},... | collective-permute-start | bytes 786440 | tf_op jit(solution)/shard_map/ppermute | solution.py:429
  73.5 1.9 %collective-permute-start.10 = (bf16[256,512]{1,0:T(8,128)(2,1)S(1)}, bf16[256,512]{1,0:T(8,128)(2,1)S(1)}, u32[]{:S(2)}, u32[]{:S(2)}) collective-permute-start(bf16[256,512]{1,0:T(8,128)(2,1)S(1)} %get-tuple-element.84.sent_ref), channel_id=1, source_target_pairs={{0,24},{4,28},{8,0},{12,4},{16,8},{20,12},{24,16},{28,20},{32,56},... | collective-permute-start | bytes 786440 | tf_op jit(solution)/shard_map/ppermute | solution.py:429
  75.5 10.4 %shard_map.153 = (bf16[768,2048]{1,0:T(8,128)(2,1)}, s32[1]{0:T(128)}) custom-call(s32[1]{0:T(128)} %bitcast.core_ref, bf16[768,2048]{1,0:T(8,128)(2,1)} %get-tuple-element.30.x_ref, bf16[768,256]{1,0:T(8,128)(2,1)} %get-tuple-element.31.b_ref, bf16[768,256]{1,0:T(8,128)(2,1)} %get-tuple-element.28.c_ref, f32[64,768]{1,0:T(8,128)} %get-tuple-element.32.run_ref, ...), custom_call_target="tpu_custom_call" | custom-call | flops 3221225472 | bytes 12582912 | tf_op jit(solution)/shard_map/pallas_call | solution.py:321
  86.8 1.5 %fusion.3 = (bf16[256,2048]{1,0:T(8,128)(2,1)}, bf16[256,2048]{1,0:T(8,128)(2,1)S(1)}) fusion(f32[2048]{0:T(1024)S(1)} %bitcast.119, pred[]{:T(512)S(6)} %eq.26, bf16[272,2048]{1,0:T(8,128)(2,1)S(1)} %get-tuple-element.62, bf16[256,512]{1,0:T(8,128)(2,1)S(1)} %get-tuple-element.78, bf16[256,512]{1,0:T(8,128)(2,1)S(1)} %get-tuple-element.79, ...), kind=kLoop, calls=%fused_computation.11 | loop fusion | flops 7864320 | bytes 4202497 | tf_op jit(solution)/shard_map/jit(_where)/select_n | solution.py:473
  88.3 1.3 %collective-permute-start.11 = (bf16[256,2048]{1,0:T(8,128)(2,1)S(1)}, bf16[256,2048]{1,0:T(8,128)(2,1)S(1)}, u32[]{:S(2)}, u32[]{:S(2)}) collective-permute-start(bf16[256,2048]{1,0:T(8,128)(2,1)S(1)} %get-tuple-element.65), channel_id=1, source_target_pairs={{0,4},{4,0},{8,12},{12,8},{16,20},{20,16},{24,28},{28,24},{32,36},... | collective-permute-start | bytes 3145736 | tf_op jit(solution)/shard_map/ppermute | solution.py:429
  89.7 7.7 %shard_map.154 = (bf16[768,4096]{1,0:T(8,128)(2,1)}, f32[768,128]{1,0:T(8,128)}) custom-call(s32[1]{0:T(128)} %bitcast.core_ref, bf16[768,256]{1,0:T(8,128)(2,1)} %get-tuple-element.40.c_ref, bf16[768,128]{1,0:T(8,128)(2,1)} %get-tuple-element.29.eabs_ref, bf16[2,128,2048]{2,1,0:T(8,128)(2,1)} %constant.172.clone.spread_ref, bf16[768,4096]{1,0:T(8,128)(2,1)} %z_ref.3, ...), custom_call_target="tpu_custom_call" | custom-call | flops 805306368 | bytes 12582912 | tf_op jit(solution)/shard_map/pallas_call | solution.py:384
  97.4 1.6 %gather_fusion = f32[64,128]{1,0:T(8,128)S(1)} fusion(f32[768,128]{1,0:T(8,128)} %get-tuple-element.47, s32[1024]{0:T(1024)S(1)} %pad_clamp_fusion), kind=kCustom, calls=%fused_computation.clone | custom fusion | bytes 65792 | tf_op jit(solution)/shard_map/jit(_take)/gather | solution.py:527
  99.0 1.0 copy-done.1
  100.0 7.7 %shard_map.155 = (bf16[768,4096]{1,0:T(8,128)(2,1)}, f32[768,128]{1,0:T(8,128)}) custom-call(s32[1]{0:T(128)} %bitcast.core_ref, bf16[768,256]{1,0:T(8,128)(2,1)} %get-tuple-element.28.c_ref, bf16[768,128]{1,0:T(8,128)(2,1)} %get-tuple-element.29.eabs_ref, bf16[2,128,2048]{2,1,0:T(8,128)(2,1)} %constant.172.clone.spread_ref, ...), custom_call_target="tpu_custom_call", output_to_operand_aliasing={{0}: (9, {})} | custom-call | flops 805306368 | bytes 12582912 | tf_op jit(solution)/shard_map/pallas_call | solution.py:384
  107.6 1.6 %gather_fusion.1 = f32[64,128]{1,0:T(8,128)S(1)} fusion(f32[768,128]{1,0:T(8,128)} %get-tuple-element.48, s32[1024]{0:T(1024)S(1)} %pad_clamp_fusion), kind=kCustom, calls=%fused_computation.1.clone | custom fusion | bytes 65792 | tf_op jit(solution)/shard_map/jit(_take)/gather | solution.py:527
  109.5 19.0 %all_to_all.6 = f32[128,1,64]{2,1,0:T(1,128)S(1)} all-to-all(f32[128,1,64]{2,1,0:T(1,128)S(1)} %broadcast_in_dim.39), channel_id=1, replica_groups=mesh['seq'=32,'head'=4] {'seq','head'}, dimensions={0} | all-to-all | bytes 65536 | tf_op jit(solution)/shard_map/all_to_all | solution.py:530
  128.5 0.7 reduce_sum.19
  (53 shorter events, 2.4 us)
Async XLA Ops:
  2.4 10.5 %collective-permute-start = (bf16[16,5120]{1,0:T(8,128)(2,1)S(1)}, bf16[16,5120]{1,0:T(8,128)(2,1)S(1)}, u32[]{:S(2)}, u32[]{:S(2)}) collective-permute-start(bf16[16,5120]{1,0:T(8,128)(2,1)S(1)} %pad_maximum_fusion.5), channel_id=1, source_target_pairs={{0,4},{4,8},{8,12},{12,16},{16,20},{20,24},{24,28},{28,32},{32,36}... | collective-permute-start | bytes 491528 | tf_op jit(solution)/shard_map/ppermute | solution.py:429
  12.9 0.7 copy-start
  23.1 9.8 %collective-permute-start.1 = (bf16[272,2048]{1,0:T(8,128)(2,1)}, bf16[272,2048]{1,0:T(8,128)(2,1)S(1)}, u32[]{:S(2)}, u32[]{:S(2)}) collective-permute-start(bf16[272,2048]{1,0:T(8,128)(2,1)} %get-tuple-element.36), channel_id=1, source_target_pairs={{0,4},{4,0},{8,12},{12,8},{16,20},{20,16},{24,28},{28,24},{32,36},... | collective-permute-start | bytes 3342344 | tf_op jit(solution)/shard_map/ppermute | solution.py:429
  35.0 4.2 %copy-start.2 = (bf16[272,512]{1,0:T(8,128)(2,1)}, bf16[272,512]{1,0:T(8,128)(2,1)S(1)}, u32[]{:S(2)}) copy-start(bf16[272,512]{1,0:T(8,128)(2,1)S(1)} %get-tuple-element.76.sent_ref) | copy-start | bytes 835588
  35.0 15.4 %collective-permute-start.3 = (bf16[272,512]{1,0:T(8,128)(2,1)S(1)}, bf16[272,512]{1,0:T(8,128)(2,1)S(1)}, u32[]{:S(2)}, u32[]{:S(2)}) collective-permute-start(bf16[272,512]{1,0:T(8,128)(2,1)S(1)} %get-tuple-element.75), channel_id=1, source_target_pairs={{0,16},{4,20},{8,24},{12,28},{16,0},{20,4},{24,8},{28,12},{32,48},... | collective-permute-start | bytes 835592 | tf_op jit(solution)/shard_map/ppermute | solution.py:429
  37.7 12.7 %collective-permute-start.4 = (bf16[272,512]{1,0:T(8,128)(2,1)S(1)}, bf16[272,512]{1,0:T(8,128)(2,1)S(1)}, u32[]{:S(2)}, u32[]{:S(2)}) collective-permute-start(bf16[272,512]{1,0:T(8,128)(2,1)S(1)} %get-tuple-element.76.sent_ref), channel_id=1, source_target_pairs={{0,24},{4,28},{8,0},{12,4},{16,8},{20,12},{24,16},{28,20},{32,56},... | collective-permute-start | bytes 835592 | tf_op jit(solution)/shard_map/ppermute | solution.py:429
  38.8 12.4 %collective-permute-start.2 = (bf16[272,512]{1,0:T(8,128)(2,1)S(1)}, bf16[272,512]{1,0:T(8,128)(2,1)S(1)}, u32[]{:S(2)}, u32[]{:S(2)}) collective-permute-start(bf16[272,512]{1,0:T(8,128)(2,1)S(1)} %get-tuple-element.74), channel_id=1, source_target_pairs={{0,8},{4,12},{8,16},{12,20},{16,24},{20,28},{24,0},{28,4},{32,40},... | collective-permute-start | bytes 835592 | tf_op jit(solution)/shard_map/ppermute | solution.py:429
  51.6 9.1 %collective-permute-start.5 = (bf16[272,512]{1,0:T(8,128)(2,1)S(1)}, bf16[272,512]{1,0:T(8,128)(2,1)S(1)}, u32[]{:S(2)}, u32[]{:S(2)}) collective-permute-start(bf16[272,512]{1,0:T(8,128)(2,1)S(1)} %pad_maximum_fusion.4), channel_id=1, source_target_pairs={{0,32},{4,36},{8,40},{12,44},{16,48},{20,52},{24,56},{28,60},{32,6... | collective-permute-start | bytes 835592 | tf_op jit(solution)/shard_map/ppermute | solution.py:429
  54.9 11.4 %collective-permute-start.6 = (bf16[272,512]{1,0:T(8,128)(2,1)S(1)}, bf16[272,512]{1,0:T(8,128)(2,1)S(1)}, u32[]{:S(2)}, u32[]{:S(2)}) collective-permute-start(bf16[272,512]{1,0:T(8,128)(2,1)S(1)} %pad_maximum_fusion.4), channel_id=1, source_target_pairs={{0,64},{4,68},{8,72},{12,76},{16,80},{20,84},{24,88},{28,92},{32,9... | collective-permute-start | bytes 835592 | tf_op jit(solution)/shard_map/ppermute | solution.py:429
  59.2 10.8 %collective-permute-start.7 = (bf16[272,512]{1,0:T(8,128)(2,1)S(1)}, bf16[272,512]{1,0:T(8,128)(2,1)S(1)}, u32[]{:S(2)}, u32[]{:S(2)}) collective-permute-start(bf16[272,512]{1,0:T(8,128)(2,1)S(1)} %pad_maximum_fusion.4), channel_id=1, source_target_pairs={{0,96},{4,100},{8,104},{12,108},{16,112},{20,116},{24,120},{28,124... | collective-permute-start | bytes 835592 | tf_op jit(solution)/shard_map/ppermute | solution.py:429
  70.7 4.8 %copy-start.3 = (bf16[256,512]{1,0:T(8,128)(2,1)}, bf16[256,512]{1,0:T(8,128)(2,1)S(1)}, u32[]{:S(2)}) copy-start(bf16[256,512]{1,0:T(8,128)(2,1)S(1)} %get-tuple-element.84.sent_ref) | copy-start | bytes 786436
  70.7 15.8 %collective-permute-start.8 = (bf16[256,512]{1,0:T(8,128)(2,1)S(1)}, bf16[256,512]{1,0:T(8,128)(2,1)S(1)}, u32[]{:S(2)}, u32[]{:S(2)}) collective-permute-start(bf16[256,512]{1,0:T(8,128)(2,1)S(1)} %get-tuple-element.83), channel_id=1, source_target_pairs={{0,8},{4,12},{8,16},{12,20},{16,24},{20,28},{24,0},{28,4},{32,40},... | collective-permute-start | bytes 786440 | tf_op jit(solution)/shard_map/ppermute | solution.py:429
  71.2 15.3 %collective-permute-start.9 = (bf16[256,512]{1,0:T(8,128)(2,1)S(1)}, bf16[256,512]{1,0:T(8,128)(2,1)S(1)}, u32[]{:S(2)}, u32[]{:S(2)}) collective-permute-start(bf16[256,512]{1,0:T(8,128)(2,1)S(1)} %get-tuple-element.82), channel_id=1, source_target_pairs={{0,16},{4,20},{8,24},{12,28},{16,0},{20,4},{24,8},{28,12},{32,48},... | collective-permute-start | bytes 786440 | tf_op jit(solution)/shard_map/ppermute | solution.py:429
  73.5 13.0 %collective-permute-start.10 = (bf16[256,512]{1,0:T(8,128)(2,1)S(1)}, bf16[256,512]{1,0:T(8,128)(2,1)S(1)}, u32[]{:S(2)}, u32[]{:S(2)}) collective-permute-start(bf16[256,512]{1,0:T(8,128)(2,1)S(1)} %get-tuple-element.84.sent_ref), channel_id=1, source_target_pairs={{0,24},{4,28},{8,0},{12,4},{16,8},{20,12},{24,16},{28,20},{32,56},... | collective-permute-start | bytes 786440 | tf_op jit(solution)/shard_map/ppermute | solution.py:429
  86.8 2.9 %copy-start.4 = (s32[64]{0:T(128)S(1)}, s32[64]{0:T(128)}, u32[]{:S(2)}) copy-start(s32[64]{0:T(128)} %param.28) | copy-start | bytes 772
  88.3 10.7 %collective-permute-start.11 = (bf16[256,2048]{1,0:T(8,128)(2,1)S(1)}, bf16[256,2048]{1,0:T(8,128)(2,1)S(1)}, u32[]{:S(2)}, u32[]{:S(2)}) collective-permute-start(bf16[256,2048]{1,0:T(8,128)(2,1)S(1)} %get-tuple-element.65), channel_id=1, source_target_pairs={{0,4},{4,0},{8,12},{12,8},{16,20},{20,16},{24,28},{28,24},{32,36},... | collective-permute-start | bytes 3145736 | tf_op jit(solution)/shard_map/ppermute | solution.py:429
  99.0 1.0 copy-start.1

commit v3 on v2

--- a/solution.py
+++ b/solution.py
@@ -48,9 +48,12 @@
     return high, mid, (rest - mid.astype(F32)).astype(BF16)
 
 
+def silu_of_twice(half):
+    return half + half * jnp.tanh(half)
+
+
 def silu(v):
-    half = 0.5 * v
-    return half + half * jnp.tanh(half)
+    return silu_of_twice(0.5 * v)
 
 
 def decay_kernel(
@@ -129,18 +132,20 @@
     )(dt_in, bias, a_log)
 
 
-def conv_column(pad, series, tail, taps, offset, store):
-    rows = series.shape[0]
+def load_column(pad, series, tail):
     pad[0:8, :] = tail[...].astype(F32)[TAIL - 8 :]
-    pad[8 : 8 + rows, :] = series[...].astype(F32)
-    for start in range(0, rows, CHUNK):
-        total = offset + taps[3] * pad[8 + start : 8 + start + CHUNK, :]
-        for k in range(3):
-            total = total + taps[k] * pad[5 + k + start : 5 + k + start + CHUNK, :]
-        store(start, silu(total))
+    pad[8 : 8 + series.shape[0], :] = series[...].astype(F32)
+
+
+def conv_rows(pad, start, taps, offset):
+    total = offset + taps[3] * pad[8 + start : 8 + start + CHUNK, :]
+    for k in range(3):
+        total = total + taps[k] * pad[5 + k + start : 5 + k + start + CHUNK, :]
+    return silu_of_twice(total).astype(BF16)
 
 
 def state_kernel(core_ref, x_ref, xt_ref, wx_ref, ox_ref, wabs_ref, spread_ref, tot_ref, *rest):
+    rows = x_ref.shape[0]
     cx_ref, state_ref, pad, scaled, bturn = rest[-5:]
     if len(rest) == 6:
         made_ref = rest[0]
@@ -156,34 +161,34 @@
         def _():
             for n, (src, tail, dst) in enumerate(((b_ref, bt_ref, cb_ref), (c_ref, ct_ref, cc_ref))):
                 for lane in range(0, STATE, 128):
-                    cut = (slice(None), slice(lane, lane + 128))
-
-                    def store(start, v, dst=dst, lane=lane):
-                        dst[start : start + CHUNK, lane : lane + 128] = v.astype(BF16)
-
-                    taps = [wb_ref[k, n : n + 1, lane : lane + 128] for k in range(4)]
-                    offset = ob_ref[n : n + 1, lane : lane + 128]
-                    conv_column(pad, src.at[cut], tail.at[cut], taps, offset, store)
+                    own = slice(lane, lane + 128)
+                    load_column(pad.at[0], src.at[:, own], tail.at[:, own])
+                    taps = [0.5 * wb_ref[k, n : n + 1, own] for k in range(4)]
+                    offset = 0.5 * ob_ref[n : n + 1, own]
+                    for start in range(0, rows, CHUNK):
+                        dst[start : start + CHUNK, own] = conv_rows(pad.at[0], start, taps, offset)
             bturn[...] = cb_ref[...].T
 
-    for lane in range(0, TILE, 128):
-        own = slice(lane, lane + 128)
-        cut = (slice(None), own)
-
-        def store(start, v, own=own):
-            v = v.astype(BF16)
-            cx_ref[start : start + CHUNK, own] = v
-            w = dot(wabs_ref[start : start + CHUNK, :], spread_ref[0, :, own])
-            scaled[start : start + CHUNK, own] = (w * v.astype(F32)).astype(BF16)
-
-        taps = [wx_ref[k : k + 1, own] for k in range(4)]
-        conv_column(pad, x_ref.at[cut], xt_ref.at[cut], taps, ox_ref[:, own], store)
+    for lane in range(0, TILE, 256):
+        sides = [slice(lane + 128 * n, lane + 128 * n + 128) for n in range(2)]
+        for n, own in enumerate(sides):
+            load_column(pad.at[n], x_ref.at[:, own], xt_ref.at[:, own])
+        taps = [[0.5 * wx_ref[k : k + 1, own] for k in range(4)] for own in sides]
+        offsets = [0.5 * ox_ref[:, own] for own in sides]
+        for start in range(0, rows, CHUNK):
+            here = slice(start, start + CHUNK)
+            w = dot(wabs_ref[here, :], spread_ref[0, :, lane : lane + 256])
+            for n, own in enumerate(sides):
+                v = conv_rows(pad.at[n], start, taps[n], offsets[n])
+                cx_ref[here, own] = v
+                scaled[here, own] = (w[:, 128 * n : 128 * n + 128] * v.astype(F32)).astype(BF16)
     state_ref[0:STATE, :] = dot(bturn[...], scaled[...]).astype(BF16)
     state_ref[STATE:, :] = dot(tot_ref[...], spread_ref[0]).astype(BF16)
 
 
 def group_of(turn, core):
-    return core[0] if turn else 1 - core[0]
+    own = lax.rem(core[0], 2)
+    return own if turn else 1 - own
 
 
 def local_states(turn, half, core, x, tails, wx, ox, wabs, spread, tot, bc, wbc, obc, made=None):
@@ -228,7 +233,7 @@
             out_specs=[pl.BlockSpec((rows, STATE), still)] * fresh
             + [pl.BlockSpec((rows, TILE), out), pl.BlockSpec((STATE + EXTRA, TILE), out)],
             scratch_shapes=[
-                pltpu.VMEM((rows + 8, 128), F32),
+                pltpu.VMEM((2, rows + 8, 128), F32),
                 pltpu.VMEM((rows, TILE), BF16),
                 pltpu.VMEM((STATE, rows), BF16),
             ],
@@ -349,18 +354,19 @@
     )(core, x, b, c, run, row, ehl, whl, spread, sent)
 
 
-def norm_kernel(core_ref, c_ref, eabs_ref, spread_ref, z_ref, gain_ref, reward_ref, *rest):
-    values, states = rest[:HALVES], rest[HALVES : 2 * HALVES]
-    out_ref, term_ref, gated = rest[-3:]
+def norm_kernel(
+    devices, place_ref, c_ref, state_ref, values_ref, z_ref, eabs_ref, spread_ref, gain_ref, reward_ref, ends_ref, *rest
+):
+    earlier = rest[0] if devices else None
+    out_ref, term_ref, gated, sums = rest[-4:]
     rows = c_ref.shape[0]
+    step = pl.program_id(0)
     c = c_ref[...]
     decay = eabs_ref[...]
     squares = jnp.zeros((rows, 128), F32)
     for lane in range(0, LANES, 256):
         cut = slice(lane, lane + 256)
-        half, low = divmod(lane, LANES // HALVES)
-        own = slice(low, low + 256)
-        v = values[half][:, own].astype(F32) + dot(decay, spread_ref[0, :, cut]) * dot(c, states[half][:, own])
+        v = values_ref[:, cut].astype(F32) + dot(decay, spread_ref[0, :, cut]) * dot(c, state_ref[:, cut])
         v = v * silu(z_ref[:, cut].astype(F32))
         gated[:, cut] = v
         squares = squares + v[:, :128] * v[:, :128] + v[:, 128:] * v[:, 128:]
@@ -371,42 +377,66 @@
         v = (gated[:, cut] * scale * gain_ref[:, cut]).astype(BF16)
         out_ref[:, cut] = v
         terms = terms + v.astype(F32) * reward_ref[:, cut]
-    term_ref[...] = terms
-
-
-def gated_norm(turn, core, values, c, states, eabs, spread, z, gain, reward, target):
+    if devices:
+        first = (place_ref[0] * pl.num_programs(0) + step) * rows
+        row = lax.broadcasted_iota(jnp.int32, (rows, ends_ref.shape[1]), 0)
+        term = jnp.sum(terms + earlier[...], axis=1, keepdims=True)
+        found = jnp.where(row == ends_ref[...] - first, term, 0.0)
+        found = jnp.sum(found, axis=0, keepdims=True)
+
+        @pl.when(step == 0)
+        def _():
+            sums[...] = jnp.zeros_like(sums)
+
+        sums[0:1, :] = sums[0:1, :] + found
+
+        @pl.when(step == pl.num_programs(0) - 1)
+        def _():
+            term_ref[...] = jnp.broadcast_to(sums[0:1, :], term_ref.shape)
+
+    else:
+        term_ref[...] = terms
+
+
+def gated_norm(turn, core, values, c, state, eabs, spread, z, gain, reward, ends, earlier=None, devices=0):
     rows = c.shape[0]
-    width = LANES // HALVES
+    count = ends.shape[1]
     own = lambda i, core: (i, group_of(turn, core))
     side = lambda i, core: (0, group_of(turn, core))
     down = lambda i, core: (i, 0)
     still = lambda i, core: (0, 0)
+    more = [pl.BlockSpec((ROWS, 128), down), pl.BlockSpec(memory_space=pl.ANY)] if devices else []
+    terms = (devices, count) if devices else (rows, 128)
     return pl.pallas_call(
-        norm_kernel,
+        functools.partial(norm_kernel, devices),
         grid_spec=pltpu.PrefetchScalarGridSpec(
             num_scalar_prefetch=1,
             grid=(rows // ROWS,),
             in_specs=[
                 pl.BlockSpec((ROWS, STATE), down),
+                pl.BlockSpec((STATE, LANES), still),
+                pl.BlockSpec((ROWS, LANES), down),
+                pl.BlockSpec((ROWS, LANES), own),
                 pl.BlockSpec((ROWS, eabs.shape[1]), down),
                 pl.BlockSpec((1, spread.shape[1], LANES), lambda i, core: (group_of(turn, core), 0, 0)),
-                pl.BlockSpec((ROWS, LANES), own),
                 pl.BlockSpec((1, LANES), side),
                 pl.BlockSpec((1, LANES), side),
+                pl.BlockSpec((1, count), still),
             ]
-            + [pl.BlockSpec((ROWS, width), down)] * HALVES
-            + [pl.BlockSpec((STATE, width), still)] * HALVES
-            + ([] if target is None else [pl.BlockSpec(memory_space=pl.ANY)]),
-            out_specs=[pl.BlockSpec((ROWS, LANES), own), pl.BlockSpec((ROWS, 128), down)],
-            scratch_shapes=[pltpu.VMEM((ROWS, LANES), F32)],
-        ),
-        out_shape=[jax.ShapeDtypeStruct(z.shape, BF16), jax.ShapeDtypeStruct((rows, 128), F32)],
-        input_output_aliases={} if target is None else {7 + 2 * HALVES: 0},
+            + more,
+            out_specs=[
+                pl.BlockSpec((ROWS, LANES), own),
+                pl.BlockSpec(terms, still) if devices else pl.BlockSpec((ROWS, 128), down),
+            ],
+            scratch_shapes=[pltpu.VMEM((ROWS, LANES), F32), pltpu.VMEM((8, count), F32)],
+        ),
+        out_shape=[jax.ShapeDtypeStruct(z.shape, BF16), jax.ShapeDtypeStruct(terms, F32)],
+        input_output_aliases={11: 0} if devices else {},
         compiler_params=params("arbitrary"),
         cost_estimate=pl.CostEstimate(
-            flops=2 * rows * STATE * LANES, bytes_accessed=8 * rows * LANES, transcendentals=rows * LANES
-        ),
-    )(core, c, eabs, spread, z, gain, reward, *values, *states, *(() if target is None else (target,)))
+            flops=2 * rows * STATE * LANES, bytes_accessed=6 * rows * LANES, transcendentals=rows * LANES
+        ),
+    )(core, c, state, values, z, eabs, spread, gain, reward, ends, *(earlier or ()))
 
 
 def total_of(payload):
@@ -479,7 +509,7 @@
 ):
     rows = x_in.shape[0]
     place = lax.axis_index("seq")
-    core = (place % 2).reshape(1)
+    core = place.reshape(1)
     bc = bc_in.reshape(rows, -1)
     tails = jnp.concatenate([x_in[rows - TAIL :], bc_in[rows - TAIL :].reshape(TAIL, -1)], axis=1)
     tails = over(tails, lambda i: i + 1 if i + 1 < 32 else None)
@@ -498,36 +528,29 @@
                     made[turn][0][0] if half else None,
                 )
             )
-    values = [[], []]
+    values = [None, None]
 
     def inner(turn, sent):
         m = made[turn]
-        done = None
-        for half in range(HALVES):
-            v, done = local_values(
-                turn, half, core, m[half][-2], m[0][0], m[0][1], run, row, ehl, whl, spread, sent
-            )
-            values[turn].append(v)
+        values[turn], done = local_values(
+            turn, 0, core, m[0][-2], m[0][0], m[0][1], run, row, ehl, whl, spread, sent
+        )
         return done[0]
 
     steps = entering_state(made[0][0][-1], made[1][0][-1])
     sent = next(steps)
     sent = steps.send(inner(1, sent))
-    entered = [steps.send(inner(0, sent))]
-    normed, sums = None, []
-    for turn in (1, 0):
-        normed, part = gated_norm(
-            turn, core, values[turn], made[turn][0][1], [e[turn] for e in entered], eabs, spread, z_in,
-            norm_gain[None], reward_w[None], normed,
-        )
-        sums.append(part)
-    local_pos = step_ends - place * rows
-    inside = (local_pos >= 0) & (local_pos < rows)
-    at = jnp.clip(local_pos, 0, rows - 1)
-    terms = jnp.sum(jnp.take(sums[0], at, axis=0) + jnp.take(sums[1], at, axis=0), axis=1)
-    terms = jnp.where(inside, terms, 0.0)
+    entered = steps.send(inner(0, sent))
+    gain, reward, ends = norm_gain[None], reward_w[None], step_ends[None]
     devices = lax.axis_size("seq") * lax.axis_size("head")
-    terms = lax.all_to_all(jnp.broadcast_to(terms, (devices, terms.shape[0])), ("seq", "head"), 0, 0)
+    normed, terms = gated_norm(
+        1, core, values[1], made[1][0][1], entered[1], eabs, spread, z_in, gain, reward, ends
+    )
+    normed, terms = gated_norm(
+        0, core, values[0], made[0][0][1], entered[0], eabs, spread, z_in, gain, reward, ends,
+        (terms, normed), devices,
+    )
+    terms = lax.all_to_all(terms, ("seq", "head"), 0, 0)
     return normed, jnp.sum(terms, axis=0)
 
 

time: 130 us -> 126 us (0.969)
  local copies, waits for them, and re-layouts: 9.76 us -> 6.54 us
    gather x2 -> x0, local copies, waits for them, and re-layouts: 3.18 us -> none  [the longest x1 1.59 us: per_device(): jnp.take(sums[1], at, axis=0)]
    unnamed x12 -> x10, local copies, waits for them, and re-layouts: 4.68 us -> 4.68 us
  transfers between devices with their start and end apart: 12 -> 12, of which waited for: 3 -> 3; matrix products, arithmetic and copies ran while one was open for 4% -> 2% of each run, Pallas kernels for 32% -> 33%
where the time goes in v3:
time: 126 us; the launch traced here: 125 us
  Pallas kernels  58.7 us (47%)
  starting transfers between devices  23.4 us (19%)
  blocking collectives  19.3 us (15%)
  waiting for transfers between devices  9.31 us (7%)
  local copies, waits for them, and re-layouts  6.54 us (5%)
  other arithmetic  5.44 us (4%)
  between operations  2.56 us (2%)
    ppermute x12, starting transfers between devices, over(): lax.ppermute(value, 'seq', [(i, move(i)) for i in range(count) if move(i)...  23.4 us
    pallas_call x2, Pallas kernels, local_values(): pl.pallas_call(values_kernel, grid_spec=pltpu.PrefetchScalarGridSpec(num_...  20.9 us
    all_to_all x1, blocking collectives, per_device(): terms = lax.all_to_all(terms, ('seq', 'head'), 0, 0)  19.3 us
    pallas_call x2, Pallas kernels, local_states(): pl.pallas_call(state_kernel, grid_spec=pltpu.PrefetchScalarGridSpec(num_s...  18.5 us
    pallas_call x2, Pallas kernels, gated_norm(): pl.pallas_call(functools.partial(norm_kernel, devices), grid_spec=pltpu.P...  16.5 us
    ppermute x12, waiting for transfers between devices, over(): lax.ppermute(value, 'seq', [(i, move(i)) for i in range(count) if move(i)...  9.31 us
    unnamed x10, local copies, waits for them, and re-layouts  4.68 us
    pallas_call x1, Pallas kernels, decays(): pl.pallas_call(decay_kernel, out_shape=[jax.ShapeDtypeStruct((heads, rows...  2.91 us
  transfers between devices with their start and end apart: 12, of which 3 were waited for; matrix products, arithmetic and copies ran while one was open for 2% of the time, Pallas kernels for 33%

profile of v3, /device:TPU:1, one launch (start us, length us, event | category | flops | bytes accessed | tf_op | source)
XLA Modules:
  0.0 125.2 jit_solution(14957598565165302303)
XLA Ops:
  0.6 0.8 slice.186
  1.4 0.9 slice.185
  2.4 4.6 %collective-permute-start = (bf16[16,5120]{1,0:T(8,128)(2,1)S(1)}, bf16[16,5120]{1,0:T(8,128)(2,1)S(1)}, u32[]{:S(2)}, u32[]{:S(2)}) collective-permute-start(bf16[16,5120]{1,0:T(8,128)(2,1)S(1)} %pad_maximum_fusion.5), channel_id=1, source_target_pairs={{0,4},{4,8},{8,12},{12,16},{16,20},{20,24},{24,28},{28,32},{32,36}... | collective-permute-start | bytes 491528 | tf_op jit(solution)/shard_map/ppermute | solution.py:459
  7.0 3.0 %copy.19 = bf16[96,8,2,512]{3,1,2,0:T(8,128)(2,1)} copy(bf16[96,8,2,512]{3,2,1,0:T(2,128)(2,1)} %bitcast.108) | data formatting | bytes 3145728
  10.0 2.9 %shard_map.149 = (f32[64,768]{1,0:T(8,128)}, f32[64,768]{1,0:T(8,128)}, bf16[768,128]{1,0:T(8,128)(2,1)}, bf16[768,128]{1,0:T(8,128)(2,1)}, bf16[768,128]{1,0:T(...) custom-call(f32[64,768]{1,0:T(8,128)} %bitcast.138, f32[1,64]{1,0:T(1,128)} %bitcast.139, f32[1,64]{1,0:T(1,128)} %bitcast.140), custom_call_target="tpu_custom_call" | custom-call | flops 100000000 | bytes 2000000 | tf_op jit(solution)/shard_map/pallas_call | solution.py:119
  12.9 0.7 copy-done
  13.6 9.2 %shard_map.150 = (bf16[768,256]{1,0:T(8,128)(2,1)}, bf16[768,256]{1,0:T(8,128)(2,1)}, bf16[768,2048]{1,0:T(8,128)(2,1)}, bf16[272,2048]{1,0:T(8,128)(2,1)}) custom-call(s32[1]{0:T(128)} %bitcast.core_ref.place_ref, bf16[768,4096]{1,0:T(8,128)(2,1)} %x_ref.3, bf16[16,5120]{1,0:T(8,128)(2,1)} %copy-done, f32[4,4096]{1,0:T(4,128)} %wx_ref.3, ...), custom_call_target="tpu_custom_call" | custom-call | flops 805306368 | bytes 6291456 | tf_op jit(solution)/shard_map/pallas_call | solution.py:218
  23.0 9.3 %shard_map.151 = (bf16[768,256]{1,0:T(8,128)(2,1)}, bf16[768,256]{1,0:T(8,128)(2,1)}, bf16[768,2048]{1,0:T(8,128)(2,1)}, bf16[272,2048]{1,0:T(8,128)(2,1)}) custom-call(s32[1]{0:T(128)} %bitcast.core_ref.place_ref, bf16[768,4096]{1,0:T(8,128)(2,1)} %x_ref.3, bf16[16,5120]{1,0:T(8,128)(2,1)} %copy-done, f32[4,4096]{1,0:T(4,128)} %wx_ref.3, ...), custom_call_target="tpu_custom_call" | custom-call | flops 805306368 | bytes 6291456 | tf_op jit(solution)/shard_map/pallas_call | solution.py:218
  32.3 1.4 %broadcast_select_fusion.1 = (bf16[272,2048]{1,0:T(8,128)(2,1)S(1)}, bf16[272,2048]{1,0:T(8,128)(2,1)S(1)}) fusion(bf16[272,2048]{1,0:T(8,128)(2,1)} %get-tuple-element.28, bf16[272,2048]{1,0:T(8,128)(2,1)S(1)} %collective-permute-done.1, pred[]{:T(512)S(6)} %eq.25), kind=kLoop, calls=%fused_computation.13 | loop fusion | flops 1114112 | bytes 4456449 | tf_op jit(solution)/shard_map/jit(_where)/select_n | solution.py:471
  33.8 0.4 fusion.1
  34.4 1.4 %collective-permute-start.2 = (bf16[272,512]{1,0:T(8,128)(2,1)S(1)}, bf16[272,512]{1,0:T(8,128)(2,1)S(1)}, u32[]{:S(2)}, u32[]{:S(2)}) collective-permute-start(bf16[272,512]{1,0:T(8,128)(2,1)S(1)} %get-tuple-element.70), channel_id=1, source_target_pairs={{0,8},{4,12},{8,16},{12,20},{16,24},{20,28},{24,0},{28,4},{32,40},... | collective-permute-start | bytes 835592 | tf_op jit(solution)/shard_map/ppermute | solution.py:459
  35.8 2.2 %collective-permute-start.3 = (bf16[272,512]{1,0:T(8,128)(2,1)S(1)}, bf16[272,512]{1,0:T(8,128)(2,1)S(1)}, u32[]{:S(2)}, u32[]{:S(2)}) collective-permute-start(bf16[272,512]{1,0:T(8,128)(2,1)S(1)} %get-tuple-element.71), channel_id=1, source_target_pairs={{0,16},{4,20},{8,24},{12,28},{16,0},{20,4},{24,8},{28,12},{32,48},... | collective-permute-start | bytes 835592 | tf_op jit(solution)/shard_map/ppermute | solution.py:459
  38.0 1.2 collective-permute-start.4
  39.2 10.4 %shard_map.152 = (bf16[768,2048]{1,0:T(8,128)(2,1)}, s32[1]{0:T(128)}) custom-call(s32[1]{0:T(128)} %bitcast.core_ref.place_ref, bf16[768,2048]{1,0:T(8,128)(2,1)} %get-tuple-element.30.x_ref, bf16[768,256]{1,0:T(8,128)(2,1)} %get-tuple-element.31.b_ref, bf16[768,256]{1,0:T(8,128)(2,1)} %get-tuple-element.32.c_ref, f32[64,768]{1,0:T(8,128)} %get-tuple-element.33.run_ref, ...), custom_call_target="tpu_custom_call" | custom-call | flops 3221225472 | bytes 12582912 | tf_op jit(solution)/shard_map/pallas_call | solution.py:326
  50.9 4.7 %collective-permute-start.6 = (bf16[272,512]{1,0:T(8,128)(2,1)S(1)}, bf16[272,512]{1,0:T(8,128)(2,1)S(1)}, u32[]{:S(2)}, u32[]{:S(2)}) collective-permute-start(bf16[272,512]{1,0:T(8,128)(2,1)S(1)} %pad_maximum_fusion.4), channel_id=1, source_target_pairs={{0,64},{4,68},{8,72},{12,76},{16,80},{20,84},{24,88},{28,92},{32,9... | collective-permute-start | bytes 835592 | tf_op jit(solution)/shard_map/ppermute | solution.py:459
  55.7 1.3 %collective-permute-start.7 = (bf16[272,512]{1,0:T(8,128)(2,1)S(1)}, bf16[272,512]{1,0:T(8,128)(2,1)S(1)}, u32[]{:S(2)}, u32[]{:S(2)}) collective-permute-start(bf16[272,512]{1,0:T(8,128)(2,1)S(1)} %pad_maximum_fusion.4), channel_id=1, source_target_pairs={{0,96},{4,100},{8,104},{12,108},{16,112},{20,116},{24,120},{28,124... | collective-permute-start | bytes 835592 | tf_op jit(solution)/shard_map/ppermute | solution.py:459
  57.0 1.6 %collective-permute-start.5 = (bf16[272,512]{1,0:T(8,128)(2,1)S(1)}, bf16[272,512]{1,0:T(8,128)(2,1)S(1)}, u32[]{:S(2)}, u32[]{:S(2)}) collective-permute-start(bf16[272,512]{1,0:T(8,128)(2,1)S(1)} %pad_maximum_fusion.4), channel_id=1, source_target_pairs={{0,32},{4,36},{8,40},{12,44},{16,48},{20,52},{24,56},{28,60},{32,6... | collective-permute-start | bytes 835592 | tf_op jit(solution)/shard_map/ppermute | solution.py:459
  58.6 1.7 %collective-permute-done.6 = bf16[272,512]{1,0:T(8,128)(2,1)S(1)} collective-permute-done((bf16[272,512]{1,0:T(8,128)(2,1)S(1)}, bf16[272,512]{1,0:T(8,128)(2,1)S(1)}, u32[]{:S(2)}, u32[]{:S(2)}) %collective-permute-start.6) | collective-permute-done | bytes 278560 | tf_op jit(solution)/shard_map/ppermute | solution.py:459
  60.4 6.0 %collective-permute-done.5 = bf16[272,512]{1,0:T(8,128)(2,1)S(1)} collective-permute-done((bf16[272,512]{1,0:T(8,128)(2,1)S(1)}, bf16[272,512]{1,0:T(8,128)(2,1)S(1)}, u32[]{:S(2)}, u32[]{:S(2)}) %collective-permute-start.5) | collective-permute-done | bytes 278560 | tf_op jit(solution)/shard_map/ppermute | solution.py:459
  66.4 1.6 %collective-permute-done.7 = bf16[272,512]{1,0:T(8,128)(2,1)S(1)} collective-permute-done((bf16[272,512]{1,0:T(8,128)(2,1)S(1)}, bf16[272,512]{1,0:T(8,128)(2,1)S(1)}, u32[]{:S(2)}, u32[]{:S(2)}) %collective-permute-start.7) | collective-permute-done | bytes 278560 | tf_op jit(solution)/shard_map/ppermute | solution.py:459
  68.1 0.3 convert_bitcast_fusion
  68.6 2.4 %collective-permute-start.9 = (bf16[256,512]{1,0:T(8,128)(2,1)S(1)}, bf16[256,512]{1,0:T(8,128)(2,1)S(1)}, u32[]{:S(2)}, u32[]{:S(2)}) collective-permute-start(bf16[256,512]{1,0:T(8,128)(2,1)S(1)} %get-tuple-element.79), channel_id=1, source_target_pairs={{0,16},{4,20},{8,24},{12,28},{16,0},{20,4},{24,8},{28,12},{32,48},... | collective-permute-start | bytes 786440 | tf_op jit(solution)/shard_map/ppermute | solution.py:459
  71.0 1.3 %collective-permute-start.8 = (bf16[256,512]{1,0:T(8,128)(2,1)S(1)}, bf16[256,512]{1,0:T(8,128)(2,1)S(1)}, u32[]{:S(2)}, u32[]{:S(2)}) collective-permute-start(bf16[256,512]{1,0:T(8,128)(2,1)S(1)} %get-tuple-element.80), channel_id=1, source_target_pairs={{0,8},{4,12},{8,16},{12,20},{16,24},{20,28},{24,0},{28,4},{32,40},... | collective-permute-start | bytes 786440 | tf_op jit(solution)/shard_map/ppermute | solution.py:459
  72.3 1.4 %collective-permute-start.10 = (bf16[256,512]{1,0:T(8,128)(2,1)S(1)}, bf16[256,512]{1,0:T(8,128)(2,1)S(1)}, u32[]{:S(2)}, u32[]{:S(2)}) collective-permute-start(bf16[256,512]{1,0:T(8,128)(2,1)S(1)} %get-tuple-element.78.sent_ref), channel_id=1, source_target_pairs={{0,24},{4,28},{8,0},{12,4},{16,8},{20,12},{24,16},{28,20},{32,56},... | collective-permute-start | bytes 786440 | tf_op jit(solution)/shard_map/ppermute | solution.py:459
  73.7 10.4 %shard_map.153 = (bf16[768,2048]{1,0:T(8,128)(2,1)}, s32[1]{0:T(128)}) custom-call(s32[1]{0:T(128)} %bitcast.core_ref.place_ref, bf16[768,2048]{1,0:T(8,128)(2,1)} %get-tuple-element.38.x_ref, bf16[768,256]{1,0:T(8,128)(2,1)} %get-tuple-element.39.b_ref, bf16[768,256]{1,0:T(8,128)(2,1)} %get-tuple-element.27.c_ref, f32[64,768]{1,0:T(8,128)} %get-tuple-element.33.run_ref, ...), custom_call_target="tpu_custom_call" | custom-call | flops 3221225472 | bytes 12582912 | tf_op jit(solution)/shard_map/pallas_call | solution.py:326
  85.0 1.5 %fusion.3 = (bf16[256,2048]{1,0:T(8,128)(2,1)}, bf16[256,2048]{1,0:T(8,128)(2,1)S(1)}) fusion(f32[2048]{0:T(1024)S(1)} %bitcast.124, pred[]{:T(512)S(6)} %eq.25, bf16[272,2048]{1,0:T(8,128)(2,1)S(1)} %get-tuple-element.58, bf16[256,512]{1,0:T(8,128)(2,1)S(1)} %get-tuple-element.74, bf16[256,512]{1,0:T(8,128)(2,1)S(1)} %get-tuple-element.75, ...), kind=kLoop, calls=%fused_computation.9 | loop fusion | flops 7864320 | bytes 4202497 | tf_op jit(solution)/shard_map/jit(_where)/select_n | solution.py:503
  86.5 1.4 %collective-permute-start.11 = (bf16[256,2048]{1,0:T(8,128)(2,1)S(1)}, bf16[256,2048]{1,0:T(8,128)(2,1)S(1)}, u32[]{:S(2)}, u32[]{:S(2)}) collective-permute-start(bf16[256,2048]{1,0:T(8,128)(2,1)S(1)} %get-tuple-element.61), channel_id=1, source_target_pairs={{0,4},{4,0},{8,12},{12,8},{16,20},{20,16},{24,28},{28,24},{32,36},... | collective-permute-start | bytes 3145736 | tf_op jit(solution)/shard_map/ppermute | solution.py:459
  87.9 7.9 %shard_map.154 = (bf16[768,4096]{1,0:T(8,128)(2,1)}, f32[768,128]{1,0:T(8,128)}) custom-call(s32[1]{0:T(128)} %bitcast.core_ref.place_ref, bf16[768,256]{1,0:T(8,128)(2,1)} %get-tuple-element.32.c_ref, bf16[256,2048]{1,0:T(8,128)(2,1)} %get-tuple-element.60.state_ref, bf16[768,2048]{1,0:T(8,128)(2,1)} %get-tuple-element.43.values_ref, ...), custom_call_target="tpu_custom_call" | custom-call | flops 805306368 | bytes 9437184 | tf_op jit(solution)/shard_map/pallas_call | solution.py:410
  95.8 1.0 copy-done.1
  96.7 8.6 %shard_map.155 = (bf16[768,4096]{1,0:T(8,128)(2,1)}, f32[128,64]{1,0:T(8,128)}) custom-call(s32[1]{0:T(128)} %bitcast.core_ref.place_ref, bf16[768,256]{1,0:T(8,128)(2,1)} %get-tuple-element.27.c_ref, bf16[256,2048]{1,0:T(8,128)(2,1)} %copy-done.1, bf16[768,2048]{1,0:T(8,128)(2,1)} %get-tuple-element.41.values_ref, ...), custom_call_target="tpu_custom_call", output_to_operand_aliasing={{0}: (11, {})} | custom-call | flops 805306368 | bytes 9437184 | tf_op jit(solution)/shard_map/pallas_call | solution.py:410
  105.3 19.3 %all_to_all.9 = f32[128,1,64]{2,1,0:T(1,128)S(1)} all-to-all(f32[128,1,64]{2,1,0:T(1,128)} %bitcast.123), channel_id=1, replica_groups=mesh['seq'=32,'head'=4] {'seq','head'}, dimensions={0} | all-to-all | bytes 65536 | tf_op jit(solution)/shard_map/all_to_all | solution.py:553
  124.6 0.7 reduce_sum.9
  (43 shorter events, 1.5 us)
Async XLA Ops:
  2.4 10.5 %collective-permute-start = (bf16[16,5120]{1,0:T(8,128)(2,1)S(1)}, bf16[16,5120]{1,0:T(8,128)(2,1)S(1)}, u32[]{:S(2)}, u32[]{:S(2)}) collective-permute-start(bf16[16,5120]{1,0:T(8,128)(2,1)S(1)} %pad_maximum_fusion.5), channel_id=1, source_target_pairs={{0,4},{4,8},{8,12},{12,16},{16,20},{20,24},{24,28},{28,32},{32,36}... | collective-permute-start | bytes 491528 | tf_op jit(solution)/shard_map/ppermute | solution.py:459
  12.9 0.7 copy-start
  22.8 9.5 %collective-permute-start.1 = (bf16[272,2048]{1,0:T(8,128)(2,1)}, bf16[272,2048]{1,0:T(8,128)(2,1)S(1)}, u32[]{:S(2)}, u32[]{:S(2)}) collective-permute-start(bf16[272,2048]{1,0:T(8,128)(2,1)} %get-tuple-element.29), channel_id=1, source_target_pairs={{0,4},{4,0},{8,12},{12,8},{16,20},{20,16},{24,28},{28,24},{32,36},... | collective-permute-start | bytes 3342344 | tf_op jit(solution)/shard_map/ppermute | solution.py:459
  34.4 4.8 %copy-start.2 = (bf16[272,512]{1,0:T(8,128)(2,1)}, bf16[272,512]{1,0:T(8,128)(2,1)S(1)}, u32[]{:S(2)}) copy-start(bf16[272,512]{1,0:T(8,128)(2,1)S(1)} %get-tuple-element.72.sent_ref) | copy-start | bytes 835588
  34.4 16.0 %collective-permute-start.2 = (bf16[272,512]{1,0:T(8,128)(2,1)S(1)}, bf16[272,512]{1,0:T(8,128)(2,1)S(1)}, u32[]{:S(2)}, u32[]{:S(2)}) collective-permute-start(bf16[272,512]{1,0:T(8,128)(2,1)S(1)} %get-tuple-element.70), channel_id=1, source_target_pairs={{0,8},{4,12},{8,16},{12,20},{16,24},{20,28},{24,0},{28,4},{32,40},... | collective-permute-start | bytes 835592 | tf_op jit(solution)/shard_map/ppermute | solution.py:459
  35.8 14.6 %collective-permute-start.3 = (bf16[272,512]{1,0:T(8,128)(2,1)S(1)}, bf16[272,512]{1,0:T(8,128)(2,1)S(1)}, u32[]{:S(2)}, u32[]{:S(2)}) collective-permute-start(bf16[272,512]{1,0:T(8,128)(2,1)S(1)} %get-tuple-element.71), channel_id=1, source_target_pairs={{0,16},{4,20},{8,24},{12,28},{16,0},{20,4},{24,8},{28,12},{32,48},... | collective-permute-start | bytes 835592 | tf_op jit(solution)/shard_map/ppermute | solution.py:459
  38.0 12.4 %collective-permute-start.4 = (bf16[272,512]{1,0:T(8,128)(2,1)S(1)}, bf16[272,512]{1,0:T(8,128)(2,1)S(1)}, u32[]{:S(2)}, u32[]{:S(2)}) collective-permute-start(bf16[272,512]{1,0:T(8,128)(2,1)S(1)} %get-tuple-element.72.sent_ref), channel_id=1, source_target_pairs={{0,24},{4,28},{8,0},{12,4},{16,8},{20,12},{24,16},{28,20},{32,56},... | collective-permute-start | bytes 835592 | tf_op jit(solution)/shard_map/ppermute | solution.py:459
  50.9 9.4 %collective-permute-start.6 = (bf16[272,512]{1,0:T(8,128)(2,1)S(1)}, bf16[272,512]{1,0:T(8,128)(2,1)S(1)}, u32[]{:S(2)}, u32[]{:S(2)}) collective-permute-start(bf16[272,512]{1,0:T(8,128)(2,1)S(1)} %pad_maximum_fusion.4), channel_id=1, source_target_pairs={{0,64},{4,68},{8,72},{12,76},{16,80},{20,84},{24,88},{28,92},{32,9... | collective-permute-start | bytes 835592 | tf_op jit(solution)/shard_map/ppermute | solution.py:459
  55.7 12.3 %collective-permute-start.7 = (bf16[272,512]{1,0:T(8,128)(2,1)S(1)}, bf16[272,512]{1,0:T(8,128)(2,1)S(1)}, u32[]{:S(2)}, u32[]{:S(2)}) collective-permute-start(bf16[272,512]{1,0:T(8,128)(2,1)S(1)} %pad_maximum_fusion.4), channel_id=1, source_target_pairs={{0,96},{4,100},{8,104},{12,108},{16,112},{20,116},{24,120},{28,124... | collective-permute-start | bytes 835592 | tf_op jit(solution)/shard_map/ppermute | solution.py:459
  57.0 9.3 %collective-permute-start.5 = (bf16[272,512]{1,0:T(8,128)(2,1)S(1)}, bf16[272,512]{1,0:T(8,128)(2,1)S(1)}, u32[]{:S(2)}, u32[]{:S(2)}) collective-permute-start(bf16[272,512]{1,0:T(8,128)(2,1)S(1)} %pad_maximum_fusion.4), channel_id=1, source_target_pairs={{0,32},{4,36},{8,40},{12,44},{16,48},{20,52},{24,56},{28,60},{32,6... | collective-permute-start | bytes 835592 | tf_op jit(solution)/shard_map/ppermute | solution.py:459
  68.6 5.0 %copy-start.3 = (bf16[256,512]{1,0:T(8,128)(2,1)}, bf16[256,512]{1,0:T(8,128)(2,1)S(1)}, u32[]{:S(2)}) copy-start(bf16[256,512]{1,0:T(8,128)(2,1)S(1)} %get-tuple-element.78.sent_ref) | copy-start | bytes 786436
  68.6 16.1 %collective-permute-start.9 = (bf16[256,512]{1,0:T(8,128)(2,1)S(1)}, bf16[256,512]{1,0:T(8,128)(2,1)S(1)}, u32[]{:S(2)}, u32[]{:S(2)}) collective-permute-start(bf16[256,512]{1,0:T(8,128)(2,1)S(1)} %get-tuple-element.79), channel_id=1, source_target_pairs={{0,16},{4,20},{8,24},{12,28},{16,0},{20,4},{24,8},{28,12},{32,48},... | collective-permute-start | bytes 786440 | tf_op jit(solution)/shard_map/ppermute | solution.py:459
  71.0 13.8 %collective-permute-start.8 = (bf16[256,512]{1,0:T(8,128)(2,1)S(1)}, bf16[256,512]{1,0:T(8,128)(2,1)S(1)}, u32[]{:S(2)}, u32[]{:S(2)}) collective-permute-start(bf16[256,512]{1,0:T(8,128)(2,1)S(1)} %get-tuple-element.80), channel_id=1, source_target_pairs={{0,8},{4,12},{8,16},{12,20},{16,24},{20,28},{24,0},{28,4},{32,40},... | collective-permute-start | bytes 786440 | tf_op jit(solution)/shard_map/ppermute | solution.py:459
  72.3 12.5 %collective-permute-start.10 = (bf16[256,512]{1,0:T(8,128)(2,1)S(1)}, bf16[256,512]{1,0:T(8,128)(2,1)S(1)}, u32[]{:S(2)}, u32[]{:S(2)}) collective-permute-start(bf16[256,512]{1,0:T(8,128)(2,1)S(1)} %get-tuple-element.78.sent_ref), channel_id=1, source_target_pairs={{0,24},{4,28},{8,0},{12,4},{16,8},{20,12},{24,16},{28,20},{32,56},... | collective-permute-start | bytes 786440 | tf_op jit(solution)/shard_map/ppermute | solution.py:459
  86.5 9.3 %collective-permute-start.11 = (bf16[256,2048]{1,0:T(8,128)(2,1)S(1)}, bf16[256,2048]{1,0:T(8,128)(2,1)S(1)}, u32[]{:S(2)}, u32[]{:S(2)}) collective-permute-start(bf16[256,2048]{1,0:T(8,128)(2,1)S(1)} %get-tuple-element.61), channel_id=1, source_target_pairs={{0,4},{4,0},{8,12},{12,8},{16,20},{20,16},{24,28},{28,24},{32,36},... | collective-permute-start | bytes 3145736 | tf_op jit(solution)/shard_map/ppermute | solution.py:459
  95.8 1.0 copy-start.1

commit v4 on v3

--- a/solution.py
+++ b/solution.py
@@ -24,12 +24,11 @@
 F32 = jnp.float32
 BF16 = jnp.bfloat16
 VMEM_LIMIT = 56 * 1024 * 1024
-
-
-def params(*semantics):
-    return pltpu.CompilerParams(
-        dimension_semantics=semantics or None, vmem_limit_bytes=VMEM_LIMIT
-    )
+LESS_VMEM = 24 * 1024 * 1024
+
+
+def params(*semantics, limit=VMEM_LIMIT):
+    return pltpu.CompilerParams(dimension_semantics=semantics or None, vmem_limit_bytes=limit)
 
 
 def dot(a, b, ca=1, cb=0):
@@ -432,7 +431,7 @@
         ),
         out_shape=[jax.ShapeDtypeStruct(z.shape, BF16), jax.ShapeDtypeStruct(terms, F32)],
         input_output_aliases={11: 0} if devices else {},
-        compiler_params=params("arbitrary"),
+        compiler_params=params("arbitrary", limit=LESS_VMEM),
         cost_estimate=pl.CostEstimate(
             flops=2 * rows * STATE * LANES, bytes_accessed=6 * rows * LANES, transcendentals=rows * LANES
         ),

time: 126 us -> 123 us (0.976)
  Pallas kernels: 58.7 us -> 54.1 us
  local copies, waits for them, and re-layouts: 6.54 us -> 8.58 us
    pallas_call x2, Pallas kernels: 16.5 us -> 11.8 us  [gated_norm(): pl.pallas_call(functools.partial(norm_kernel, devices), grid_spec=pltpu.P...]
    unnamed x10 -> x32, local copies, waits for them, and re-layouts: 4.68 us -> 6.72 us
  transfers between devices with their start and end apart: 12 -> 12, of which waited for: 3 -> 3; matrix products, arithmetic and copies ran while one was open for 2% -> 2% of each run, Pallas kernels for 33% -> 32%
where the time goes in v4:
time: 123 us
  Pallas kernels  54.1 us (44%)
  starting transfers between devices  23.5 us (19%)
  blocking collectives  20.1 us (16%)
  waiting for transfers between devices  9.31 us (8%)
  local copies, waits for them, and re-layouts  8.58 us (7%)
  other arithmetic  4.5 us (4%)
  between operations  2.79 us (2%)
    ppermute x12, starting transfers between devices, over(): lax.ppermute(value, 'seq', [(i, move(i)) for i in range(count) if move(i)...  23.5 us
    pallas_call x2, Pallas kernels, local_values(): pl.pallas_call(values_kernel, grid_spec=pltpu.PrefetchScalarGridSpec(num_...  20.9 us
    all_to_all x1, blocking collectives, per_device(): terms = lax.all_to_all(terms, ('seq', 'head'), 0, 0)  20.1 us
    pallas_call x2, Pallas kernels, local_states(): pl.pallas_call(state_kernel, grid_spec=pltpu.PrefetchScalarGridSpec(num_s...  18.5 us
    pallas_call x2, Pallas kernels, gated_norm(): pl.pallas_call(functools.partial(norm_kernel, devices), grid_spec=pltpu.P...  11.8 us
    ppermute x12, waiting for transfers between devices, over(): lax.ppermute(value, 'seq', [(i, move(i)) for i in range(count) if move(i)...  9.31 us
    unnamed x32, local copies, waits for them, and re-layouts  6.72 us
    pallas_call x1, Pallas kernels, decays(): pl.pallas_call(decay_kernel, out_shape=[jax.ShapeDtypeStruct((heads, rows...  2.88 us
  transfers between devices with their start and end apart: 12, of which 3 were waited for; matrix products, arithmetic and copies ran while one was open for 2% of the time, Pallas kernels for 32%

profile of v4, /device:TPU:1, one launch (start us, length us, event | category | flops | bytes accessed | tf_op | source)
XLA Modules:
  0.0 122.9 jit_solution(4237359775199399139)
XLA Ops:
  0.6 0.8 slice.186
  1.4 0.9 slice.185
  2.4 4.6 %collective-permute-start = (bf16[16,5120]{1,0:T(8,128)(2,1)S(1)}, bf16[16,5120]{1,0:T(8,128)(2,1)S(1)}, u32[]{:S(2)}, u32[]{:S(2)}) collective-permute-start(bf16[16,5120]{1,0:T(8,128)(2,1)S(1)} %pad_maximum_fusion.5), channel_id=1, source_target_pairs={{0,4},{4,8},{8,12},{12,16},{16,20},{20,24},{24,28},{28,32},{32,36}... | collective-permute-start | bytes 491528 | tf_op jit(solution)/shard_map/ppermute | solution.py:458
  7.0 3.0 %copy.19 = bf16[96,8,2,512]{3,1,2,0:T(8,128)(2,1)} copy(bf16[96,8,2,512]{3,2,1,0:T(2,128)(2,1)} %bitcast.117) | data formatting | bytes 3145728
  10.0 2.9 %shard_map.149 = (f32[64,768]{1,0:T(8,128)}, f32[64,768]{1,0:T(8,128)}, bf16[768,128]{1,0:T(8,128)(2,1)}, bf16[768,128]{1,0:T(8,128)(2,1)}, bf16[768,128]{1,0:T(...) custom-call(f32[64,768]{1,0:T(8,128)} %bitcast.140, f32[1,64]{1,0:T(1,128)} %bitcast.141, f32[1,64]{1,0:T(1,128)} %bitcast.142), custom_call_target="tpu_custom_call" | custom-call | flops 100000000 | bytes 2000000 | tf_op jit(solution)/shard_map/pallas_call | solution.py:118
  12.9 0.7 copy-done.10
  13.5 9.2 %shard_map.150 = (bf16[768,256]{1,0:T(8,128)(2,1)}, bf16[768,256]{1,0:T(8,128)(2,1)}, bf16[768,2048]{1,0:T(8,128)(2,1)}, bf16[272,2048]{1,0:T(8,128)(2,1)}) custom-call(s32[1]{0:T(128)} %bitcast.core_ref.place_ref, bf16[768,4096]{1,0:T(8,128)(2,1)} %x_ref.3, bf16[16,5120]{1,0:T(8,128)(2,1)} %copy-done.10, f32[4,4096]{1,0:T(4,128)} %wx_ref.3, ...), custom_call_target="tpu_custom_call" | custom-call | flops 805306368 | bytes 6291456 | tf_op jit(solution)/shard_map/pallas_call | solution.py:217
  23.0 9.3 %shard_map.151 = (bf16[768,256]{1,0:T(8,128)(2,1)}, bf16[768,256]{1,0:T(8,128)(2,1)}, bf16[768,2048]{1,0:T(8,128)(2,1)}, bf16[272,2048]{1,0:T(8,128)(2,1)}) custom-call(s32[1]{0:T(128)} %bitcast.core_ref.place_ref, bf16[768,4096]{1,0:T(8,128)(2,1)} %x_ref.3, bf16[16,5120]{1,0:T(8,128)(2,1)} %copy-done.10, f32[4,4096]{1,0:T(4,128)} %wx_ref.3, ...), custom_call_target="tpu_custom_call" | custom-call | flops 805306368 | bytes 6291456 | tf_op jit(solution)/shard_map/pallas_call | solution.py:217
  32.3 1.4 %broadcast_select_fusion.1 = (bf16[272,2048]{1,0:T(8,128)(2,1)S(1)}, bf16[272,2048]{1,0:T(8,128)(2,1)S(1)}) fusion(bf16[272,2048]{1,0:T(8,128)(2,1)} %get-tuple-element.28, bf16[272,2048]{1,0:T(8,128)(2,1)S(1)} %collective-permute-done.1, pred[]{:T(512)S(6)} %eq.25), kind=kLoop, calls=%fused_computation.13 | loop fusion | flops 1114112 | bytes 4456449 | tf_op jit(solution)/shard_map/jit(_where)/select_n | solution.py:470
  33.8 0.4 fusion.1
  34.4 1.4 %collective-permute-start.2 = (bf16[272,512]{1,0:T(8,128)(2,1)S(1)}, bf16[272,512]{1,0:T(8,128)(2,1)S(1)}, u32[]{:S(2)}, u32[]{:S(2)}) collective-permute-start(bf16[272,512]{1,0:T(8,128)(2,1)S(1)} %get-tuple-element.70), channel_id=1, source_target_pairs={{0,8},{4,12},{8,16},{12,20},{16,24},{20,28},{24,0},{28,4},{32,40},... | collective-permute-start | bytes 835592 | tf_op jit(solution)/shard_map/ppermute | solution.py:458
  35.7 2.2 %collective-permute-start.3 = (bf16[272,512]{1,0:T(8,128)(2,1)S(1)}, bf16[272,512]{1,0:T(8,128)(2,1)S(1)}, u32[]{:S(2)}, u32[]{:S(2)}) collective-permute-start(bf16[272,512]{1,0:T(8,128)(2,1)S(1)} %get-tuple-element.71), channel_id=1, source_target_pairs={{0,16},{4,20},{8,24},{12,28},{16,0},{20,4},{24,8},{28,12},{32,48},... | collective-permute-start | bytes 835592 | tf_op jit(solution)/shard_map/ppermute | solution.py:458
  37.9 1.2 collective-permute-start.4
  39.1 10.4 %shard_map.152 = (bf16[768,2048]{1,0:T(8,128)(2,1)}, s32[1]{0:T(128)}) custom-call(s32[1]{0:T(128)} %bitcast.core_ref.place_ref, bf16[768,2048]{1,0:T(8,128)(2,1)} %get-tuple-element.30.x_ref, bf16[768,256]{1,0:T(8,128)(2,1)} %get-tuple-element.31.b_ref, bf16[768,256]{1,0:T(8,128)(2,1)} %get-tuple-element.32.c_ref, f32[64,768]{1,0:T(8,128)} %get-tuple-element.33.run_ref, ...), custom_call_target="tpu_custom_call" | custom-call | flops 3221225472 | bytes 12582912 | tf_op jit(solution)/shard_map/pallas_call | solution.py:325
  50.9 4.7 %collective-permute-start.6 = (bf16[272,512]{1,0:T(8,128)(2,1)S(1)}, bf16[272,512]{1,0:T(8,128)(2,1)S(1)}, u32[]{:S(2)}, u32[]{:S(2)}) collective-permute-start(bf16[272,512]{1,0:T(8,128)(2,1)S(1)} %pad_maximum_fusion.4), channel_id=1, source_target_pairs={{0,64},{4,68},{8,72},{12,76},{16,80},{20,84},{24,88},{28,92},{32,9... | collective-permute-start | bytes 835592 | tf_op jit(solution)/shard_map/ppermute | solution.py:458
  55.6 1.3 %collective-permute-start.7 = (bf16[272,512]{1,0:T(8,128)(2,1)S(1)}, bf16[272,512]{1,0:T(8,128)(2,1)S(1)}, u32[]{:S(2)}, u32[]{:S(2)}) collective-permute-start(bf16[272,512]{1,0:T(8,128)(2,1)S(1)} %pad_maximum_fusion.4), channel_id=1, source_target_pairs={{0,96},{4,100},{8,104},{12,108},{16,112},{20,116},{24,120},{28,124... | collective-permute-start | bytes 835592 | tf_op jit(solution)/shard_map/ppermute | solution.py:458
  57.0 1.6 %collective-permute-start.5 = (bf16[272,512]{1,0:T(8,128)(2,1)S(1)}, bf16[272,512]{1,0:T(8,128)(2,1)S(1)}, u32[]{:S(2)}, u32[]{:S(2)}) collective-permute-start(bf16[272,512]{1,0:T(8,128)(2,1)S(1)} %pad_maximum_fusion.4), channel_id=1, source_target_pairs={{0,32},{4,36},{8,40},{12,44},{16,48},{20,52},{24,56},{28,60},{32,6... | collective-permute-start | bytes 835592 | tf_op jit(solution)/shard_map/ppermute | solution.py:458
  58.6 1.7 %collective-permute-done.6 = bf16[272,512]{1,0:T(8,128)(2,1)S(1)} collective-permute-done((bf16[272,512]{1,0:T(8,128)(2,1)S(1)}, bf16[272,512]{1,0:T(8,128)(2,1)S(1)}, u32[]{:S(2)}, u32[]{:S(2)}) %collective-permute-start.6) | collective-permute-done | bytes 278560 | tf_op jit(solution)/shard_map/ppermute | solution.py:458
  60.3 6.0 %collective-permute-done.5 = bf16[272,512]{1,0:T(8,128)(2,1)S(1)} collective-permute-done((bf16[272,512]{1,0:T(8,128)(2,1)S(1)}, bf16[272,512]{1,0:T(8,128)(2,1)S(1)}, u32[]{:S(2)}, u32[]{:S(2)}) %collective-permute-start.5) | collective-permute-done | bytes 278560 | tf_op jit(solution)/shard_map/ppermute | solution.py:458
  66.3 1.6 %collective-permute-done.7 = bf16[272,512]{1,0:T(8,128)(2,1)S(1)} collective-permute-done((bf16[272,512]{1,0:T(8,128)(2,1)S(1)}, bf16[272,512]{1,0:T(8,128)(2,1)S(1)}, u32[]{:S(2)}, u32[]{:S(2)}) %collective-permute-start.7) | collective-permute-done | bytes 278560 | tf_op jit(solution)/shard_map/ppermute | solution.py:458
  68.0 0.3 convert_bitcast_fusion
  68.6 2.4 %collective-permute-start.9 = (bf16[256,512]{1,0:T(8,128)(2,1)S(1)}, bf16[256,512]{1,0:T(8,128)(2,1)S(1)}, u32[]{:S(2)}, u32[]{:S(2)}) collective-permute-start(bf16[256,512]{1,0:T(8,128)(2,1)S(1)} %get-tuple-element.79), channel_id=1, source_target_pairs={{0,16},{4,20},{8,24},{12,28},{16,0},{20,4},{24,8},{28,12},{32,48},... | collective-permute-start | bytes 786440 | tf_op jit(solution)/shard_map/ppermute | solution.py:458
  71.0 1.3 %collective-permute-start.8 = (bf16[256,512]{1,0:T(8,128)(2,1)S(1)}, bf16[256,512]{1,0:T(8,128)(2,1)S(1)}, u32[]{:S(2)}, u32[]{:S(2)}) collective-permute-start(bf16[256,512]{1,0:T(8,128)(2,1)S(1)} %get-tuple-element.80), channel_id=1, source_target_pairs={{0,8},{4,12},{8,16},{12,20},{16,24},{20,28},{24,0},{28,4},{32,40},... | collective-permute-start | bytes 786440 | tf_op jit(solution)/shard_map/ppermute | solution.py:458
  72.2 1.4 %collective-permute-start.10 = (bf16[256,512]{1,0:T(8,128)(2,1)S(1)}, bf16[256,512]{1,0:T(8,128)(2,1)S(1)}, u32[]{:S(2)}, u32[]{:S(2)}) collective-permute-start(bf16[256,512]{1,0:T(8,128)(2,1)S(1)} %get-tuple-element.78.sent_ref), channel_id=1, source_target_pairs={{0,24},{4,28},{8,0},{12,4},{16,8},{20,12},{24,16},{28,20},{32,56},... | collective-permute-start | bytes 786440 | tf_op jit(solution)/shard_map/ppermute | solution.py:458
  73.6 10.5 %shard_map.153 = (bf16[768,2048]{1,0:T(8,128)(2,1)}, s32[1]{0:T(128)}) custom-call(s32[1]{0:T(128)} %bitcast.core_ref.place_ref, bf16[768,2048]{1,0:T(8,128)(2,1)} %get-tuple-element.38.x_ref, bf16[768,256]{1,0:T(8,128)(2,1)} %get-tuple-element.39.b_ref, bf16[768,256]{1,0:T(8,128)(2,1)} %get-tuple-element.27.c_ref, f32[64,768]{1,0:T(8,128)} %get-tuple-element.33.run_ref, ...), custom_call_target="tpu_custom_call" | custom-call | flops 3221225472 | bytes 12582912 | tf_op jit(solution)/shard_map/pallas_call | solution.py:325
  85.3 0.6 fusion.3
  85.8 1.5 %collective-permute-start.11 = (bf16[256,2048]{1,0:T(8,128)(2,1)S(1)}, bf16[256,2048]{1,0:T(8,128)(2,1)S(1)}, u32[]{:S(2)}, u32[]{:S(2)}) collective-permute-start(bf16[256,2048]{1,0:T(8,128)(2,1)S(1)} %get-tuple-element.61), channel_id=1, source_target_pairs={{0,4},{4,0},{8,12},{12,8},{16,20},{20,16},{24,28},{28,24},{32,36},... | collective-permute-start | bytes 3145736 | tf_op jit(solution)/shard_map/ppermute | solution.py:458
  87.5 2.8 %copy-done = bf16[768,4096]{1,0:T(8,128)(2,1)S(1)} copy-done((bf16[768,4096]{1,0:T(8,128)(2,1)S(1)}, bf16[768,4096]{1,0:T(8,128)(2,1)}, u32[]{:S(2)}) %copy-start) | copy-done | bytes 6291480
  90.3 5.7 %shard_map.154 = (bf16[768,4096]{1,0:T(8,128)(2,1)}, f32[768,128]{1,0:T(8,128)S(1)}) custom-call(s32[1]{0:T(128)} %bitcast.core_ref.place_ref, bf16[768,256]{1,0:T(8,128)(2,1)S(1)} %copy-done.5, bf16[256,2048]{1,0:T(8,128)(2,1)S(1)} %get-tuple-element.60.state_ref, bf16[768,2048]{1,0:T(8,128)(2,1)S(1)} %copy-done.3, bf16[768,4096]{1,0:T(8,128)(2,1)S(1)} %copy-done, ...), custom_call_target="tpu_custom_call" | custom-call | flops 805306368 | bytes 9437184 | tf_op jit(solution)/shard_map/pallas_call | solution.py:409
  96.1 6.1 %shard_map.155 = (bf16[768,4096]{1,0:T(8,128)(2,1)}, f32[128,64]{1,0:T(8,128)S(1)}) custom-call(s32[1]{0:T(128)} %bitcast.core_ref.place_ref, bf16[768,256]{1,0:T(8,128)(2,1)S(1)} %copy-done.6, bf16[256,2048]{1,0:T(8,128)(2,1)S(1)} %collective-permute-done.11.state_ref, bf16[768,2048]{1,0:T(8,128)(2,1)S(1)} %copy-done.2, ...), custom_call_target="tpu_custom_call", output_to_operand_aliasing={{0}: (11, {})} | custom-call | flops 805306368 | bytes 9437184 | tf_op jit(solution)/shard_map/pallas_call | solution.py:409
  102.2 20.1 %all_to_all.9 = f32[128,1,64]{2,1,0:T(1,128)S(1)} all-to-all(f32[128,1,64]{2,1,0:T(1,128)S(1)} %bitcast.110), channel_id=1, replica_groups=mesh['seq'=32,'head'=4] {'seq','head'}, dimensions={0} | all-to-all | bytes 65536 | tf_op jit(solution)/shard_map/all_to_all | solution.py:552
  122.3 0.7 reduce_sum.9
  (66 shorter events, 1.7 us)
Async XLA Ops:
  2.4 10.5 %collective-permute-start = (bf16[16,5120]{1,0:T(8,128)(2,1)S(1)}, bf16[16,5120]{1,0:T(8,128)(2,1)S(1)}, u32[]{:S(2)}, u32[]{:S(2)}) collective-permute-start(bf16[16,5120]{1,0:T(8,128)(2,1)S(1)} %pad_maximum_fusion.5), channel_id=1, source_target_pairs={{0,4},{4,8},{8,12},{12,16},{16,20},{20,24},{24,28},{28,32},{32,36}... | collective-permute-start | bytes 491528 | tf_op jit(solution)/shard_map/ppermute | solution.py:458
  12.9 0.7 copy-start.10
  22.8 9.5 %collective-permute-start.1 = (bf16[272,2048]{1,0:T(8,128)(2,1)}, bf16[272,2048]{1,0:T(8,128)(2,1)S(1)}, u32[]{:S(2)}, u32[]{:S(2)}) collective-permute-start(bf16[272,2048]{1,0:T(8,128)(2,1)} %get-tuple-element.29), channel_id=1, source_target_pairs={{0,4},{4,0},{8,12},{12,8},{16,20},{20,16},{24,28},{28,24},{32,36},... | collective-permute-start | bytes 3342344 | tf_op jit(solution)/shard_map/ppermute | solution.py:458
  34.4 4.8 %copy-start.11 = (bf16[272,512]{1,0:T(8,128)(2,1)}, bf16[272,512]{1,0:T(8,128)(2,1)S(1)}, u32[]{:S(2)}) copy-start(bf16[272,512]{1,0:T(8,128)(2,1)S(1)} %get-tuple-element.72.sent_ref) | copy-start | bytes 835588
  34.4 16.0 %collective-permute-start.2 = (bf16[272,512]{1,0:T(8,128)(2,1)S(1)}, bf16[272,512]{1,0:T(8,128)(2,1)S(1)}, u32[]{:S(2)}, u32[]{:S(2)}) collective-permute-start(bf16[272,512]{1,0:T(8,128)(2,1)S(1)} %get-tuple-element.70), channel_id=1, source_target_pairs={{0,8},{4,12},{8,16},{12,20},{16,24},{20,28},{24,0},{28,4},{32,40},... | collective-permute-start | bytes 835592 | tf_op jit(solution)/shard_map/ppermute | solution.py:458
  35.7 14.6 %collective-permute-start.3 = (bf16[272,512]{1,0:T(8,128)(2,1)S(1)}, bf16[272,512]{1,0:T(8,128)(2,1)S(1)}, u32[]{:S(2)}, u32[]{:S(2)}) collective-permute-start(bf16[272,512]{1,0:T(8,128)(2,1)S(1)} %get-tuple-element.71), channel_id=1, source_target_pairs={{0,16},{4,20},{8,24},{12,28},{16,0},{20,4},{24,8},{28,12},{32,48},... | collective-permute-start | bytes 835592 | tf_op jit(solution)/shard_map/ppermute | solution.py:458
  37.9 12.4 %collective-permute-start.4 = (bf16[272,512]{1,0:T(8,128)(2,1)S(1)}, bf16[272,512]{1,0:T(8,128)(2,1)S(1)}, u32[]{:S(2)}, u32[]{:S(2)}) collective-permute-start(bf16[272,512]{1,0:T(8,128)(2,1)S(1)} %get-tuple-element.72.sent_ref), channel_id=1, source_target_pairs={{0,24},{4,28},{8,0},{12,4},{16,8},{20,12},{24,16},{28,20},{32,56},... | collective-permute-start | bytes 835592 | tf_op jit(solution)/shard_map/ppermute | solution.py:458
  50.9 9.4 %collective-permute-start.6 = (bf16[272,512]{1,0:T(8,128)(2,1)S(1)}, bf16[272,512]{1,0:T(8,128)(2,1)S(1)}, u32[]{:S(2)}, u32[]{:S(2)}) collective-permute-start(bf16[272,512]{1,0:T(8,128)(2,1)S(1)} %pad_maximum_fusion.4), channel_id=1, source_target_pairs={{0,64},{4,68},{8,72},{12,76},{16,80},{20,84},{24,88},{28,92},{32,9... | collective-permute-start | bytes 835592 | tf_op jit(solution)/shard_map/ppermute | solution.py:458
  55.6 12.3 %collective-permute-start.7 = (bf16[272,512]{1,0:T(8,128)(2,1)S(1)}, bf16[272,512]{1,0:T(8,128)(2,1)S(1)}, u32[]{:S(2)}, u32[]{:S(2)}) collective-permute-start(bf16[272,512]{1,0:T(8,128)(2,1)S(1)} %pad_maximum_fusion.4), channel_id=1, source_target_pairs={{0,96},{4,100},{8,104},{12,108},{16,112},{20,116},{24,120},{28,124... | collective-permute-start | bytes 835592 | tf_op jit(solution)/shard_map/ppermute | solution.py:458
  57.0 9.3 %collective-permute-start.5 = (bf16[272,512]{1,0:T(8,128)(2,1)S(1)}, bf16[272,512]{1,0:T(8,128)(2,1)S(1)}, u32[]{:S(2)}, u32[]{:S(2)}) collective-permute-start(bf16[272,512]{1,0:T(8,128)(2,1)S(1)} %pad_maximum_fusion.4), channel_id=1, source_target_pairs={{0,32},{4,36},{8,40},{12,44},{16,48},{20,52},{24,56},{28,60},{32,6... | collective-permute-start | bytes 835592 | tf_op jit(solution)/shard_map/ppermute | solution.py:458
  68.6 5.0 %copy-start.12 = (bf16[256,512]{1,0:T(8,128)(2,1)}, bf16[256,512]{1,0:T(8,128)(2,1)S(1)}, u32[]{:S(2)}) copy-start(bf16[256,512]{1,0:T(8,128)(2,1)S(1)} %get-tuple-element.78.sent_ref) | copy-start | bytes 786436
  68.6 16.3 %collective-permute-start.9 = (bf16[256,512]{1,0:T(8,128)(2,1)S(1)}, bf16[256,512]{1,0:T(8,128)(2,1)S(1)}, u32[]{:S(2)}, u32[]{:S(2)}) collective-permute-start(bf16[256,512]{1,0:T(8,128)(2,1)S(1)} %get-tuple-element.79), channel_id=1, source_target_pairs={{0,16},{4,20},{8,24},{12,28},{16,0},{20,4},{24,8},{28,12},{32,48},... | collective-permute-start | bytes 786440 | tf_op jit(solution)/shard_map/ppermute | solution.py:458
  71.0 14.0 %collective-permute-start.8 = (bf16[256,512]{1,0:T(8,128)(2,1)S(1)}, bf16[256,512]{1,0:T(8,128)(2,1)S(1)}, u32[]{:S(2)}, u32[]{:S(2)}) collective-permute-start(bf16[256,512]{1,0:T(8,128)(2,1)S(1)} %get-tuple-element.80), channel_id=1, source_target_pairs={{0,8},{4,12},{8,16},{12,20},{16,24},{20,28},{24,0},{28,4},{32,40},... | collective-permute-start | bytes 786440 | tf_op jit(solution)/shard_map/ppermute | solution.py:458
  72.2 12.7 %collective-permute-start.10 = (bf16[256,512]{1,0:T(8,128)(2,1)S(1)}, bf16[256,512]{1,0:T(8,128)(2,1)S(1)}, u32[]{:S(2)}, u32[]{:S(2)}) collective-permute-start(bf16[256,512]{1,0:T(8,128)(2,1)S(1)} %get-tuple-element.78.sent_ref), channel_id=1, source_target_pairs={{0,24},{4,28},{8,0},{12,4},{16,8},{20,12},{24,16},{28,20},{32,56},... | collective-permute-start | bytes 786440 | tf_op jit(solution)/shard_map/ppermute | solution.py:458
  73.6 13.7 %copy-start.4 = (bf16[768,128]{1,0:T(8,128)(2,1)S(1)}, bf16[768,128]{1,0:T(8,128)(2,1)}, u32[]{:S(2)}) copy-start(bf16[768,128]{1,0:T(8,128)(2,1)} %get-tuple-element.42.eabs_ref) | copy-start | bytes 589828
  73.6 13.7 %copy-start.5 = (bf16[768,256]{1,0:T(8,128)(2,1)S(1)}, bf16[768,256]{1,0:T(8,128)(2,1)}, u32[]{:S(2)}) copy-start(bf16[768,256]{1,0:T(8,128)(2,1)} %get-tuple-element.32.c_ref) | copy-start | bytes 1179652
  85.0 11.1 %slice-start = ((s8[6291456]{0:T(1024)(128)(4,1)}), s8[4194304]{0:T(1024)(128)(4,1)S(1)}, s32[]{:S(2)}) async-start(s8[6291456]{0:T(1024)(128)(4,1)} %bitcast.104), calls=%async_computation.1 | async-start | bytes 8388608
  85.1 2.2 %copy-start.8 = (f32[4096]{0:T(1024)S(1)}, f32[4096]{0:T(1024)}, u32[]{:S(2)}) copy-start(f32[4096]{0:T(1024)} %param.25) | copy-start | bytes 49156
  85.2 2.1 %copy-start.1 = (bf16[2,128,2048]{2,1,0:T(8,128)(2,1)S(1)}, bf16[2,128,2048]{2,1,0:T(8,128)(2,1)}, u32[]{:S(2)}) copy-start(bf16[2,128,2048]{2,1,0:T(8,128)(2,1)} %constant.154.clone.spread_ref) | copy-start | bytes 3145732
  85.2 2.3 %copy-start.3 = (bf16[768,2048]{1,0:T(8,128)(2,1)S(1)}, bf16[768,2048]{1,0:T(8,128)(2,1)}, u32[]{:S(2)}) copy-start(bf16[768,2048]{1,0:T(8,128)(2,1)} %get-tuple-element.43.values_ref) | copy-start | bytes 9437188
  85.2 2.3 %copy-start.7 = (f32[4096]{0:T(1024)S(1)}, f32[4096]{0:T(1024)}, u32[]{:S(2)}) copy-start(f32[4096]{0:T(1024)} %param.24) | copy-start | bytes 49156
  85.3 2.2 %copy-start.9 = (s32[64]{0:T(128)S(1)}, s32[64]{0:T(128)}, u32[]{:S(2)}) copy-start(s32[64]{0:T(128)} %param.26) | copy-start | bytes 772
  85.8 10.2 %collective-permute-start.11 = (bf16[256,2048]{1,0:T(8,128)(2,1)S(1)}, bf16[256,2048]{1,0:T(8,128)(2,1)S(1)}, u32[]{:S(2)}, u32[]{:S(2)}) collective-permute-start(bf16[256,2048]{1,0:T(8,128)(2,1)S(1)} %get-tuple-element.61), channel_id=1, source_target_pairs={{0,4},{4,0},{8,12},{12,8},{16,20},{20,16},{24,28},{28,24},{32,36},... | collective-permute-start | bytes 3145736 | tf_op jit(solution)/shard_map/ppermute | solution.py:458
  87.5 2.8 %copy-start = (bf16[768,4096]{1,0:T(8,128)(2,1)S(1)}, bf16[768,4096]{1,0:T(8,128)(2,1)}, u32[]{:S(2)}) copy-start(bf16[768,4096]{1,0:T(8,128)(2,1)} %z_ref.3) | copy-start | bytes 18874372
  90.3 5.7 %slice-start.1 = ((s8[6291456]{0:T(1024)(128)(4,1)}), s8[2097152]{0:T(1024)(128)(4,1)S(1)}, s32[]{:S(2)}) async-start(s8[6291456]{0:T(1024)(128)(4,1)} %bitcast.104), calls=%async_computation.2 | async-start | bytes 4194304
  90.3 5.7 %copy-start.2 = (bf16[768,2048]{1,0:T(8,128)(2,1)S(1)}, bf16[768,2048]{1,0:T(8,128)(2,1)}, u32[]{:S(2)}) copy-start(bf16[768,2048]{1,0:T(8,128)(2,1)} %get-tuple-element.41.values_ref) | copy-start | bytes 9437188
  90.3 5.7 %copy-start.6 = (bf16[768,256]{1,0:T(8,128)(2,1)S(1)}, bf16[768,256]{1,0:T(8,128)(2,1)}, u32[]{:S(2)}) copy-start(bf16[768,256]{1,0:T(8,128)(2,1)} %get-tuple-element.27.c_ref) | copy-start | bytes 1179652

commit v5 on v4

--- a/solution.py
+++ b/solution.py
@@ -143,6 +143,16 @@
     return silu_of_twice(total).astype(BF16)
 
 
+def conv_state(pad, src, tail, taps_ref, offset_ref, n, dst):
+    for lane in range(0, STATE, 128):
+        own = slice(lane, lane + 128)
+        load_column(pad, src.at[:, own], tail.at[:, own])
+        taps = [0.5 * taps_ref[k, n : n + 1, own] for k in range(4)]
+        offset = 0.5 * offset_ref[n : n + 1, own]
+        for start in range(0, src.shape[0], CHUNK):
+            dst[start : start + CHUNK, own] = conv_rows(pad, start, taps, offset)
+
+
 def state_kernel(core_ref, x_ref, xt_ref, wx_ref, ox_ref, wabs_ref, spread_ref, tot_ref, *rest):
     rows = x_ref.shape[0]
     cx_ref, state_ref, pad, scaled, bturn = rest[-5:]
@@ -154,18 +164,11 @@
             bturn[...] = made_ref[...].T
 
     else:
-        b_ref, bt_ref, c_ref, ct_ref, wb_ref, ob_ref, cb_ref, cc_ref = rest[:8]
+        b_ref, bt_ref, wb_ref, ob_ref, cb_ref = rest[:5]
 
         @pl.when(pl.program_id(0) == 0)
         def _():
-            for n, (src, tail, dst) in enumerate(((b_ref, bt_ref, cb_ref), (c_ref, ct_ref, cc_ref))):
-                for lane in range(0, STATE, 128):
-                    own = slice(lane, lane + 128)
-                    load_column(pad.at[0], src.at[:, own], tail.at[:, own])
-                    taps = [0.5 * wb_ref[k, n : n + 1, own] for k in range(4)]
-                    offset = 0.5 * ob_ref[n : n + 1, own]
-                    for start in range(0, rows, CHUNK):
-                        dst[start : start + CHUNK, own] = conv_rows(pad.at[0], start, taps, offset)
+            conv_state(pad.at[0], b_ref, bt_ref, wb_ref, ob_ref, 0, cb_ref)
             bturn[...] = cb_ref[...].T
 
     for lane in range(0, TILE, 256):
@@ -204,16 +207,14 @@
         ends = [
             pl.BlockSpec((rows, STATE), own(0)),
             pl.BlockSpec((TAIL, STATE), own(first)),
-            pl.BlockSpec((rows, STATE), own(groups)),
-            pl.BlockSpec((TAIL, STATE), own(first + groups)),
             pl.BlockSpec((4, 2, STATE), lambda j, core: (0, 0, group_of(turn, core))),
             pl.BlockSpec((2, STATE), own(0)),
         ]
-        last = (bc, tails, bc, tails, wbc, obc)
+        last = (bc, tails, wbc, obc)
     else:
         ends = [pl.BlockSpec((rows, STATE), still)]
         last = (made,)
-    fresh = 2 if made is None else 0
+    fresh = 1 if made is None else 0
     return pl.pallas_call(
         state_kernel,
         grid_spec=pltpu.PrefetchScalarGridSpec(
@@ -250,7 +251,8 @@
 
 
 def values_kernel(
-    core_ref, x_ref, b_ref, c_ref, run_ref, row_ref, ehl_ref, whl_ref, spread_ref, sent_ref, out_ref, done_ref, near, inside, across
+    core_ref, x_ref, b_ref, ci_ref, ct_ref, wb_ref, ob_ref, run_ref, row_ref, ehl_ref, whl_ref, spread_ref, sent_ref,
+    out_ref, c_ref, done_ref, pad, near, inside, across,
 ):
     done_ref[0] = 0
     rows = x_ref.shape[0]
@@ -261,6 +263,7 @@
 
     @pl.when(pl.program_id(0) == 0)
     def _():
+        conv_state(pad, ci_ref, ct_ref, wb_ref, ob_ref, 1, c_ref)
         t = lax.broadcasted_iota(jnp.int32, (CHUNK, CHUNK), 0)
         s = lax.broadcasted_iota(jnp.int32, (CHUNK, CHUNK), 1)
         for n in range(2 * blocks):
@@ -314,8 +317,11 @@
                     out_ref[part(m), low : low + 128] = total.astype(out_ref.dtype)
 
 
-def local_values(turn, half, core, x, b, c, run, row, ehl, whl, spread, sent):
+def local_values(turn, half, core, x, b, bc, tails, wbc, obc, run, row, ehl, whl, spread, sent):
     rows, width = x.shape
+    groups = bc.shape[1] // (2 * STATE)
+    first = tails.shape[1] // STATE - groups
+    own = lambda shift: lambda j, core: (0, shift + group_of(turn, core))
     blocks = rows // BLOCK
     tiles = width // VTILE
     heads = VTILE // HEAD_DIM
@@ -330,7 +336,10 @@
             in_specs=[
                 pl.BlockSpec((rows, VTILE), lane),
                 pl.BlockSpec((rows, STATE), still),
-                pl.BlockSpec((rows, STATE), still),
+                pl.BlockSpec((rows, STATE), own(groups)),
+                pl.BlockSpec((TAIL, STATE), own(first)),
+                pl.BlockSpec((4, 2, STATE), lambda j, core: (0, 0, group_of(turn, core))),
+                pl.BlockSpec((2, STATE), own(0)),
                 pl.BlockSpec((heads, rows), head),
                 pl.BlockSpec((heads, rows), head),
                 pl.BlockSpec(ehl.shape, still),
@@ -338,19 +347,28 @@
                 pl.BlockSpec((1, spread.shape[1], VTILE), lambda j, core: (group_of(turn, core), 0, half * tiles + j)),
                 pl.BlockSpec(memory_space=pl.ANY),
             ],
-            out_specs=[pl.BlockSpec((rows, VTILE), lane), pl.BlockSpec(memory_space=pltpu.SMEM)],
+            out_specs=[
+                pl.BlockSpec((rows, VTILE), lane),
+                pl.BlockSpec((rows, STATE), still),
+                pl.BlockSpec(memory_space=pltpu.SMEM),
+            ],
             scratch_shapes=[
+                pltpu.VMEM((rows + 8, 128), F32),
                 pltpu.VMEM((2 * blocks, CHUNK, CHUNK), F32),
                 pltpu.VMEM((blocks, CHUNK, CHUNK), BF16),
                 pltpu.VMEM((blocks * (blocks - 1) // 2, BLOCK, BLOCK), BF16),
             ],
         ),
-        out_shape=[jax.ShapeDtypeStruct((rows, width), BF16), jax.ShapeDtypeStruct((1,), jnp.int32)],
+        out_shape=[
+            jax.ShapeDtypeStruct((rows, width), BF16),
+            jax.ShapeDtypeStruct((rows, STATE), BF16),
+            jax.ShapeDtypeStruct((1,), jnp.int32),
+        ],
         compiler_params=params("arbitrary"),
         cost_estimate=pl.CostEstimate(
             flops=8 * rows * STATE * width, bytes_accessed=8 * rows * width, transcendentals=rows * CHUNK * width // HEAD_DIM
         ),
-    )(core, x, b, c, run, row, ehl, whl, spread, sent)
+    )(core, x, b, bc, tails, wbc, obc, run, row, ehl, whl, spread, sent)
 
 
 def norm_kernel(
@@ -527,12 +545,12 @@
                     made[turn][0][0] if half else None,
                 )
             )
-    values = [None, None]
+    values, outward = [None, None], [None, None]
 
     def inner(turn, sent):
-        m = made[turn]
-        values[turn], done = local_values(
-            turn, 0, core, m[0][-2], m[0][0], m[0][1], run, row, ehl, whl, spread, sent
+        m = made[turn][0]
+        values[turn], outward[turn], done = local_values(
+            turn, 0, core, m[-2], m[0], bc, tails, conv_bc_weight, conv_bc_bias, run, row, ehl, whl, spread, sent
         )
         return done[0]
 
@@ -543,10 +561,10 @@
     gain, reward, ends = norm_gain[None], reward_w[None], step_ends[None]
     devices = lax.axis_size("seq") * lax.axis_size("head")
     normed, terms = gated_norm(
-        1, core, values[1], made[1][0][1], entered[1], eabs, spread, z_in, gain, reward, ends
+        1, core, values[1], outward[1], entered[1], eabs, spread, z_in, gain, reward, ends
     )
     normed, terms = gated_norm(
-        0, core, values[0], made[0][0][1], entered[0], eabs, spread, z_in, gain, reward, ends,
+        0, core, values[0], outward[0], entered[0], eabs, spread, z_in, gain, reward, ends,
         (terms, normed), devices,
     )
     terms = lax.all_to_all(terms, ("seq", "head"), 0, 0)

time: 123 us -> 122 us (level)
    pallas_call x2, Pallas kernels: 18.5 us -> 17.1 us  [local_states(): pl.pallas_call(state_kernel, grid_spec=pltpu.PrefetchScalarGridSpec(num_s...]
  transfers between devices with their start and end apart: 12 -> 12, of which waited for: 3 -> 3; matrix products, arithmetic and copies ran while one was open for 2% -> 3% of each run, Pallas kernels for 32% -> 32%
where the time goes in v5:
time: 122 us; the launch traced here: 121 us
  Pallas kernels  53.9 us (44%)
  starting transfers between devices  22.8 us (19%)
  blocking collectives  19.7 us (16%)
  waiting for transfers between devices  9.31 us (8%)
  local copies, waits for them, and re-layouts  8.61 us (7%)
  other arithmetic  4.5 us (4%)
  between operations  2.63 us (2%)
    ppermute x12, starting transfers between devices, over(): lax.ppermute(value, 'seq', [(i, move(i)) for i in range(count) if move(i)...  22.8 us
    pallas_call x2, Pallas kernels, local_values(): pl.pallas_call(values_kernel, grid_spec=pltpu.PrefetchScalarGridSpec(num_...  22.1 us
    all_to_all x1, blocking collectives, per_device(): terms = lax.all_to_all(terms, ('seq', 'head'), 0, 0)  19.7 us
    pallas_call x2, Pallas kernels, local_states(): pl.pallas_call(state_kernel, grid_spec=pltpu.PrefetchScalarGridSpec(num_s...  17.1 us
    pallas_call x2, Pallas kernels, gated_norm(): pl.pallas_call(functools.partial(norm_kernel, devices), grid_spec=pltpu.P...  11.8 us
    ppermute x12, waiting for transfers between devices, over(): lax.ppermute(value, 'seq', [(i, move(i)) for i in range(count) if move(i)...  9.31 us
    unnamed x32, local copies, waits for them, and re-layouts  6.74 us
    pallas_call x1, Pallas kernels, decays(): pl.pallas_call(decay_kernel, out_shape=[jax.ShapeDtypeStruct((heads, rows...  2.92 us
  transfers between devices with their start and end apart: 12, of which 3 were waited for; matrix products, arithmetic and copies ran while one was open for 3% of the time, Pallas kernels for 32%

profile of v5, /device:TPU:1, one launch (start us, length us, event | category | flops | bytes accessed | tf_op | source)
XLA Modules:
  0.0 121.3 jit_solution(1619745742952536400)
XLA Ops:
  0.6 0.8 slice.186
  1.4 0.9 slice.185
  2.4 4.6 %collective-permute-start = (bf16[16,5120]{1,0:T(8,128)(2,1)S(1)}, bf16[16,5120]{1,0:T(8,128)(2,1)S(1)}, u32[]{:S(2)}, u32[]{:S(2)}) collective-permute-start(bf16[16,5120]{1,0:T(8,128)(2,1)S(1)} %pad_maximum_fusion.5), channel_id=1, source_target_pairs={{0,4},{4,8},{8,12},{12,16},{16,20},{20,24},{24,28},{28,32},{32,36}... | collective-permute-start | bytes 491528 | tf_op jit(solution)/shard_map/ppermute | solution.py:476
  7.0 3.0 %copy.19 = bf16[96,8,2,512]{3,1,2,0:T(8,128)(2,1)} copy(bf16[96,8,2,512]{3,2,1,0:T(2,128)(2,1)} %bitcast.117) | data formatting | bytes 3145728
  10.0 2.9 %shard_map.149 = (f32[64,768]{1,0:T(8,128)}, f32[64,768]{1,0:T(8,128)}, bf16[768,128]{1,0:T(8,128)(2,1)}, bf16[768,128]{1,0:T(8,128)(2,1)}, bf16[768,128]{1,0:T(...) custom-call(f32[64,768]{1,0:T(8,128)} %bitcast.140, f32[1,64]{1,0:T(1,128)} %bitcast.141, f32[1,64]{1,0:T(1,128)} %bitcast.142), custom_call_target="tpu_custom_call" | custom-call | flops 100000000 | bytes 2000000 | tf_op jit(solution)/shard_map/pallas_call | solution.py:118
  12.9 0.7 copy-done.10
  13.6 8.5 %shard_map.150 = (bf16[768,256]{1,0:T(8,128)(2,1)}, bf16[768,2048]{1,0:T(8,128)(2,1)}, bf16[272,2048]{1,0:T(8,128)(2,1)}) custom-call(s32[1]{0:T(128)} %bitcast.core_ref.place_ref, bf16[768,4096]{1,0:T(8,128)(2,1)} %x_ref.3, bf16[16,5120]{1,0:T(8,128)(2,1)} %copy-done.10, f32[4,4096]{1,0:T(4,128)} %wx_ref.3, f32[1,4096]{1,0:T(1,128)} %bitcast.126, ...), custom_call_target="tpu_custom_call" | custom-call | flops 805306368 | bytes 6291456 | tf_op jit(solution)/shard_map/pallas_call | solution.py:218
  22.3 8.6 %shard_map.151 = (bf16[768,256]{1,0:T(8,128)(2,1)}, bf16[768,2048]{1,0:T(8,128)(2,1)}, bf16[272,2048]{1,0:T(8,128)(2,1)}) custom-call(s32[1]{0:T(128)} %bitcast.core_ref.place_ref, bf16[768,4096]{1,0:T(8,128)(2,1)} %x_ref.3, bf16[16,5120]{1,0:T(8,128)(2,1)} %copy-done.10, f32[4,4096]{1,0:T(4,128)} %wx_ref.3, f32[1,4096]{1,0:T(1,128)} %bitcast.127, ...), custom_call_target="tpu_custom_call" | custom-call | flops 805306368 | bytes 6291456 | tf_op jit(solution)/shard_map/pallas_call | solution.py:218
  30.8 1.4 %broadcast_select_fusion = (bf16[272,2048]{1,0:T(8,128)(2,1)S(1)}, bf16[272,2048]{1,0:T(8,128)(2,1)S(1)}) fusion(bf16[272,2048]{1,0:T(8,128)(2,1)} %get-tuple-element.34, bf16[272,2048]{1,0:T(8,128)(2,1)S(1)} %collective-permute-done.1, pred[]{:T(512)S(6)} %eq.25), kind=kLoop, calls=%fused_computation.12 | loop fusion | flops 1114112 | bytes 4456449 | tf_op jit(solution)/shard_map/jit(_where)/select_n | solution.py:488
  32.4 0.4 fusion.1
  33.0 1.4 %collective-permute-start.2 = (bf16[272,512]{1,0:T(8,128)(2,1)S(1)}, bf16[272,512]{1,0:T(8,128)(2,1)S(1)}, u32[]{:S(2)}, u32[]{:S(2)}) collective-permute-start(bf16[272,512]{1,0:T(8,128)(2,1)S(1)} %get-tuple-element.71), channel_id=1, source_target_pairs={{0,8},{4,12},{8,16},{12,20},{16,24},{20,28},{24,0},{28,4},{32,40},... | collective-permute-start | bytes 835592 | tf_op jit(solution)/shard_map/ppermute | solution.py:476
  34.3 2.2 %collective-permute-start.3 = (bf16[272,512]{1,0:T(8,128)(2,1)S(1)}, bf16[272,512]{1,0:T(8,128)(2,1)S(1)}, u32[]{:S(2)}, u32[]{:S(2)}) collective-permute-start(bf16[272,512]{1,0:T(8,128)(2,1)S(1)} %get-tuple-element.72), channel_id=1, source_target_pairs={{0,16},{4,20},{8,24},{12,28},{16,0},{20,4},{24,8},{28,12},{32,48},... | collective-permute-start | bytes 835592 | tf_op jit(solution)/shard_map/ppermute | solution.py:476
  36.5 1.2 collective-permute-start.4
  37.7 11.0 %shard_map.152 = (bf16[768,2048]{1,0:T(8,128)(2,1)}, bf16[768,256]{1,0:T(8,128)(2,1)}, s32[1]{0:T(128)}) custom-call(s32[1]{0:T(128)} %bitcast.core_ref.place_ref, bf16[768,2048]{1,0:T(8,128)(2,1)} %get-tuple-element.35.x_ref, bf16[768,256]{1,0:T(8,128)(2,1)} %get-tuple-element.36.b_ref, bf16[768,1024]{1,0:T(8,128)(2,1)} %bitcast.115, ...), custom_call_target="tpu_custom_call" | custom-call | flops 3221225472 | bytes 12582912 | tf_op jit(solution)/shard_map/pallas_call | solution.py:331
  50.0 4.7 %collective-permute-start.6 = (bf16[272,512]{1,0:T(8,128)(2,1)S(1)}, bf16[272,512]{1,0:T(8,128)(2,1)S(1)}, u32[]{:S(2)}, u32[]{:S(2)}) collective-permute-start(bf16[272,512]{1,0:T(8,128)(2,1)S(1)} %pad_maximum_fusion.4), channel_id=1, source_target_pairs={{0,64},{4,68},{8,72},{12,76},{16,80},{20,84},{24,88},{28,92},{32,9... | collective-permute-start | bytes 835592 | tf_op jit(solution)/shard_map/ppermute | solution.py:476
  54.8 1.3 %collective-permute-start.7 = (bf16[272,512]{1,0:T(8,128)(2,1)S(1)}, bf16[272,512]{1,0:T(8,128)(2,1)S(1)}, u32[]{:S(2)}, u32[]{:S(2)}) collective-permute-start(bf16[272,512]{1,0:T(8,128)(2,1)S(1)} %pad_maximum_fusion.4), channel_id=1, source_target_pairs={{0,96},{4,100},{8,104},{12,108},{16,112},{20,116},{24,120},{28,124... | collective-permute-start | bytes 835592 | tf_op jit(solution)/shard_map/ppermute | solution.py:476
  56.1 1.6 %collective-permute-start.5 = (bf16[272,512]{1,0:T(8,128)(2,1)S(1)}, bf16[272,512]{1,0:T(8,128)(2,1)S(1)}, u32[]{:S(2)}, u32[]{:S(2)}) collective-permute-start(bf16[272,512]{1,0:T(8,128)(2,1)S(1)} %pad_maximum_fusion.4), channel_id=1, source_target_pairs={{0,32},{4,36},{8,40},{12,44},{16,48},{20,52},{24,56},{28,60},{32,6... | collective-permute-start | bytes 835592 | tf_op jit(solution)/shard_map/ppermute | solution.py:476
  57.7 1.7 %collective-permute-done.6 = bf16[272,512]{1,0:T(8,128)(2,1)S(1)} collective-permute-done((bf16[272,512]{1,0:T(8,128)(2,1)S(1)}, bf16[272,512]{1,0:T(8,128)(2,1)S(1)}, u32[]{:S(2)}, u32[]{:S(2)}) %collective-permute-start.6) | collective-permute-done | bytes 278560 | tf_op jit(solution)/shard_map/ppermute | solution.py:476
  59.5 6.0 %collective-permute-done.5 = bf16[272,512]{1,0:T(8,128)(2,1)S(1)} collective-permute-done((bf16[272,512]{1,0:T(8,128)(2,1)S(1)}, bf16[272,512]{1,0:T(8,128)(2,1)S(1)}, u32[]{:S(2)}, u32[]{:S(2)}) %collective-permute-start.5) | collective-permute-done | bytes 278560 | tf_op jit(solution)/shard_map/ppermute | solution.py:476
  65.5 1.6 %collective-permute-done.7 = bf16[272,512]{1,0:T(8,128)(2,1)S(1)} collective-permute-done((bf16[272,512]{1,0:T(8,128)(2,1)S(1)}, bf16[272,512]{1,0:T(8,128)(2,1)S(1)}, u32[]{:S(2)}, u32[]{:S(2)}) %collective-permute-start.7) | collective-permute-done | bytes 278560 | tf_op jit(solution)/shard_map/ppermute | solution.py:476
  67.2 0.3 convert_bitcast_fusion
  67.7 1.6 %collective-permute-start.9 = (bf16[256,512]{1,0:T(8,128)(2,1)S(1)}, bf16[256,512]{1,0:T(8,128)(2,1)S(1)}, u32[]{:S(2)}, u32[]{:S(2)}) collective-permute-start(bf16[256,512]{1,0:T(8,128)(2,1)S(1)} %get-tuple-element.79), channel_id=1, source_target_pairs={{0,16},{4,20},{8,24},{12,28},{16,0},{20,4},{24,8},{28,12},{32,48},... | collective-permute-start | bytes 786440 | tf_op jit(solution)/shard_map/ppermute | solution.py:476
  69.4 1.3 %collective-permute-start.8 = (bf16[256,512]{1,0:T(8,128)(2,1)S(1)}, bf16[256,512]{1,0:T(8,128)(2,1)S(1)}, u32[]{:S(2)}, u32[]{:S(2)}) collective-permute-start(bf16[256,512]{1,0:T(8,128)(2,1)S(1)} %get-tuple-element.80), channel_id=1, source_target_pairs={{0,8},{4,12},{8,16},{12,20},{16,24},{20,28},{24,0},{28,4},{32,40},... | collective-permute-start | bytes 786440 | tf_op jit(solution)/shard_map/ppermute | solution.py:476
  70.6 1.4 %collective-permute-start.10 = (bf16[256,512]{1,0:T(8,128)(2,1)S(1)}, bf16[256,512]{1,0:T(8,128)(2,1)S(1)}, u32[]{:S(2)}, u32[]{:S(2)}) collective-permute-start(bf16[256,512]{1,0:T(8,128)(2,1)S(1)} %get-tuple-element.81.sent_ref), channel_id=1, source_target_pairs={{0,24},{4,28},{8,0},{12,4},{16,8},{20,12},{24,16},{28,20},{32,56},... | collective-permute-start | bytes 786440 | tf_op jit(solution)/shard_map/ppermute | solution.py:476
  72.0 11.1 %shard_map.153 = (bf16[768,2048]{1,0:T(8,128)(2,1)}, bf16[768,256]{1,0:T(8,128)(2,1)}, s32[1]{0:T(128)}) custom-call(s32[1]{0:T(128)} %bitcast.core_ref.place_ref, bf16[768,2048]{1,0:T(8,128)(2,1)} %get-tuple-element.27.x_ref, bf16[768,256]{1,0:T(8,128)(2,1)} %get-tuple-element.28.b_ref, bf16[768,1024]{1,0:T(8,128)(2,1)} %bitcast.116, ...), custom_call_target="tpu_custom_call" | custom-call | flops 3221225472 | bytes 12582912 | tf_op jit(solution)/shard_map/pallas_call | solution.py:331
  84.1 0.6 fusion.3
  84.7 1.5 %collective-permute-start.11 = (bf16[256,2048]{1,0:T(8,128)(2,1)S(1)}, bf16[256,2048]{1,0:T(8,128)(2,1)S(1)}, u32[]{:S(2)}, u32[]{:S(2)}) collective-permute-start(bf16[256,2048]{1,0:T(8,128)(2,1)S(1)} %get-tuple-element.62), channel_id=1, source_target_pairs={{0,4},{4,0},{8,12},{12,8},{16,20},{20,16},{24,28},{28,24},{32,36},... | collective-permute-start | bytes 3145736 | tf_op jit(solution)/shard_map/ppermute | solution.py:476
  86.4 2.8 %copy-done = bf16[768,4096]{1,0:T(8,128)(2,1)S(1)} copy-done((bf16[768,4096]{1,0:T(8,128)(2,1)S(1)}, bf16[768,4096]{1,0:T(8,128)(2,1)}, u32[]{:S(2)}) %copy-start) | copy-done | bytes 6291480
  89.2 5.7 %shard_map.154 = (bf16[768,4096]{1,0:T(8,128)(2,1)}, f32[768,128]{1,0:T(8,128)S(1)}) custom-call(s32[1]{0:T(128)} %bitcast.core_ref.place_ref, bf16[768,256]{1,0:T(8,128)(2,1)S(1)} %copy-done.5, bf16[256,2048]{1,0:T(8,128)(2,1)S(1)} %get-tuple-element.61.state_ref, bf16[768,2048]{1,0:T(8,128)(2,1)S(1)} %copy-done.3, bf16[768,4096]{1,0:T(8,128)(2,1)S(1)} %copy-done, ...), custom_call_target="tpu_custom_call" | custom-call | flops 805306368 | bytes 9437184 | tf_op jit(solution)/shard_map/pallas_call | solution.py:427
  94.9 6.1 %shard_map.155 = (bf16[768,4096]{1,0:T(8,128)(2,1)}, f32[128,64]{1,0:T(8,128)S(1)}) custom-call(s32[1]{0:T(128)} %bitcast.core_ref.place_ref, bf16[768,256]{1,0:T(8,128)(2,1)S(1)} %copy-done.6, bf16[256,2048]{1,0:T(8,128)(2,1)S(1)} %collective-permute-done.11.state_ref, bf16[768,2048]{1,0:T(8,128)(2,1)S(1)} %copy-done.2, ...), custom_call_target="tpu_custom_call", output_to_operand_aliasing={{0}: (11, {})} | custom-call | flops 805306368 | bytes 9437184 | tf_op jit(solution)/shard_map/pallas_call | solution.py:427
  101.0 19.7 %all_to_all.9 = f32[128,1,64]{2,1,0:T(1,128)S(1)} all-to-all(f32[128,1,64]{2,1,0:T(1,128)S(1)} %bitcast.110), channel_id=1, replica_groups=mesh['seq'=32,'head'=4] {'seq','head'}, dimensions={0} | all-to-all | bytes 65536 | tf_op jit(solution)/shard_map/all_to_all | solution.py:570
  120.7 0.7 reduce_sum.9
  (67 shorter events, 1.6 us)
Async XLA Ops:
  2.4 10.5 %collective-permute-start = (bf16[16,5120]{1,0:T(8,128)(2,1)S(1)}, bf16[16,5120]{1,0:T(8,128)(2,1)S(1)}, u32[]{:S(2)}, u32[]{:S(2)}) collective-permute-start(bf16[16,5120]{1,0:T(8,128)(2,1)S(1)} %pad_maximum_fusion.5), channel_id=1, source_target_pairs={{0,4},{4,8},{8,12},{12,16},{16,20},{20,24},{24,28},{28,32},{32,36}... | collective-permute-start | bytes 491528 | tf_op jit(solution)/shard_map/ppermute | solution.py:476
  12.9 0.7 copy-start.10
  22.1 8.7 %collective-permute-start.1 = (bf16[272,2048]{1,0:T(8,128)(2,1)}, bf16[272,2048]{1,0:T(8,128)(2,1)S(1)}, u32[]{:S(2)}, u32[]{:S(2)}) collective-permute-start(bf16[272,2048]{1,0:T(8,128)(2,1)} %get-tuple-element.33), channel_id=1, source_target_pairs={{0,4},{4,0},{8,12},{12,8},{16,20},{20,16},{24,28},{28,24},{32,36},... | collective-permute-start | bytes 3342344 | tf_op jit(solution)/shard_map/ppermute | solution.py:476
  32.9 4.8 %copy-start.11 = (bf16[272,512]{1,0:T(8,128)(2,1)}, bf16[272,512]{1,0:T(8,128)(2,1)S(1)}, u32[]{:S(2)}) copy-start(bf16[272,512]{1,0:T(8,128)(2,1)S(1)} %get-tuple-element.73.sent_ref) | copy-start | bytes 835588
  33.0 16.5 %collective-permute-start.2 = (bf16[272,512]{1,0:T(8,128)(2,1)S(1)}, bf16[272,512]{1,0:T(8,128)(2,1)S(1)}, u32[]{:S(2)}, u32[]{:S(2)}) collective-permute-start(bf16[272,512]{1,0:T(8,128)(2,1)S(1)} %get-tuple-element.71), channel_id=1, source_target_pairs={{0,8},{4,12},{8,16},{12,20},{16,24},{20,28},{24,0},{28,4},{32,40},... | collective-permute-start | bytes 835592 | tf_op jit(solution)/shard_map/ppermute | solution.py:476
  34.3 15.2 %collective-permute-start.3 = (bf16[272,512]{1,0:T(8,128)(2,1)S(1)}, bf16[272,512]{1,0:T(8,128)(2,1)S(1)}, u32[]{:S(2)}, u32[]{:S(2)}) collective-permute-start(bf16[272,512]{1,0:T(8,128)(2,1)S(1)} %get-tuple-element.72), channel_id=1, source_target_pairs={{0,16},{4,20},{8,24},{12,28},{16,0},{20,4},{24,8},{28,12},{32,48},... | collective-permute-start | bytes 835592 | tf_op jit(solution)/shard_map/ppermute | solution.py:476
  36.5 13.0 %collective-permute-start.4 = (bf16[272,512]{1,0:T(8,128)(2,1)S(1)}, bf16[272,512]{1,0:T(8,128)(2,1)S(1)}, u32[]{:S(2)}, u32[]{:S(2)}) collective-permute-start(bf16[272,512]{1,0:T(8,128)(2,1)S(1)} %get-tuple-element.73.sent_ref), channel_id=1, source_target_pairs={{0,24},{4,28},{8,0},{12,4},{16,8},{20,12},{24,16},{28,20},{32,56},... | collective-permute-start | bytes 835592 | tf_op jit(solution)/shard_map/ppermute | solution.py:476
  50.0 9.4 %collective-permute-start.6 = (bf16[272,512]{1,0:T(8,128)(2,1)S(1)}, bf16[272,512]{1,0:T(8,128)(2,1)S(1)}, u32[]{:S(2)}, u32[]{:S(2)}) collective-permute-start(bf16[272,512]{1,0:T(8,128)(2,1)S(1)} %pad_maximum_fusion.4), channel_id=1, source_target_pairs={{0,64},{4,68},{8,72},{12,76},{16,80},{20,84},{24,88},{28,92},{32,9... | collective-permute-start | bytes 835592 | tf_op jit(solution)/shard_map/ppermute | solution.py:476
  54.8 12.3 %collective-permute-start.7 = (bf16[272,512]{1,0:T(8,128)(2,1)S(1)}, bf16[272,512]{1,0:T(8,128)(2,1)S(1)}, u32[]{:S(2)}, u32[]{:S(2)}) collective-permute-start(bf16[272,512]{1,0:T(8,128)(2,1)S(1)} %pad_maximum_fusion.4), channel_id=1, source_target_pairs={{0,96},{4,100},{8,104},{12,108},{16,112},{20,116},{24,120},{28,124... | collective-permute-start | bytes 835592 | tf_op jit(solution)/shard_map/ppermute | solution.py:476
  56.1 9.3 %collective-permute-start.5 = (bf16[272,512]{1,0:T(8,128)(2,1)S(1)}, bf16[272,512]{1,0:T(8,128)(2,1)S(1)}, u32[]{:S(2)}, u32[]{:S(2)}) collective-permute-start(bf16[272,512]{1,0:T(8,128)(2,1)S(1)} %pad_maximum_fusion.4), channel_id=1, source_target_pairs={{0,32},{4,36},{8,40},{12,44},{16,48},{20,52},{24,56},{28,60},{32,6... | collective-permute-start | bytes 835592 | tf_op jit(solution)/shard_map/ppermute | solution.py:476
  67.7 4.3 %copy-start.12 = (bf16[256,512]{1,0:T(8,128)(2,1)}, bf16[256,512]{1,0:T(8,128)(2,1)S(1)}, u32[]{:S(2)}) copy-start(bf16[256,512]{1,0:T(8,128)(2,1)S(1)} %get-tuple-element.81.sent_ref) | copy-start | bytes 786436
  67.7 16.0 %collective-permute-start.9 = (bf16[256,512]{1,0:T(8,128)(2,1)S(1)}, bf16[256,512]{1,0:T(8,128)(2,1)S(1)}, u32[]{:S(2)}, u32[]{:S(2)}) collective-permute-start(bf16[256,512]{1,0:T(8,128)(2,1)S(1)} %get-tuple-element.79), channel_id=1, source_target_pairs={{0,16},{4,20},{8,24},{12,28},{16,0},{20,4},{24,8},{28,12},{32,48},... | collective-permute-start | bytes 786440 | tf_op jit(solution)/shard_map/ppermute | solution.py:476
  69.4 14.4 %collective-permute-start.8 = (bf16[256,512]{1,0:T(8,128)(2,1)S(1)}, bf16[256,512]{1,0:T(8,128)(2,1)S(1)}, u32[]{:S(2)}, u32[]{:S(2)}) collective-permute-start(bf16[256,512]{1,0:T(8,128)(2,1)S(1)} %get-tuple-element.80), channel_id=1, source_target_pairs={{0,8},{4,12},{8,16},{12,20},{16,24},{20,28},{24,0},{28,4},{32,40},... | collective-permute-start | bytes 786440 | tf_op jit(solution)/shard_map/ppermute | solution.py:476
  70.6 13.2 %collective-permute-start.10 = (bf16[256,512]{1,0:T(8,128)(2,1)S(1)}, bf16[256,512]{1,0:T(8,128)(2,1)S(1)}, u32[]{:S(2)}, u32[]{:S(2)}) collective-permute-start(bf16[256,512]{1,0:T(8,128)(2,1)S(1)} %get-tuple-element.81.sent_ref), channel_id=1, source_target_pairs={{0,24},{4,28},{8,0},{12,4},{16,8},{20,12},{24,16},{28,20},{32,56},... | collective-permute-start | bytes 786440 | tf_op jit(solution)/shard_map/ppermute | solution.py:476
  72.0 14.1 %copy-start.4 = (bf16[768,128]{1,0:T(8,128)(2,1)S(1)}, bf16[768,128]{1,0:T(8,128)(2,1)}, u32[]{:S(2)}) copy-start(bf16[768,128]{1,0:T(8,128)(2,1)} %get-tuple-element.41.eabs_ref) | copy-start | bytes 589828
  72.0 14.1 %copy-start.5 = (bf16[768,256]{1,0:T(8,128)(2,1)S(1)}, bf16[768,256]{1,0:T(8,128)(2,1)}, u32[]{:S(2)}) copy-start(bf16[768,256]{1,0:T(8,128)(2,1)} %get-tuple-element.42.c_ref) | copy-start | bytes 1179652
  83.8 11.1 %slice-start = ((s8[6291456]{0:T(1024)(128)(4,1)}), s8[4194304]{0:T(1024)(128)(4,1)S(1)}, s32[]{:S(2)}) async-start(s8[6291456]{0:T(1024)(128)(4,1)} %bitcast.104), calls=%async_computation.1 | async-start | bytes 8388608
  84.0 2.2 %copy-start.8 = (f32[4096]{0:T(1024)S(1)}, f32[4096]{0:T(1024)}, u32[]{:S(2)}) copy-start(f32[4096]{0:T(1024)} %param.25) | copy-start | bytes 49156
  84.1 2.1 %copy-start.1 = (bf16[2,128,2048]{2,1,0:T(8,128)(2,1)S(1)}, bf16[2,128,2048]{2,1,0:T(8,128)(2,1)}, u32[]{:S(2)}) copy-start(bf16[2,128,2048]{2,1,0:T(8,128)(2,1)} %constant.154.clone.spread_ref) | copy-start | bytes 3145732
  84.1 2.3 %copy-start.3 = (bf16[768,2048]{1,0:T(8,128)(2,1)S(1)}, bf16[768,2048]{1,0:T(8,128)(2,1)}, u32[]{:S(2)}) copy-start(bf16[768,2048]{1,0:T(8,128)(2,1)} %get-tuple-element.43.values_ref) | copy-start | bytes 9437188
  84.1 2.3 %copy-start.7 = (f32[4096]{0:T(1024)S(1)}, f32[4096]{0:T(1024)}, u32[]{:S(2)}) copy-start(f32[4096]{0:T(1024)} %param.24) | copy-start | bytes 49156
  84.1 2.2 %copy-start.9 = (s32[64]{0:T(128)S(1)}, s32[64]{0:T(128)}, u32[]{:S(2)}) copy-start(s32[64]{0:T(128)} %param.26) | copy-start | bytes 772
  84.7 10.2 %collective-permute-start.11 = (bf16[256,2048]{1,0:T(8,128)(2,1)S(1)}, bf16[256,2048]{1,0:T(8,128)(2,1)S(1)}, u32[]{:S(2)}, u32[]{:S(2)}) collective-permute-start(bf16[256,2048]{1,0:T(8,128)(2,1)S(1)} %get-tuple-element.62), channel_id=1, source_target_pairs={{0,4},{4,0},{8,12},{12,8},{16,20},{20,16},{24,28},{28,24},{32,36},... | collective-permute-start | bytes 3145736 | tf_op jit(solution)/shard_map/ppermute | solution.py:476
  86.4 2.8 %copy-start = (bf16[768,4096]{1,0:T(8,128)(2,1)S(1)}, bf16[768,4096]{1,0:T(8,128)(2,1)}, u32[]{:S(2)}) copy-start(bf16[768,4096]{1,0:T(8,128)(2,1)} %z_ref.3) | copy-start | bytes 18874372
  89.2 5.7 %slice-start.1 = ((s8[6291456]{0:T(1024)(128)(4,1)}), s8[2097152]{0:T(1024)(128)(4,1)S(1)}, s32[]{:S(2)}) async-start(s8[6291456]{0:T(1024)(128)(4,1)} %bitcast.104), calls=%async_computation.2 | async-start | bytes 4194304
  89.2 5.7 %copy-start.2 = (bf16[768,2048]{1,0:T(8,128)(2,1)S(1)}, bf16[768,2048]{1,0:T(8,128)(2,1)}, u32[]{:S(2)}) copy-start(bf16[768,2048]{1,0:T(8,128)(2,1)} %get-tuple-element.40.values_ref) | copy-start | bytes 9437188
  89.2 5.7 %copy-start.6 = (bf16[768,256]{1,0:T(8,128)(2,1)S(1)}, bf16[768,256]{1,0:T(8,128)(2,1)}, u32[]{:S(2)}) copy-start(bf16[768,256]{1,0:T(8,128)(2,1)} %get-tuple-element.38.c_ref) | copy-start | bytes 1179652
